TPU v7x, 512 devices: a whole 4x8x8 slice. The times are simulated.
512 devices in a mesh: seq: 32 (over x, y), tensor: 4 (over z_lo, core), dp: 4 (over z_hi).
Axes of the slice: x: 4, y: 8, z: 8 (z_hi: 4, z_lo: 2; z = z_hi * 2 + z_lo), core: 2. Of those that a mesh axis runs over, the one named last changes fastest.
Arguments:
- frames_in: bfloat16 [4, 32, 256, 3072], P('dp', 'seq', None, 'tensor'), parts along dimension 0, may hold values from -6 to 6
- norm_gain: float32 [3072], replicated, may hold values from 0.5 to 6
- w_qkv: bfloat16 [3072, 3, 2048], P('seq', None, 'tensor'), may hold values from -0.109375 to 0.109375
- w_out: bfloat16 [2048, 3072], P('tensor'), may hold values from -0.125 to 0.125
Outputs:
- mixed: bfloat16 [4, 32, 256, 3072], P('dp', 'seq', None, 'tensor'), parts along dimension 0
There are 4 independent parts, one for each index of `dp`. A program takes and returns all parts, laid end to end along the dimension named above; an argument that names none is the same for every part. Nothing has to cross between parts.
All inputs are finite; a program needn't handle non-finite values.
Results may differ from a plain program's by a relative error of at most 0.019.
Values may be sent and summed in bfloat16 or wider, within the bound.
No kernel may reach another device: no remote copies, remote signals or barrier semaphores. Data moves between devices by JAX's collectives and lax.ppermute only.
A program may use at most 64 MiB of HBM per device.

v0:
```python
import jax
import jax.numpy as jnp
from jax import lax
from jax.sharding import PartitionSpec as P

HD = 128


def full_features(activity):
    return lax.all_gather(activity, "tensor", axis=3, tiled=True)


def normalize(activity, norm_gain):
    widened = activity.astype(jnp.float32)
    average = jnp.mean(widened, axis=-1, keepdims=True)
    centred = widened - average
    spread = jnp.mean(centred * centred, axis=-1, keepdims=True)
    return (centred * lax.rsqrt(spread + 1e-06) * norm_gain).astype(jnp.bfloat16)


def project(normed, w_qkv):
    width_in = normed.shape[-1]
    width_out = w_qkv.shape[1] * w_qkv.shape[2]
    token_rows = normed.reshape(-1, width_in)
    weight_block = lax.all_gather(w_qkv, "seq", axis=0, tiled=True)
    flat_block = weight_block.reshape(weight_block.shape[0], width_out)
    running = jnp.dot(token_rows, flat_block, preferred_element_type=jnp.float32)
    return running.astype(jnp.bfloat16).reshape(normed.shape[:-1] + (3, w_qkv.shape[2]))


def attend(projected):
    head_size = HD
    group_width = projected.shape[-1]
    heads_here = group_width // head_size
    lead = projected.shape[:3]
    queries = projected[:, :, :, 0].reshape(lead + (heads_here, head_size))
    key_part = projected[:, :, :, 1].reshape(lead + (heads_here, head_size))
    value_part = projected[:, :, :, 2].reshape(lead + (heads_here, head_size))
    scores = jnp.einsum("cfphd,cgphd->cphfg", queries, key_part, preferred_element_type=jnp.float32)
    scores = scores * head_size ** (-0.5)
    weights = jax.nn.softmax(scores, axis=-1).astype(jnp.bfloat16)
    attended = jnp.einsum(
        "cphfg,cgphd->cfphd", weights, value_part, preferred_element_type=jnp.float32
    )
    return attended.astype(jnp.bfloat16).reshape(lead + (group_width,))


def output_sum(attended, w_out, residual):
    group_width = attended.shape[-1]
    partial_value = jnp.dot(
        attended.reshape(-1, group_width), w_out, preferred_element_type=jnp.float32
    )
    partial_value = partial_value.reshape(attended.shape[:-1] + (w_out.shape[1],))
    summed = lax.psum_scatter(
        partial_value.astype(jnp.bfloat16), "tensor", scatter_dimension=3, tiled=True
    ).astype(jnp.float32)
    return (residual.astype(jnp.float32) + summed).astype(jnp.bfloat16)


def body(frames_in, norm_gain, w_qkv, w_out):
    normed = normalize(full_features(frames_in), norm_gain)
    projected = project(normed, w_qkv)
    attended = attend(lax.all_to_all(projected, "seq", split_axis=2, concat_axis=1, tiled=True))
    attended = lax.all_to_all(attended, "seq", split_axis=1, concat_axis=2, tiled=True)
    mixed = output_sum(attended, w_out, frames_in)
    return mixed


def solution(mesh):
    in_specs = (P("dp", "seq", None, "tensor"), P(), P("seq", None, "tensor"), P("tensor", None))
    out_specs = P("dp", "seq", None, "tensor")
    return jax.shard_map(body, mesh=mesh, in_specs=in_specs, out_specs=out_specs, check_vma=False)
```

profile of v0, /device:TPU:1, one launch (start us, length us, event | category | flops | bytes accessed | tf_op | source)
XLA Modules:
  0.0 274.9 jit_solution(1943076793262360842)
XLA Ops:
  6.5 0.0 copy-start
  6.5 0.0 all-gather.3.cloned.1.call-start
  6.5 0.7 all-gather.3.cloned.1.call-update
  7.3 0.0 all-gather.5.cloned.1.call-start
  7.3 0.7 all-gather.5.cloned.1.call-update
  8.0 0.0 reduce-scatter.2.cloned.1.call-start
  8.1 37.7 %all-gather.3.cloned.1.call-done = bf16[1,1,256,3072]{3,2,1,0:T(8,128)(2,1)} async-done(((bf16[1,1,256,768]{3,2,1,0:T(8,128)(2,1)}), bf16[1,1,256,3072]{3,2,1,0:T(8,128)(2,1)}) %all-gather.3.cloned.1.call-update) | async-done | bytes 1572880 | tf_op jit(solution)/shard_map/all_gather | solution.py:10
  45.7 1.7 convert_reduce_fusion
  47.4 2.0 fusion.4
  49.4 0.0 copy-start.2
  49.4 107.7 %all-gather.5.cloned.1.call-done = bf16[3072,3,512]{2,0,1:T(8,128)(2,1)} async-done(((bf16[96,3,512]{2,0,1:T(8,128)(2,1)}), bf16[3072,3,512]{2,0,1:T(8,128)(2,1)}) %all-gather.5.cloned.1.call-update) | async-done | bytes 9437200 | tf_op jit(solution)/shard_map/all_gather | solution.py:25
  157.1 12.7 %copy.24 = bf16[3072,3,512]{0,2,1:T(8,128)(2,1)} copy(bf16[3072,3,512]{2,0,1:T(8,128)(2,1)} %all-gather.5.cloned.1.call-done) | data formatting | bytes 18874368 | tf_op jit(solution)/shard_map/all_gather | solution.py:25
  169.8 0.0 copy-done.2
  169.8 7.7 %convolution_convert_fusion.1 = bf16[256,1536]{1,0:T(8,128)(2,1)} fusion(bf16[3072,1536]{0,1:T(8,128)(2,1)} %bitcast.30, bf16[1,1,256,3072]{3,2,1,0:T(8,128)(2,1)} %all-gather.3.cloned.1.call-done, f32[3072]{0:T(1024)S(1)} %copy-done.2, f32[256]{0:T(256)S(1)} %add_rsqrt_fusion, f32[256]{0:T(256)S(1)} %broadcast_multiply_fusion), kind=kOutput, calls=%fused_computation.10 | convolution fusion | flops 2420244480 | bytes 11810816 | tf_op jit(solution)/shard_map/dot_general | solution.py:27
  177.5 2.3 copy.25
  179.8 2.6 copy.26
  182.4 30.3 %all_to_all.21 = bf16[1,1,256,3,512]{4,3,1,0,2:T(4,128)(2,1)S(1)} all-to-all(bf16[1,1,256,3,512]{4,3,1,0,2:T(4,128)(2,1)} %copy.26), channel_id=1, replica_groups=mesh['seq'=32,'tensor'=4,'dp'=4] {'seq'}, dimensions={2} | all-to-all | bytes 1572864 | tf_op jit(solution)/shard_map/all_to_all | solution.py:63
  212.7 0.2 copy.55
  212.9 0.8 slice_bitcast_fusion.2
  213.7 2.2 fusion.30
  215.9 1.3 fusion.14
  217.2 0.2 copy.56
  217.4 17.9 %all_to_all.22 = bf16[1,32,8,512]{3,2,0,1:T(8,128)(2,1)S(1)} all-to-all(bf16[1,32,8,512]{3,2,0,1:T(8,128)(2,1)S(1)} %bitcast.33), channel_id=1, replica_groups=mesh['seq'=32,'tensor'=4,'dp'=4] {'seq'}, dimensions={1} | all-to-all | bytes 524288 | tf_op jit(solution)/shard_map/all_to_all | solution.py:64
  235.2 0.0 copy-done
  235.3 0.0 copy-start.1
  235.3 2.2 fusion.3
  237.4 0.0 reduce-scatter.2.cloned.1.call-update
  237.5 29.1 %reduce-scatter.2.cloned.1.call-done = bf16[1,1,256,768]{3,2,1,0:T(8,128)(2,1)} async-done(((bf16[1,1,256,3072]{3,2,1,0:T(8,128)(2,1)}), bf16[1,1,256,768]{3,2,1,0:T(8,128)(2,1)}) %reduce-scatter.2.cloned.1.call-update) | async-done | bytes 393232 | tf_op jit(solution)/shard_map/reduce_scatter | solution.py:54
  266.6 0.0 copy-done.1
  266.6 1.8 add_convert_fusion
  (2 shorter events, 0.0 us)
Async XLA Ops:
  6.5 228.7 %copy-start = (bf16[512,3072]{1,0:T(8,128)(2,1)S(1)}, bf16[512,3072]{1,0:T(8,128)(2,1)}, u32[]{:S(2)}) copy-start(bf16[512,3072]{1,0:T(8,128)(2,1)} %param.7) | copy-start | bytes 9437188
  6.5 39.2 %all-gather.3.cloned.1.call-start = ((), (), s32[]{:S(2)}) async-start(), calls=%async_computation.3 | async-start | bytes 1966080 | tf_op jit(solution)/shard_map/all_gather | solution.py:10
  7.3 149.8 %all-gather.5.cloned.1.call-start = ((), (), s32[]{:S(2)}) async-start(), calls=%async_computation.4 | async-start | bytes 9732096 | tf_op jit(solution)/shard_map/all_gather | solution.py:25
  8.0 258.6 %reduce-scatter.2.cloned.1.call-start = ((), (), s32[]{:S(2)}) async-start(), calls=%async_computation.5 | async-start | bytes 1966080 | tf_op jit(solution)/shard_map/reduce_scatter | solution.py:54
  49.4 120.4 %copy-start.2 = (f32[3072]{0:T(1024)S(1)}, f32[3072]{0:T(1024)}, u32[]{:S(2)}) copy-start(f32[3072]{0:T(1024)} %param.5) | copy-start | bytes 36868
  235.3 31.3 %copy-start.1 = (bf16[1,1,256,768]{3,2,1,0:T(8,128)(2,1)S(1)}, bf16[1,1,256,768]{3,2,1,0:T(8,128)(2,1)}, u32[]{:S(2)}) copy-start(bf16[1,1,256,768]{3,2,1,0:T(8,128)(2,1)} %param.4) | copy-start | bytes 1179652
Sparse Core Ops, SparseCore 0:
  9.5 36.2 all-gather.2
  48.9 108.1 all-gather.4
  237.6 28.9 reduce-scatter.1
where the time goes:
time: 276 us; the launch traced here: 275 us
  waiting for transfers between devices  176 us (64%)
  blocking collectives  48.2 us (17%)
  local copies, waits for them, and re-layouts  18.8 us (7%)
  matrix products  13.4 us (5%)
  between operations  13.1 us (5%)
  other arithmetic  5.5 us (2%)
    all_gather x1, waiting for transfers between devices, project(): weight_block = lax.all_gather(w_qkv, 'seq', axis=0, tiled=True)  108 us
    all_gather x1, waiting for transfers between devices, full_features(): return lax.all_gather(activity, 'tensor', axis=3, tiled=True)  37.7 us
    all_to_all x1, blocking collectives, body(): lax.all_to_all(projected, 'seq', split_axis=2, concat_axis=1, tiled=True)  30.3 us
    reduce_scatter x1, waiting for transfers between devices, output_sum(): lax.psum_scatter(partial_value.astype(jnp.bfloat16), 'tensor', scatter_di...  29.1 us
    all_to_all x1, blocking collectives, body(): lax.all_to_all(attended, 'seq', split_axis=1, concat_axis=2, tiled=True)  17.9 us
    all_gather x1, local copies, waits for them, and re-layouts, project(): weight_block = lax.all_gather(w_qkv, 'seq', axis=0, tiled=True)  12.7 us
    dot_general x1, matrix products, project(): jnp.dot(token_rows, flat_block, preferred_element_type=jnp.float32)  7.71 us
  transfers between devices with their start and end apart: 3, of which 3 were waited for; matrix products, arithmetic and copies ran while one was open for 1% of the time, Pallas kernels for 0%

commit v1 on v0

v1 whole, which is shorter than its diff:
```python
import jax
import jax.numpy as jnp
from jax import lax
from jax.experimental import pallas as pl
from jax.experimental.pallas import tpu as pltpu
from jax.sharding import Mesh, PartitionSpec as P

HD = 128
WIDTH = 3072
QUARTER = 768
F32 = jnp.float32
BF16 = jnp.bfloat16
VMEM = pl.BlockSpec(memory_space=pltpu.VMEM)
SMEM = pl.BlockSpec(memory_space=pltpu.SMEM)


def ring(size, shift):
    return [(i, (i + shift) % size) for i in range(size)]


def swap(value, axis):
    return lax.ppermute(value, axis, [(0, 1), (1, 0)])


def normalize_block(x, z, near, far, gain, store):
    parts = []
    for z_far, side in enumerate((near, far)):
        for core in range(2):
            piece = side[:, 16 * core : 16 * core + 16, :].reshape(128, QUARTER).astype(F32)
            parts.append((2 * lax.rem(z + z_far, 2) + core, piece))
    total = parts[0][1] + parts[1][1] + parts[2][1] + parts[3][1]
    average = jnp.sum(total, axis=-1, keepdims=True) * (1.0 / WIDTH)
    squares = 0.0
    for _, value in parts:
        centred = value - average
        squares = squares + centred * centred
    spread = jnp.sum(squares, axis=-1, keepdims=True) * (1.0 / WIDTH)
    scale = lax.rsqrt(spread + 1e-06)
    for q, value in parts:
        store(q, ((value - average) * scale * gain[q]).astype(BF16))


def normalize_kernel(place, xa, xb, la, lb, ra, rb, gain, out):
    for block, (near, far) in enumerate(((xa, xb), (la, lb), (ra, rb))):

        def store(q, value, block=block):
            out[q, block] = value

        normalize_block(place[0], place[1], near, far, gain, store)


def attend_kernel(place, normed, oa, ob, gain, w_rows, out, last):
    x, z, c = place[0], place[1], place[2]

    def store(q, value):
        last[q] = value

    normalize_block(x, z, oa, ob, gain, store)
    sides = [jnp.zeros((512, 3 * HD), F32) for _ in range(2)]
    for k in range(4):
        q = lax.rem(x + 4 - k, 4)
        tokens = jnp.concatenate([normed[q].reshape(384, QUARTER), last[q]], axis=0)
        for core in range(2):
            weight = w_rows[k, QUARTER * core : QUARTER * core + QUARTER]
            sides[core] = sides[core] + jnp.dot(tokens, weight, preferred_element_type=F32)

    row = lax.broadcasted_iota(jnp.int32, (512, 512), 0)
    column = lax.broadcasted_iota(jnp.int32, (512, 512), 1)
    same_patch = lax.rem(row, 16) == lax.rem(column, 16)
    heads = []
    for projected in sides:
        query = projected[:, :HD].astype(BF16)
        key = projected[:, HD : 2 * HD].astype(BF16)
        value = projected[:, 2 * HD :].astype(BF16)
        scores = lax.dot_general(query, key, (((1,), (1,)), ((), ())), preferred_element_type=F32)
        scores = jnp.where(same_patch, scores * HD**-0.5, -jnp.inf)
        top = jnp.max(scores, axis=-1, keepdims=True)
        weights = jnp.exp(scores - top)
        weights = (weights / jnp.sum(weights, axis=-1, keepdims=True)).astype(BF16)
        heads.append(jnp.dot(weights, value, preferred_element_type=F32).astype(BF16))
    both = jnp.concatenate(heads, axis=1)
    for block, shift in enumerate((0, 3, 1, 2)):
        piece = both[128 * block : 128 * block + 128].reshape(8, 16, 2 * HD)
        frame = lax.rem(x + shift, 4)
        out[frame, :, 0] = piece
        out[frame, :, 1] = piece


def output_kernel(place, near, far, wo00, wo10, wo01, wo11, residual, out):
    z, c = place[1], place[2]
    total = jnp.zeros((256, QUARTER), F32)
    for z_far, weights in enumerate(((wo00, wo01), (wo10, wo11))):
        source = lax.rem(z + z_far, 2)
        for core in range(2):
            pieces = []
            for half in (near, far):
                columns = [
                    half[s, :, source, :, HD * core : HD * core + HD].reshape(128, HD) for s in range(4)
                ]
                pieces.append(jnp.concatenate(columns, axis=1))
            attended = jnp.concatenate(pieces, axis=0)
            weight = jnp.where(c == core, weights[0][...], weights[1][...])
            total = total + jnp.dot(attended, weight, preferred_element_type=F32)
    for half in range(2):
        side = lax.rem(c + half, 2)
        mixed = residual[:, side].astype(F32) + total[128 * half : 128 * half + 128].reshape(8, 16, QUARTER)
        out[:, side] = mixed.astype(BF16)


def slice_kernel(place, source, *outs):
    for k, out in enumerate(outs):
        head = lax.rem(place[0] + k, 4)
        for part in range(3):
            out[:, HD * part : HD * part + HD] = source[part, :, pl.ds(pl.multiple_of(head * HD, HD), HD)]


def after(value, *others):
    return lax.optimization_barrier((value, *others))[0]


def kernel_call(kernel, shapes, operands, flops, moved, scratch=()):
    return pl.pallas_call(
        kernel,
        out_shape=shapes,
        in_specs=[SMEM] + [VMEM] * (len(operands) - 1),
        out_specs=jax.tree.map(lambda _: VMEM, shapes),
        scratch_shapes=list(scratch),
        compiler_params=pltpu.CompilerParams(vmem_limit_bytes=40 * 2**20),
        cost_estimate=pl.CostEstimate(flops=flops, bytes_accessed=moved, transcendentals=0),
    )(*operands)


def body(frames_in, norm_gain, w_qkv, w_out):
    x, z, c = lax.axis_index("x"), lax.axis_index("z"), lax.axis_index("c")
    place = jnp.stack([x, z, c]).astype(jnp.int32)
    gain = norm_gain.reshape(4, 1, QUARTER)

    slots = kernel_call(
        slice_kernel,
        [jax.ShapeDtypeStruct((96, 3 * HD), BF16)] * 4,
        (place, w_qkv.transpose(1, 0, 2)),
        0,
        6 * 10**5,
    )
    w_rows = [slots[0]] + [lax.ppermute(slots[k], "x", ring(4, k)) for k in (1, 2, 3)]
    w_rows = lax.all_gather(jnp.stack(w_rows), ("c", "y"), axis=1, tiled=True)

    tokens = frames_in.reshape(16, 16, QUARTER)
    xa = lax.all_to_all(tokens, ("y", "c"), 0, 0, tiled=True).reshape(8, 32, QUARTER)
    xb = swap(xa, "z")
    la, ra, oa = (lax.ppermute(xa, "x", ring(4, shift)) for shift in (1, 3, 2))
    lb, rb, ob = (lax.ppermute(xb, "x", ring(4, shift)) for shift in (1, 3, 2))

    normed = kernel_call(
        normalize_kernel,
        jax.ShapeDtypeStruct((4, 3, 128, QUARTER), BF16),
        (place, xa, xb, la, lb, ra, rb, gain),
        10**7,
        5 * 10**6,
    )
    attended = kernel_call(
        attend_kernel,
        jax.ShapeDtypeStruct((4, 8, 2, 16, 2 * HD), BF16),
        (place, normed, oa, ob, gain, w_rows),
        3 * 10**9,
        9 * 10**6,
        [pltpu.VMEM((4, 128, QUARTER), BF16)],
    )

    def half(value, index, size):
        return lax.dynamic_slice_in_dim(value, index * size, size, axis=1)

    wo_keep = half(w_out, z, 2 * QUARTER)
    wo_got = swap(after(half(w_out, 1 - z, 2 * QUARTER), xb), "z")
    wo00, wo10 = half(wo_keep, c, QUARTER), half(wo_got, c, QUARTER)
    wo01, wo11 = swap(half(wo_keep, 1 - c, QUARTER), "c"), swap(half(wo_got, 1 - c, QUARTER), "c")

    attended = lax.all_to_all(attended.reshape(64, 16, 2 * HD), ("x", "y", "z"), 0, 0, tiled=True)
    other = swap(attended, "c")
    shape = (4, 8, 2, 16, 2 * HD)
    mixed = kernel_call(
        output_kernel,
        jax.ShapeDtypeStruct((8, 2, 16, QUARTER), BF16),
        (
            place,
            attended.reshape(shape),
            other.reshape(shape),
            wo00,
            wo10,
            wo01,
            wo11,
            frames_in.reshape(8, 2, 16, QUARTER),
        ),
        8 * 10**8,
        6 * 10**6,
    )
    return mixed.reshape(1, 1, 256, QUARTER)


def solution(mesh):
    fine = Mesh(mesh.devices.reshape(4, 8, 2, 2, 4), ("x", "y", "z", "c", "dp"))
    seq, tensor = ("x", "y"), ("z", "c")
    in_specs = (P("dp", seq, None, tensor), P(), P(seq, None, tensor), P(tensor, None))
    out_specs = P("dp", seq, None, tensor)
    return jax.shard_map(body, mesh=fine, in_specs=in_specs, out_specs=out_specs, check_vma=False)
```

time: 276 us -> 150 us (0.54)
  waiting for transfers between devices: 176 us -> 25.5 us
  starting transfers between devices: 0.08 us -> 56.1 us
  blocking collectives: 48.2 us -> 24.1 us
  matrix products: 13.4 us -> 0 us
  Pallas kernels: 0 us -> 12 us
  other arithmetic: 5.5 us -> 0.85 us
  local copies, waits for them, and re-layouts: 18.8 us -> 15 us
    all_gather x2 -> x1, waiting for transfers between devices: 145 us -> 0.01 us  [body(): w_rows = lax.all_gather(jnp.stack(w_rows), ('c', 'y'), axis=1, tiled=True)]
    ppermute x0 -> x14, starting transfers between devices: none -> 50.2 us  [the longest x5 20.3 us: swap(): return lax.ppermute(value, axis, [(0, 1), (1, 0)])]
    reduce_scatter x1 -> x0, waiting for transfers between devices: 29.1 us -> none  [output_sum(): lax.psum_scatter(partial_value.astype(jnp.bfloat16), 'tensor', scatter_di...]
    all_to_all x2 -> x1, blocking collectives: 48.2 us -> 24.1 us  [body(): lax.all_to_all(tokens, ('y', 'c'), 0, 0, tiled=True).reshape(8, 32, QUARTER)]
    ppermute x0 -> x14, waiting for transfers between devices: none -> 23.1 us  [the longest x3 17.8 us: body(): lb, rb, ob = (lax.ppermute(xb, 'x', ring(4, shift)) for shift in (1, 3, 2))]
    all_gather x1 -> x0, local copies, waits for them, and re-layouts: 12.7 us -> none  [project(): weight_block = lax.all_gather(w_qkv, 'seq', axis=0, tiled=True)]
    pallas_call x0 -> x4, Pallas kernels: none -> 12 us  [kernel_call(): pl.pallas_call(kernel, out_shape=shapes, in_specs=[SMEM] + [VMEM] * (len(...]
    dot_general x3 -> x0, matrix products: 11.2 us -> none  [the longest x1 7.71 us: project(): jnp.dot(token_rows, flat_block, preferred_element_type=jnp.float32)]
  transfers between devices with their start and end apart: 3 -> 16, of which waited for: 3 -> 6; matrix products, arithmetic and copies ran while one was open for 1% -> 6% of each run, Pallas kernels for 0% -> 6%
where the time goes in v1:
time: 150 us; the launch traced here: 147 us
  starting transfers between devices  56.1 us (37%)
  waiting for transfers between devices  25.5 us (17%)
  blocking collectives  24.1 us (16%)
  local copies, waits for them, and re-layouts  15 us (10%)
  between operations  13.6 us (9%)
  Pallas kernels  12 us (8%)
    all_to_all x1, blocking collectives, body(): lax.all_to_all(tokens, ('y', 'c'), 0, 0, tiled=True).reshape(8, 32, QUARTER)  24.1 us
    ppermute x5, starting transfers between devices, swap(): return lax.ppermute(value, axis, [(0, 1), (1, 0)])  20.3 us
    ppermute x3, waiting for transfers between devices, body(): lb, rb, ob = (lax.ppermute(xb, 'x', ring(4, shift)) for shift in (1, 3, 2))  17.8 us
    pallas_call x4, Pallas kernels, kernel_call(): pl.pallas_call(kernel, out_shape=shapes, in_specs=[SMEM] + [VMEM] * (len(...  12 us
    ppermute x3, starting transfers between devices, body(): lb, rb, ob = (lax.ppermute(xb, 'x', ring(4, shift)) for shift in (1, 3, 2))  11.4 us
    ppermute x3, starting transfers between devices, body(): lax.ppermute(slots[k], 'x', ring(4, k))  10.2 us
    ppermute x3, starting transfers between devices, body(): la, ra, oa = (lax.ppermute(xa, 'x', ring(4, shift)) for shift in (1, 3, 2))  8.42 us
    dynamic_slice x3, local copies, waits for them, and re-layouts, half(): return lax.dynamic_slice_in_dim(value, index * size, size, axis=1)  8.2 us
  transfers between devices with their start and end apart: 16, of which 6 were waited for; matrix products, arithmetic and copies ran while one was open for 6% of the time, Pallas kernels for 6%

profile of v1, /device:TPU:1, one launch (start us, length us, event | category | flops | bytes accessed | tf_op | source)
XLA Modules:
  0.0 147.1 jit_solution(5227389855448531904)
XLA Ops:
  6.6 1.0 copy-done.1
  8.2 5.2 %collective-permute-start.9 = (bf16[96,384]{1,0:T(8,128)(2,1)S(1)}, bf16[96,384]{1,0:T(8,128)(2,1)S(1)}, u32[]{:S(2)}, u32[]{:S(2)}) collective-permute-start(bf16[96,384]{1,0:T(8,128)(2,1)S(1)} %get-tuple-element.13), channel_id=1, source_target_pairs={{0,384},{128,0},{256,128},{384,256},{1,385},{129,1},{257,129},{385... | collective-permute-start | bytes 221192 | tf_op jit(solution)/shard_map/ppermute | solution.py:145
  13.4 2.4 %collective-permute-start.8 = (bf16[96,384]{1,0:T(8,128)(2,1)S(1)}, bf16[96,384]{1,0:T(8,128)(2,1)S(1)}, u32[]{:S(2)}, u32[]{:S(2)}) collective-permute-start(bf16[96,384]{1,0:T(8,128)(2,1)S(1)} %get-tuple-element.12), channel_id=1, source_target_pairs={{0,256},{128,384},{256,0},{384,128},{1,257},{129,385},{257,1},{385... | collective-permute-start | bytes 221192 | tf_op jit(solution)/shard_map/ppermute | solution.py:145
  15.8 2.5 %collective-permute-start.7 = (bf16[96,384]{1,0:T(8,128)(2,1)S(1)}, bf16[96,384]{1,0:T(8,128)(2,1)S(1)}, u32[]{:S(2)}, u32[]{:S(2)}) collective-permute-start(bf16[96,384]{1,0:T(8,128)(2,1)S(1)} %get-tuple-element.11), channel_id=1, source_target_pairs={{0,128},{128,256},{256,384},{384,0},{1,129},{129,257},{257,385},{3... | collective-permute-start | bytes 221192 | tf_op jit(solution)/shard_map/ppermute | solution.py:145
  18.4 1.6 %collective-permute-done.8 = bf16[96,384]{1,0:T(8,128)(2,1)S(1)} collective-permute-done((bf16[96,384]{1,0:T(8,128)(2,1)S(1)}, bf16[96,384]{1,0:T(8,128)(2,1)S(1)}, u32[]{:S(2)}, u32[]{:S(2)}) %collective-permute-start.8) | collective-permute-done | bytes 73760 | tf_op jit(solution)/shard_map/ppermute | solution.py:145
  20.0 2.1 %collective-permute-done.7 = bf16[96,384]{1,0:T(8,128)(2,1)S(1)} collective-permute-done((bf16[96,384]{1,0:T(8,128)(2,1)S(1)}, bf16[96,384]{1,0:T(8,128)(2,1)S(1)}, u32[]{:S(2)}, u32[]{:S(2)}) %collective-permute-start.7) | collective-permute-done | bytes 73760 | tf_op jit(solution)/shard_map/ppermute | solution.py:145
  23.0 24.1 %all_to_all.10 = bf16[16,16,768]{2,1,0:T(8,128)(2,1)S(1)} all-to-all(bf16[16,16,768]{2,1,0:T(8,128)(2,1)} %bitcast.17), channel_id=1, replica_groups=mesh['x'=4,'y'=8,'z'=2,'c'=2,'dp'=4] {'y','c'}, dimensions={0} | all-to-all | bytes 786432 | tf_op jit(solution)/shard_map/all_to_all | solution.py:149
  47.0 4.0 %collective-permute-start = (bf16[8,32,768]{2,1,0:T(8,128)(2,1)S(1)}, bf16[8,32,768]{2,1,0:T(8,128)(2,1)S(1)}, u32[]{:S(2)}, u32[]{:S(2)}) collective-permute-start(bf16[8,32,768]{2,1,0:T(8,128)(2,1)S(1)} %bitcast.19), channel_id=1, source_target_pairs={{0,8},{8,0},{1,9},{9,1},{2,10},{10,2},{3,11},{11,3},{4,12},{12,4},... | collective-permute-start | bytes 1179656 | tf_op jit(solution)/shard_map/ppermute | solution.py:22
  51.0 1.9 %collective-permute-start.1 = (bf16[8,32,768]{2,1,0:T(8,128)(2,1)S(1)}, bf16[8,32,768]{2,1,0:T(8,128)(2,1)S(1)}, u32[]{:S(2)}, u32[]{:S(2)}) collective-permute-start(bf16[8,32,768]{2,1,0:T(8,128)(2,1)S(1)} %bitcast.20), channel_id=1, source_target_pairs={{0,128},{128,256},{256,384},{384,0},{1,129},{129,257},{257,385},{3... | collective-permute-start | bytes 1179656 | tf_op jit(solution)/shard_map/ppermute | solution.py:151
  52.9 4.6 %collective-permute-start.3 = (bf16[8,32,768]{2,1,0:T(8,128)(2,1)S(1)}, bf16[8,32,768]{2,1,0:T(8,128)(2,1)S(1)}, u32[]{:S(2)}, u32[]{:S(2)}) collective-permute-start(bf16[8,32,768]{2,1,0:T(8,128)(2,1)S(1)} %bitcast.21), channel_id=1, source_target_pairs={{0,384},{128,0},{256,128},{384,256},{1,385},{129,1},{257,129},{385... | collective-permute-start | bytes 1179656 | tf_op jit(solution)/shard_map/ppermute | solution.py:151
  57.5 2.7 %constant_dynamic-slice_fusion.3 = bf16[512,1536]{1,0:T(8,128)(2,1)} fusion(bf16[512,3072]{1,0:T(8,128)(2,1)} %param.7, s32[]{:T(128)S(6)} %select_n.24), kind=kLoop, calls=%fused_computation.4 | loop fusion | bytes 3145732 | tf_op jit(solution)/shard_map/dynamic_slice | solution.py:171
  60.2 3.6 %collective-permute-start.11 = (bf16[512,1536]{1,0:T(8,128)(2,1)}, bf16[512,1536]{1,0:T(8,128)(2,1)}, u32[]{:S(2)}, u32[]{:S(2)}) collective-permute-start(bf16[512,1536]{1,0:T(8,128)(2,1)} %constant_dynamic-slice_fusion.3), channel_id=1, source_target_pairs={{0,8},{8,0},{1,9},{9,1},{2,10},{10,2},{3,11},{11,3},{4,12},{12,4},... | collective-permute-start | bytes 4718600 | tf_op jit(solution)/shard_map/ppermute | solution.py:22
  63.8 1.9 %collective-permute-start.2 = (bf16[8,32,768]{2,1,0:T(8,128)(2,1)S(1)}, bf16[8,32,768]{2,1,0:T(8,128)(2,1)S(1)}, u32[]{:S(2)}, u32[]{:S(2)}) collective-permute-start(bf16[8,32,768]{2,1,0:T(8,128)(2,1)S(1)} %collective-permute-done.xb), channel_id=1, source_target_pairs={{0,128},{128,256},{256,384},{384,0},{1,129},{129,257},{257,385},{3... | collective-permute-start | bytes 1179656 | tf_op jit(solution)/shard_map/ppermute | solution.py:152
  65.8 4.6 %collective-permute-start.4 = (bf16[8,32,768]{2,1,0:T(8,128)(2,1)S(1)}, bf16[8,32,768]{2,1,0:T(8,128)(2,1)S(1)}, u32[]{:S(2)}, u32[]{:S(2)}) collective-permute-start(bf16[8,32,768]{2,1,0:T(8,128)(2,1)S(1)} %collective-permute-done.xb), channel_id=1, source_target_pairs={{0,384},{128,0},{256,128},{384,256},{1,385},{129,1},{257,129},{385... | collective-permute-start | bytes 1179656 | tf_op jit(solution)/shard_map/ppermute | solution.py:152
  70.4 1.9 %collective-permute-start.5 = (bf16[8,32,768]{2,1,0:T(8,128)(2,1)S(1)}, bf16[8,32,768]{2,1,0:T(8,128)(2,1)S(1)}, u32[]{:S(2)}, u32[]{:S(2)}) collective-permute-start(bf16[8,32,768]{2,1,0:T(8,128)(2,1)S(1)} %bitcast.22), channel_id=1, source_target_pairs={{0,256},{128,384},{256,0},{384,128},{1,257},{129,385},{257,1},{385... | collective-permute-start | bytes 1179656 | tf_op jit(solution)/shard_map/ppermute | solution.py:151
  72.3 4.9 %collective-permute-start.6 = (bf16[8,32,768]{2,1,0:T(8,128)(2,1)S(1)}, bf16[8,32,768]{2,1,0:T(8,128)(2,1)S(1)}, u32[]{:S(2)}, u32[]{:S(2)}) collective-permute-start(bf16[8,32,768]{2,1,0:T(8,128)(2,1)S(1)} %collective-permute-done.xb), channel_id=1, source_target_pairs={{0,256},{128,384},{256,0},{384,128},{1,257},{129,385},{257,1},{385... | collective-permute-start | bytes 1179656 | tf_op jit(solution)/shard_map/ppermute | solution.py:152
  77.2 17.1 %collective-permute-done.2.lb = bf16[8,32,768]{2,1,0:T(8,128)(2,1)S(1)} collective-permute-done((bf16[8,32,768]{2,1,0:T(8,128)(2,1)S(1)}, bf16[8,32,768]{2,1,0:T(8,128)(2,1)S(1)}, u32[]{:S(2)}, u32[]{:S(2)}) %collective-permute-start.2) | collective-permute-done | bytes 393248 | tf_op jit(solution)/shard_map/ppermute | solution.py:152
  95.0 2.1 %shard_map.46.normed = bf16[4,3,128,768]{3,2,1,0:T(8,128)(2,1)S(1)} custom-call(s32[3]{0:T(128)S(1)} %pad_add_fusion.place, bf16[8,32,768]{2,1,0:T(8,128)(2,1)S(1)} %bitcast.23, bf16[8,32,768]{2,1,0:T(8,128)(2,1)S(1)} %collective-permute-done.xb, bf16[8,32,768]{2,1,0:T(8,128)(2,1)S(1)} %collective-permute-done.1.la, ...), custom_call_target="tpu_custom_call" | custom-call | flops 10000000 | bytes 5000000 | tf_op jit(solution)/shard_map/pallas_call | solution.py:122
  97.8 0.8 copy-done.6
  98.6 2.3 %copy-done.3 = bf16[4,1536,384]{2,1,0:T(8,128)(2,1)S(1)} copy-done((bf16[4,1536,384]{2,1,0:T(8,128)(2,1)S(1)}, bf16[4,1536,384]{2,1,0:T(8,128)(2,1)}, u32[]{:S(2)}) %copy-start.3) | copy-done | bytes 4718616
  100.9 1.0 copy-done.5
  101.9 1.0 copy-done.7
  102.9 6.3 %shard_map.48 = bf16[4,8,2,16,256]{4,3,2,1,0:T(8,128)(2,1)} custom-call(s32[3]{0:T(128)S(1)} %pad_add_fusion.place, bf16[4,3,128,768]{3,2,1,0:T(8,128)(2,1)S(1)} %shard_map.46.normed, bf16[8,32,768]{2,1,0:T(8,128)(2,1)S(1)} %copy-done.5, bf16[8,32,768]{2,1,0:T(8,128)(2,1)S(1)} %copy-done.7, f32[4,1,768]{2,1,0:T(1,128)S(1)} %bitcast.28, ...), custom_call_target="tpu_custom_call" | custom-call | flops 3000000000 | bytes 9000000 | tf_op jit(solution)/shard_map/pallas_call | solution.py:122
  109.3 5.8 %all-to-all-start.1 = ((bf16[64,16,256]{2,1,0:T(8,128)(2,1)}), bf16[64,16,256]{2,1,0:T(8,128)(2,1)S(1)}, u32[]{:S(2)}, u32[]{:S(2)}) async-start(bf16[64,16,256]{2,1,0:T(8,128)(2,1)} %bitcast.11), calls=%async_computation.1 | async-start | bytes 1048576 | tf_op jit(solution)/shard_map/all_to_all | solution.py:178
  115.1 3.1 %constant_dynamic-slice_fusion.1 = (bf16[512,768]{1,0:T(8,128)(2,1)}, bf16[512,768]{1,0:T(8,128)(2,1)S(1)}) fusion(bf16[512,3072]{1,0:T(8,128)(2,1)} %param.7, s32[]{:T(128)S(6)} %dynamic_slice.25, s32[]{:T(128)S(6)} %dynamic_slice.21), kind=kLoop, calls=%fused_computation.2 | loop fusion | bytes 3145736 | tf_op jit(solution)/shard_map/dynamic_slice | solution.py:171
  118.2 4.5 %collective-permute-start.12 = (bf16[512,768]{1,0:T(8,128)(2,1)}, bf16[512,768]{1,0:T(8,128)(2,1)S(1)}, u32[]{:S(2)}, u32[]{:S(2)}) collective-permute-start(bf16[512,768]{1,0:T(8,128)(2,1)} %get-tuple-element.15), channel_id=1, source_target_pairs={{0,4},{4,0},{1,5},{5,1},{2,6},{6,2},{3,7},{7,3},{8,12},{12,8},{9,1... | collective-permute-start | bytes 2359304 | tf_op jit(solution)/shard_map/ppermute | solution.py:22
  122.7 2.4 %constant_dynamic-slice_fusion = (bf16[512,768]{1,0:T(8,128)(2,1)}, bf16[512,768]{1,0:T(8,128)(2,1)S(1)}) fusion(bf16[512,1536]{1,0:T(8,128)(2,1)} %collective-permute-done.11, s32[]{:T(128)S(6)} %select_n.25, s32[]{:T(128)S(6)} %select_n.20), kind=kLoop, calls=%fused_computation.1 | loop fusion | bytes 3145736 | tf_op jit(solution)/shard_map/dynamic_slice | solution.py:171
  125.2 1.9 %collective-permute-start.13 = (bf16[512,768]{1,0:T(8,128)(2,1)}, bf16[512,768]{1,0:T(8,128)(2,1)}, u32[]{:S(2)}, u32[]{:S(2)}) collective-permute-start(bf16[512,768]{1,0:T(8,128)(2,1)} %get-tuple-element.17), channel_id=1, source_target_pairs={{0,4},{4,0},{1,5},{5,1},{2,6},{6,2},{3,7},{7,3},{8,12},{12,8},{9,1... | collective-permute-start | bytes 2359304 | tf_op jit(solution)/shard_map/ppermute | solution.py:22
  127.1 2.4 %all-to-all-done.1 = bf16[64,16,256]{2,1,0:T(8,128)(2,1)S(1)} async-done(((bf16[64,16,256]{2,1,0:T(8,128)(2,1)}), bf16[64,16,256]{2,1,0:T(8,128)(2,1)S(1)}, u32[]{:S(2)}, u32[]{:S(2)}) %all-to-all-start.1) | async-done | bytes 524320 | tf_op jit(solution)/shard_map/all_to_all | solution.py:178
  129.4 6.3 %collective-permute-start.10 = (bf16[64,16,256]{2,1,0:T(8,128)(2,1)S(1)}, bf16[64,16,256]{2,1,0:T(8,128)(2,1)S(1)}, u32[]{:S(2)}, u32[]{:S(2)}) collective-permute-start(bf16[64,16,256]{2,1,0:T(8,128)(2,1)S(1)} %all-to-all-done.1), channel_id=1, source_target_pairs={{0,4},{4,0},{1,5},{5,1},{2,6},{6,2},{3,7},{7,3},{8,12},{12,8},{9,1... | collective-permute-start | bytes 1572872 | tf_op jit(solution)/shard_map/ppermute | solution.py:22
  135.8 1.5 %collective-permute-done.10 = bf16[64,16,256]{2,1,0:T(8,128)(2,1)S(1)} collective-permute-done((bf16[64,16,256]{2,1,0:T(8,128)(2,1)S(1)}, bf16[64,16,256]{2,1,0:T(8,128)(2,1)S(1)}, u32[]{:S(2)}, u32[]{:S(2)}) %collective-permute-start.10) | collective-permute-done | bytes 524320 | tf_op jit(solution)/shard_map/ppermute | solution.py:22
  137.3 3.0 %shard_map.49 = bf16[8,2,16,768]{3,2,1,0:T(8,128)(2,1)} custom-call(s32[3]{0:T(128)S(1)} %pad_add_fusion.place, bf16[4,8,2,16,256]{4,3,2,1,0:T(8,128)(2,1)S(1)} %bitcast.16, bf16[4,8,2,16,256]{4,3,2,1,0:T(8,128)(2,1)S(1)} %bitcast.24, bf16[512,768]{1,0:T(8,128)(2,1)S(1)} %get-tuple-element.16.wo00, bf16[512,768]{1,0:T(8,128)(2,1)S(1)} %get-tuple-element.18.wo10, ...), custom_call_target="tpu_custom_call" | custom-call | flops 800000000 | bytes 6000000 | tf_op jit(solution)/shard_map/pallas_call | solution.py:122
  (27 shorter events, 3.0 us)
Async XLA Ops:
  6.5 92.1 %all-gather.2.cloned.1.call-start = ((), (), s32[]{:S(2)}) async-start(), calls=%async_computation.2 | async-start | bytes 5013504 | tf_op jit(solution)/shard_map/all_gather | solution.py:146
  6.6 1.0 copy-start.1
  8.2 10.2 %collective-permute-start.9 = (bf16[96,384]{1,0:T(8,128)(2,1)S(1)}, bf16[96,384]{1,0:T(8,128)(2,1)S(1)}, u32[]{:S(2)}, u32[]{:S(2)}) collective-permute-start(bf16[96,384]{1,0:T(8,128)(2,1)S(1)} %get-tuple-element.13), channel_id=1, source_target_pairs={{0,384},{128,0},{256,128},{384,256},{1,385},{129,1},{257,129},{385... | collective-permute-start | bytes 221192 | tf_op jit(solution)/shard_map/ppermute | solution.py:145
  13.4 6.6 %collective-permute-start.8 = (bf16[96,384]{1,0:T(8,128)(2,1)S(1)}, bf16[96,384]{1,0:T(8,128)(2,1)S(1)}, u32[]{:S(2)}, u32[]{:S(2)}) collective-permute-start(bf16[96,384]{1,0:T(8,128)(2,1)S(1)} %get-tuple-element.12), channel_id=1, source_target_pairs={{0,256},{128,384},{256,0},{384,128},{1,257},{129,385},{257,1},{385... | collective-permute-start | bytes 221192 | tf_op jit(solution)/shard_map/ppermute | solution.py:145
  15.8 6.3 %collective-permute-start.7 = (bf16[96,384]{1,0:T(8,128)(2,1)S(1)}, bf16[96,384]{1,0:T(8,128)(2,1)S(1)}, u32[]{:S(2)}, u32[]{:S(2)}) collective-permute-start(bf16[96,384]{1,0:T(8,128)(2,1)S(1)} %get-tuple-element.11), channel_id=1, source_target_pairs={{0,128},{128,256},{256,384},{384,0},{1,129},{129,257},{257,385},{3... | collective-permute-start | bytes 221192 | tf_op jit(solution)/shard_map/ppermute | solution.py:145
  22.2 72.8 %copy-start.2 = (f32[3072]{0:T(1024)S(1)}, f32[3072]{0:T(1024)}, u32[]{:S(2)}) copy-start(f32[3072]{0:T(1024)} %param.5) | copy-start | bytes 36868
  47.0 13.2 %collective-permute-start = (bf16[8,32,768]{2,1,0:T(8,128)(2,1)S(1)}, bf16[8,32,768]{2,1,0:T(8,128)(2,1)S(1)}, u32[]{:S(2)}, u32[]{:S(2)}) collective-permute-start(bf16[8,32,768]{2,1,0:T(8,128)(2,1)S(1)} %bitcast.19), channel_id=1, source_target_pairs={{0,8},{8,0},{1,9},{9,1},{2,10},{10,2},{3,11},{11,3},{4,12},{12,4},... | collective-permute-start | bytes 1179656 | tf_op jit(solution)/shard_map/ppermute | solution.py:22
  51.0 19.3 %collective-permute-start.1 = (bf16[8,32,768]{2,1,0:T(8,128)(2,1)S(1)}, bf16[8,32,768]{2,1,0:T(8,128)(2,1)S(1)}, u32[]{:S(2)}, u32[]{:S(2)}) collective-permute-start(bf16[8,32,768]{2,1,0:T(8,128)(2,1)S(1)} %bitcast.20), channel_id=1, source_target_pairs={{0,128},{128,256},{256,384},{384,0},{1,129},{129,257},{257,385},{3... | collective-permute-start | bytes 1179656 | tf_op jit(solution)/shard_map/ppermute | solution.py:151
  52.9 19.3 %collective-permute-start.3 = (bf16[8,32,768]{2,1,0:T(8,128)(2,1)S(1)}, bf16[8,32,768]{2,1,0:T(8,128)(2,1)S(1)}, u32[]{:S(2)}, u32[]{:S(2)}) collective-permute-start(bf16[8,32,768]{2,1,0:T(8,128)(2,1)S(1)} %bitcast.21), channel_id=1, source_target_pairs={{0,384},{128,0},{256,128},{384,256},{1,385},{129,1},{257,129},{385... | collective-permute-start | bytes 1179656 | tf_op jit(solution)/shard_map/ppermute | solution.py:151
  60.2 62.5 %collective-permute-start.11 = (bf16[512,1536]{1,0:T(8,128)(2,1)}, bf16[512,1536]{1,0:T(8,128)(2,1)}, u32[]{:S(2)}, u32[]{:S(2)}) collective-permute-start(bf16[512,1536]{1,0:T(8,128)(2,1)} %constant_dynamic-slice_fusion.3), channel_id=1, source_target_pairs={{0,8},{8,0},{1,9},{9,1},{2,10},{10,2},{3,11},{11,3},{4,12},{12,4},... | collective-permute-start | bytes 4718600 | tf_op jit(solution)/shard_map/ppermute | solution.py:22
  63.8 30.4 %collective-permute-start.2 = (bf16[8,32,768]{2,1,0:T(8,128)(2,1)S(1)}, bf16[8,32,768]{2,1,0:T(8,128)(2,1)S(1)}, u32[]{:S(2)}, u32[]{:S(2)}) collective-permute-start(bf16[8,32,768]{2,1,0:T(8,128)(2,1)S(1)} %collective-permute-done.xb), channel_id=1, source_target_pairs={{0,128},{128,256},{256,384},{384,0},{1,129},{129,257},{257,385},{3... | collective-permute-start | bytes 1179656 | tf_op jit(solution)/shard_map/ppermute | solution.py:152
  65.8 29.2 %collective-permute-start.4 = (bf16[8,32,768]{2,1,0:T(8,128)(2,1)S(1)}, bf16[8,32,768]{2,1,0:T(8,128)(2,1)S(1)}, u32[]{:S(2)}, u32[]{:S(2)}) collective-permute-start(bf16[8,32,768]{2,1,0:T(8,128)(2,1)S(1)} %collective-permute-done.xb), channel_id=1, source_target_pairs={{0,384},{128,0},{256,128},{384,256},{1,385},{129,1},{257,129},{385... | collective-permute-start | bytes 1179656 | tf_op jit(solution)/shard_map/ppermute | solution.py:152
  70.4 26.7 %collective-permute-start.5 = (bf16[8,32,768]{2,1,0:T(8,128)(2,1)S(1)}, bf16[8,32,768]{2,1,0:T(8,128)(2,1)S(1)}, u32[]{:S(2)}, u32[]{:S(2)}) collective-permute-start(bf16[8,32,768]{2,1,0:T(8,128)(2,1)S(1)} %bitcast.22), channel_id=1, source_target_pairs={{0,256},{128,384},{256,0},{384,128},{1,257},{129,385},{257,1},{385... | collective-permute-start | bytes 1179656 | tf_op jit(solution)/shard_map/ppermute | solution.py:151
  72.3 25.5 %collective-permute-start.6 = (bf16[8,32,768]{2,1,0:T(8,128)(2,1)S(1)}, bf16[8,32,768]{2,1,0:T(8,128)(2,1)S(1)}, u32[]{:S(2)}, u32[]{:S(2)}) collective-permute-start(bf16[8,32,768]{2,1,0:T(8,128)(2,1)S(1)} %collective-permute-done.xb), channel_id=1, source_target_pairs={{0,256},{128,384},{256,0},{384,128},{1,257},{129,385},{257,1},{385... | collective-permute-start | bytes 1179656 | tf_op jit(solution)/shard_map/ppermute | solution.py:152
  97.1 0.7 copy-start.4
  97.8 0.8 copy-start.6
  98.6 2.3 %copy-start.3 = (bf16[4,1536,384]{2,1,0:T(8,128)(2,1)S(1)}, bf16[4,1536,384]{2,1,0:T(8,128)(2,1)}, u32[]{:S(2)}) copy-start(bf16[4,1536,384]{2,1,0:T(8,128)(2,1)} %all-gather.2.cloned.1.call-done.w_rows) | copy-start | bytes 14155780
  100.9 1.0 copy-start.5
  101.9 1.0 copy-start.7
  109.3 20.2 %all-to-all-start.1 = ((bf16[64,16,256]{2,1,0:T(8,128)(2,1)}), bf16[64,16,256]{2,1,0:T(8,128)(2,1)S(1)}, u32[]{:S(2)}, u32[]{:S(2)}) async-start(bf16[64,16,256]{2,1,0:T(8,128)(2,1)} %bitcast.11), calls=%async_computation.1 | async-start | bytes 1048576 | tf_op jit(solution)/shard_map/all_to_all | solution.py:178
  118.2 19.0 %copy-start = (bf16[1,1,256,768]{3,2,1,0:T(8,128)(2,1)S(1)}, bf16[1,1,256,768]{3,2,1,0:T(8,128)(2,1)}, u32[]{:S(2)}) copy-start(bf16[1,1,256,768]{3,2,1,0:T(8,128)(2,1)} %param.4) | copy-start | bytes 1179652
  118.2 17.5 %collective-permute-start.12 = (bf16[512,768]{1,0:T(8,128)(2,1)}, bf16[512,768]{1,0:T(8,128)(2,1)S(1)}, u32[]{:S(2)}, u32[]{:S(2)}) collective-permute-start(bf16[512,768]{1,0:T(8,128)(2,1)} %get-tuple-element.15), channel_id=1, source_target_pairs={{0,4},{4,0},{1,5},{5,1},{2,6},{6,2},{3,7},{7,3},{8,12},{12,8},{9,1... | collective-permute-start | bytes 2359304 | tf_op jit(solution)/shard_map/ppermute | solution.py:22
  125.2 10.6 %collective-permute-start.13 = (bf16[512,768]{1,0:T(8,128)(2,1)}, bf16[512,768]{1,0:T(8,128)(2,1)}, u32[]{:S(2)}, u32[]{:S(2)}) collective-permute-start(bf16[512,768]{1,0:T(8,128)(2,1)} %get-tuple-element.17), channel_id=1, source_target_pairs={{0,4},{4,0},{1,5},{5,1},{2,6},{6,2},{3,7},{7,3},{8,12},{12,8},{9,1... | collective-permute-start | bytes 2359304 | tf_op jit(solution)/shard_map/ppermute | solution.py:22
  129.4 7.8 %collective-permute-start.10 = (bf16[64,16,256]{2,1,0:T(8,128)(2,1)S(1)}, bf16[64,16,256]{2,1,0:T(8,128)(2,1)S(1)}, u32[]{:S(2)}, u32[]{:S(2)}) collective-permute-start(bf16[64,16,256]{2,1,0:T(8,128)(2,1)S(1)} %all-to-all-done.1), channel_id=1, source_target_pairs={{0,4},{4,0},{1,5},{5,1},{2,6},{6,2},{3,7},{7,3},{8,12},{12,8},{9,1... | collective-permute-start | bytes 1572872 | tf_op jit(solution)/shard_map/ppermute | solution.py:22
Sparse Core Ops, SparseCore 0:
  23.1 50.6 all-gather.1

commit v2 on v1

v2 whole, which is shorter than its diff:
```python
import jax
import jax.numpy as jnp
from jax import lax
from jax.experimental import pallas as pl
from jax.experimental.pallas import tpu as pltpu
from jax.sharding import Mesh, PartitionSpec as P

HD = 128
WIDTH = 3072
QUARTER = 768
F32 = jnp.float32
BF16 = jnp.bfloat16
VMEM = pl.BlockSpec(memory_space=pltpu.VMEM)
ANY = pl.BlockSpec(memory_space=pl.ANY)
SMEM = pl.BlockSpec(memory_space=pltpu.SMEM)


def ring(size, shift):
    return [(i, (i + shift) % size) for i in range(size)]


def swap(value, axis):
    return lax.ppermute(value, axis, [(0, 1), (1, 0)])


def normalize_block(z, near, far, gain, store):
    parts = []
    for z_far, side in enumerate((near, far)):
        for core in range(2):
            quarter = 2 * lax.rem(z + z_far, 2) + core
            piece = side[:, 16 * core : 16 * core + 16, :].reshape(128, QUARTER).astype(F32)
            parts.append((quarter, piece))
    total = parts[0][1] + parts[1][1] + parts[2][1] + parts[3][1]
    average = jnp.sum(total, axis=-1, keepdims=True) * (1.0 / WIDTH)
    squares = 0.0
    for _, value in parts:
        centred = value - average
        squares = squares + centred * centred
    spread = jnp.sum(squares, axis=-1, keepdims=True) * (1.0 / WIDTH)
    scale = lax.rsqrt(spread + 1e-06)
    for q, value in parts:
        store(q, ((value - average) * scale * gain[q]).astype(BF16))


def attend(projected):
    row = lax.broadcasted_iota(jnp.int32, (256, 256), 0)
    column = lax.broadcasted_iota(jnp.int32, (256, 256), 1)
    same_patch = lax.rem(row, 8) == lax.rem(column, 8)
    heads = []
    for core in range(2):
        groups = []
        for group in range(2):

            def pick(part, core=core, group=group):
                first = (3 * core + part) * HD
                rows = projected[:, first : first + HD].reshape(32, 16, HD)
                return rows[:, 8 * group : 8 * group + 8].reshape(256, HD).astype(BF16)

            query, key, value = pick(0), pick(1), pick(2)
            scores = lax.dot_general(query, key, (((1,), (1,)), ((), ())), preferred_element_type=F32)
            scores = jnp.where(same_patch, scores * HD**-0.5, -jnp.inf)
            weights = jnp.exp(scores - jnp.max(scores, axis=-1, keepdims=True))
            weights = (weights / jnp.sum(weights, axis=-1, keepdims=True)).astype(BF16)
            groups.append(jnp.dot(weights, value, preferred_element_type=F32).reshape(32, 8, HD))
        heads.append(jnp.concatenate(groups, axis=1))
    return jnp.concatenate(heads, axis=2).astype(BF16)


def attend_kernel(place, xa, xb, la, lb, ra, rb, oa_hbm, ob_hbm, gain, w_hbm, out, *scratch):
    opposite, normed, w_rows, projected, opposite_sent, w_sent = scratch
    x, z = place[0], place[1]
    copies = [
        pltpu.make_async_copy(source, opposite.at[i], opposite_sent.at[i])
        for i, source in enumerate((oa_hbm, ob_hbm))
    ]
    for k in range(4):
        for core in range(2):
            target = w_rows.at[pl.ds(QUARTER * k, QUARTER), pl.ds(3 * HD * core, 3 * HD)]
            source = w_hbm.at[k, pl.ds(QUARTER * core, QUARTER)]
            copies.append(pltpu.make_async_copy(source, target, w_sent.at[2 * k + core]))
    for copy in copies:
        copy.start()
    blocks = ((xa, xb), (la, lb), (ra, rb), (opposite.at[0], opposite.at[1]))
    for i, (near, far) in enumerate(blocks):
        rows = slice(128 * i, 128 * i + 128)

        def store(q, value, rows=rows):
            slot = pl.multiple_of(lax.rem(x + 4 - q, 4) * QUARTER, QUARTER)
            normed[rows, pl.ds(slot, QUARTER)] = value

        normalize_block(z, near, far, gain, store)
        if i == 1:
            for copy in copies:
                copy.wait()
            projected[:128] = jnp.dot(normed[:128], w_rows[...], preferred_element_type=F32)
        if i >= 1:
            projected[rows] = jnp.dot(normed[rows], w_rows[...], preferred_element_type=F32)
    attended = attend(projected[...])
    for i, shift in enumerate((0, 3, 1, 2)):
        frame = lax.rem(x + shift, 4)
        for chip in range(2):
            out[frame, :, chip] = attended[8 * i : 8 * i + 8]


def output_kernel(place, near, far, wo00, wo10, wo01, wo11, residual, out):
    z, c = place[1], place[2]
    total = jnp.zeros((256, QUARTER), F32)
    for z_far, weights in enumerate(((wo00, wo01), (wo10, wo11))):
        source = lax.rem(z + z_far, 2)
        for core in range(2):
            pieces = []
            for half in (near, far):
                columns = [
                    half[s, :, source, :, HD * core : HD * core + HD].reshape(128, HD) for s in range(4)
                ]
                pieces.append(jnp.concatenate(columns, axis=1))
            attended = jnp.concatenate(pieces, axis=0)
            weight = jnp.where(c == core, weights[0][...], weights[1][...])
            total = total + jnp.dot(attended, weight, preferred_element_type=F32)
    for half in range(2):
        side = lax.rem(c + half, 2)
        mixed = residual[:, side].astype(F32) + total[128 * half : 128 * half + 128].reshape(8, 16, QUARTER)
        out[:, side] = mixed.astype(BF16)


def slice_kernel(place, source, *outs):
    for k, out in enumerate(outs):
        head = lax.rem(place[0] + k, 4)
        for part in range(3):
            out[:, HD * part : HD * part + HD] = source[part, :, pl.ds(pl.multiple_of(head * HD, HD), HD)]


def after(value, *others):
    return lax.optimization_barrier((value, *others))[0]


def kernel_call(kernel, shapes, operands, flops, moved, mebibytes, scratch=(), left_out=()):
    return pl.pallas_call(
        kernel,
        out_shape=shapes,
        in_specs=[
            SMEM if value.dtype == jnp.int32 else ANY if i in left_out else VMEM
            for i, value in enumerate(operands)
        ],
        out_specs=jax.tree.map(lambda _: VMEM, shapes),
        scratch_shapes=list(scratch),
        compiler_params=pltpu.CompilerParams(vmem_limit_bytes=mebibytes * 2**20),
        cost_estimate=pl.CostEstimate(flops=flops, bytes_accessed=moved, transcendentals=0),
    )(*operands)


def body(frames_in, norm_gain, w_qkv, w_out):
    x, z, c = lax.axis_index("x"), lax.axis_index("z"), lax.axis_index("c")
    place = jnp.stack([x, z, c]).astype(jnp.int32)
    gain = norm_gain.reshape(4, 1, QUARTER)

    slots = kernel_call(
        slice_kernel,
        [jax.ShapeDtypeStruct((96, 3 * HD), BF16)] * 4,
        (place, w_qkv.transpose(1, 0, 2)),
        0,
        6 * 10**5,
        4,
    )
    w_rows = [slots[0]] + [lax.ppermute(slots[k], "x", ring(4, k)) for k in (1, 2, 3)]
    w_rows = jnp.stack(w_rows)

    tokens = frames_in.reshape(16, 16, QUARTER)
    xa = lax.all_to_all(tokens, ("y", "c"), 0, 0, tiled=True).reshape(8, 32, QUARTER)
    xa, w_rows = lax.optimization_barrier((xa, w_rows))
    w_rows = lax.all_gather(w_rows, ("c", "y"), axis=1, tiled=True)
    xb = swap(xa, "z")
    la, ra, oa = (lax.ppermute(xa, "x", ring(4, shift)) for shift in (1, 3, 2))
    xb_late = after(xb, la, ra)
    lb, rb, ob = (lax.ppermute(xb_late, "x", ring(4, shift)) for shift in (1, 3, 2))

    def half(value, index, size):
        return lax.dynamic_slice_in_dim(value, index * size, size, axis=1)

    columns = [2 * z + c, 2 * z + 1 - c]
    far_columns = [2 * (1 - z) + c, 2 * (1 - z) + 1 - c]
    w_late = after(w_out, xb)
    wo00 = half(w_out, columns[0], QUARTER)
    wo10 = swap(half(w_late, far_columns[0], QUARTER), "z")
    wo_side = swap(half(w_late, far_columns[1], QUARTER), "z")
    wo01 = swap(half(w_out, columns[1], QUARTER), "c")
    wo11 = swap(wo_side, "c")

    attended = kernel_call(
        attend_kernel,
        jax.ShapeDtypeStruct((4, 8, 2, 16, 2 * HD), BF16),
        (place, xa, xb, la, lb, ra, rb, oa, after(ob, wo10), gain, w_rows),
        3 * 10**9,
        9 * 10**6,
        57,
        [
            pltpu.VMEM((2, 8, 32, QUARTER), BF16),
            pltpu.VMEM((512, WIDTH), BF16),
            pltpu.VMEM((WIDTH, 6 * HD), BF16),
            pltpu.VMEM((512, 6 * HD), F32),
            pltpu.SemaphoreType.DMA((2,)),
            pltpu.SemaphoreType.DMA((8,)),
        ],
        left_out=(7, 8, 10),
    )

    attended = lax.all_to_all(attended.reshape(64, 16, 2 * HD), ("x", "y", "z"), 0, 0, tiled=True)
    other = swap(attended, "c")
    shape = (4, 8, 2, 16, 2 * HD)
    mixed = kernel_call(
        output_kernel,
        jax.ShapeDtypeStruct((8, 2, 16, QUARTER), BF16),
        (
            place,
            attended.reshape(shape),
            other.reshape(shape),
            wo00,
            wo10,
            wo01,
            wo11,
            frames_in.reshape(8, 2, 16, QUARTER),
        ),
        8 * 10**8,
        6 * 10**6,
        16,
    )
    return mixed.reshape(1, 1, 256, QUARTER)


def solution(mesh):
    fine = Mesh(mesh.devices.reshape(4, 8, 2, 2, 4), ("x", "y", "z", "c", "dp"))
    seq, tensor = ("x", "y"), ("z", "c")
    in_specs = (P("dp", seq, None, tensor), P(), P(seq, None, tensor), P(tensor, None))
    out_specs = P("dp", seq, None, tensor)
    return jax.shard_map(body, mesh=fine, in_specs=in_specs, out_specs=out_specs, check_vma=False)
```

time: 150 us -> 132 us (0.88); the launches traced: 147 us -> 131 us
  blocking collectives: 24.1 us -> 0 us
  local copies, waits for them, and re-layouts: 15 us -> 5.94 us
  starting transfers between devices: 56.1 us -> 64.5 us
  waiting for transfers between devices: 25.5 us -> 33.8 us
    all_to_all x1 -> x0, blocking collectives: 24.1 us -> none  [body(): lax.all_to_all(tokens, ('y', 'c'), 0, 0, tiled=True).reshape(8, 32, QUARTER)]
    all_to_all x0 -> x1, starting transfers between devices: none -> 10.2 us  [body(): lax.all_to_all(tokens, ('y', 'c'), 0, 0, tiled=True).reshape(8, 32, QUARTER)]
    ppermute x3, waiting for transfers between devices: 17.8 us -> 10.9 us  [body(): lax.ppermute(xb_late, 'x', ring(4, shift))]
    all_to_all x1, waiting for transfers between devices: 2.37 us -> 9.21 us  [body(): lax.all_to_all(attended.reshape(64, 16, 2 * HD), ('x', 'y', 'z'), 0, 0, t...]
    unnamed x16 -> x22, local copies, waits for them, and re-layouts: 6.82 us -> 1.01 us
    ppermute x3, waiting for transfers between devices: 0.01 us -> 5.1 us  [body(): la, ra, oa = (lax.ppermute(xa, 'x', ring(4, shift)) for shift in (1, 3, 2))]
    ppermute x5 -> x6, starting transfers between devices: 20.3 us -> 16.4 us  [swap(): return lax.ppermute(value, axis, [(0, 1), (1, 0)])]
    dynamic_slice x3 -> x2, local copies, waits for them, and re-layouts: 8.2 us -> 4.94 us  [half(): return lax.dynamic_slice_in_dim(value, index * size, size, axis=1)]
  transfers between devices with their start and end apart: 16 -> 18, of which waited for: 6 -> 10; matrix products, arithmetic and copies ran while one was open for 6% -> 4% of each run, Pallas kernels for 6% -> 7%
where the time goes in v2:
time: 132 us; the launch traced here: 131 us
  starting transfers between devices  64.5 us (49%)
  waiting for transfers between devices  33.8 us (26%)
  between operations  13.7 us (10%)
  Pallas kernels  12.5 us (9%)
  local copies, waits for them, and re-layouts  5.94 us (4%)
    ppermute x6, starting transfers between devices, swap(): return lax.ppermute(value, axis, [(0, 1), (1, 0)])  16.4 us
    pallas_call x3, Pallas kernels, kernel_call(): pl.pallas_call(kernel, out_shape=shapes, in_specs=[SMEM if value.dtype ==...  12.5 us
    ppermute x3, starting transfers between devices, body(): lax.ppermute(xb_late, 'x', ring(4, shift))  11.9 us
    ppermute x3, waiting for transfers between devices, body(): lax.ppermute(xb_late, 'x', ring(4, shift))  10.9 us
    all_to_all x1, starting transfers between devices, body(): lax.all_to_all(tokens, ('y', 'c'), 0, 0, tiled=True).reshape(8, 32, QUARTER)  10.2 us
    all_to_all x1, waiting for transfers between devices, body(): lax.all_to_all(attended.reshape(64, 16, 2 * HD), ('x', 'y', 'z'), 0, 0, t...  9.21 us
    ppermute x3, starting transfers between devices, body(): lax.ppermute(slots[k], 'x', ring(4, k))  8.96 us
    all_to_all x1, starting transfers between devices, body(): lax.all_to_all(attended.reshape(64, 16, 2 * HD), ('x', 'y', 'z'), 0, 0, t...  8.59 us
  transfers between devices with their start and end apart: 18, of which 10 were waited for; matrix products, arithmetic and copies ran while one was open for 4% of the time, Pallas kernels for 7%

profile of v2, /device:TPU:1, one launch (start us, length us, event | category | flops | bytes accessed | tf_op | source)
XLA Modules:
  0.0 131.2 jit_solution(15045787547222727675)
XLA Ops:
  6.5 10.2 %all-to-all-start = ((bf16[16,16,768]{2,1,0:T(8,128)(2,1)}), bf16[16,16,768]{2,1,0:T(8,128)(2,1)S(1)}, u32[]{:S(2)}, u32[]{:S(2)}) async-start(bf16[16,16,768]{2,1,0:T(8,128)(2,1)} %bitcast.17), calls=%async_computation | async-start | bytes 786432 | tf_op jit(solution)/shard_map/all_to_all | solution.py:169
  16.9 1.0 copy-done.1
  17.9 0.6 shard_map.46
  18.5 1.9 %collective-permute-start = (bf16[96,384]{1,0:T(8,128)(2,1)S(1)}, bf16[96,384]{1,0:T(8,128)(2,1)S(1)}, u32[]{:S(2)}, u32[]{:S(2)}) collective-permute-start(bf16[96,384]{1,0:T(8,128)(2,1)S(1)} %get-tuple-element.15), channel_id=1, source_target_pairs={{0,128},{128,256},{256,384},{384,0},{1,129},{129,257},{257,385},{3... | collective-permute-start | bytes 221192 | tf_op jit(solution)/shard_map/ppermute | solution.py:165
  20.4 4.0 %collective-permute-start.1 = (bf16[96,384]{1,0:T(8,128)(2,1)S(1)}, bf16[96,384]{1,0:T(8,128)(2,1)S(1)}, u32[]{:S(2)}, u32[]{:S(2)}) collective-permute-start(bf16[96,384]{1,0:T(8,128)(2,1)S(1)} %get-tuple-element.16), channel_id=1, source_target_pairs={{0,256},{128,384},{256,0},{384,128},{1,257},{129,385},{257,1},{385... | collective-permute-start | bytes 221192 | tf_op jit(solution)/shard_map/ppermute | solution.py:165
  24.4 3.1 %collective-permute-start.2 = (bf16[96,384]{1,0:T(8,128)(2,1)S(1)}, bf16[96,384]{1,0:T(8,128)(2,1)S(1)}, u32[]{:S(2)}, u32[]{:S(2)}) collective-permute-start(bf16[96,384]{1,0:T(8,128)(2,1)S(1)} %get-tuple-element.17), channel_id=1, source_target_pairs={{0,384},{128,0},{256,128},{384,256},{1,385},{129,1},{257,129},{385... | collective-permute-start | bytes 221192 | tf_op jit(solution)/shard_map/ppermute | solution.py:165
  27.5 2.3 %collective-permute-done.2 = bf16[96,384]{1,0:T(8,128)(2,1)S(1)} collective-permute-done((bf16[96,384]{1,0:T(8,128)(2,1)S(1)}, bf16[96,384]{1,0:T(8,128)(2,1)S(1)}, u32[]{:S(2)}, u32[]{:S(2)}) %collective-permute-start.2) | collective-permute-done | bytes 73760 | tf_op jit(solution)/shard_map/ppermute | solution.py:165
  29.8 0.8 pad_maximum_fusion
  30.5 0.8 all-to-all-done
  31.3 2.9 %collective-permute-start.3 = (bf16[8,32,768]{2,1,0:T(8,128)(2,1)S(1)}, bf16[8,32,768]{2,1,0:T(8,128)(2,1)S(1)}, u32[]{:S(2)}, u32[]{:S(2)}) collective-permute-start(bf16[8,32,768]{2,1,0:T(8,128)(2,1)S(1)} %bitcast.23), channel_id=1, source_target_pairs={{0,8},{8,0},{1,9},{9,1},{2,10},{10,2},{3,11},{11,3},{4,12},{12,4},... | collective-permute-start | bytes 1179656 | tf_op jit(solution)/shard_map/ppermute | solution.py:23
  34.3 2.6 %collective-permute-start.4 = (bf16[8,32,768]{2,1,0:T(8,128)(2,1)S(1)}, bf16[8,32,768]{2,1,0:T(8,128)(2,1)S(1)}, u32[]{:S(2)}, u32[]{:S(2)}) collective-permute-start(bf16[8,32,768]{2,1,0:T(8,128)(2,1)S(1)} %bitcast.24), channel_id=1, source_target_pairs={{0,128},{128,256},{256,384},{384,0},{1,129},{129,257},{257,385},{3... | collective-permute-start | bytes 1179656 | tf_op jit(solution)/shard_map/ppermute | solution.py:173
  36.9 3.9 %collective-permute-start.5 = (bf16[8,32,768]{2,1,0:T(8,128)(2,1)S(1)}, bf16[8,32,768]{2,1,0:T(8,128)(2,1)S(1)}, u32[]{:S(2)}, u32[]{:S(2)}) collective-permute-start(bf16[8,32,768]{2,1,0:T(8,128)(2,1)S(1)} %bitcast.25), channel_id=1, source_target_pairs={{0,384},{128,0},{256,128},{384,256},{1,385},{129,1},{257,129},{385... | collective-permute-start | bytes 1179656 | tf_op jit(solution)/shard_map/ppermute | solution.py:173
  40.8 2.0 %collective-permute-done.3.xb = bf16[8,32,768]{2,1,0:T(8,128)(2,1)S(1)} collective-permute-done((bf16[8,32,768]{2,1,0:T(8,128)(2,1)S(1)}, bf16[8,32,768]{2,1,0:T(8,128)(2,1)S(1)}, u32[]{:S(2)}, u32[]{:S(2)}) %collective-permute-start.3) | collective-permute-done | bytes 393248 | tf_op jit(solution)/shard_map/ppermute | solution.py:23
  42.8 2.5 %constant_dynamic-slice_fusion = (bf16[512,768]{1,0:T(8,128)(2,1)}, bf16[512,768]{1,0:T(8,128)(2,1)S(1)}) fusion(bf16[512,3072]{1,0:T(8,128)(2,1)} %param.7, s32[]{:T(128)S(6)} %select_n.15, s32[]{:T(128)S(6)} %select_n.12), kind=kLoop, calls=%fused_computation.1 | loop fusion | bytes 3145736 | tf_op jit(solution)/shard_map/dynamic_slice | solution.py:178
  45.3 2.2 %collective-permute-start.10 = (bf16[512,768]{1,0:T(8,128)(2,1)S(1)}, bf16[512,768]{1,0:T(8,128)(2,1)S(1)}, u32[]{:S(2)}, u32[]{:S(2)}) collective-permute-start(bf16[512,768]{1,0:T(8,128)(2,1)S(1)} %get-tuple-element.24), channel_id=1, source_target_pairs={{0,8},{8,0},{1,9},{9,1},{2,10},{10,2},{3,11},{11,3},{4,12},{12,4},... | collective-permute-start | bytes 2359304 | tf_op jit(solution)/shard_map/ppermute | solution.py:23
  48.0 5.4 %collective-permute-start.9 = (bf16[8,32,768]{2,1,0:T(8,128)(2,1)S(1)}, bf16[8,32,768]{2,1,0:T(8,128)(2,1)S(1)}, u32[]{:S(2)}, u32[]{:S(2)}) collective-permute-start(bf16[8,32,768]{2,1,0:T(8,128)(2,1)S(1)} %collective-permute-done.3.xb), channel_id=1, source_target_pairs={{0,256},{128,384},{256,0},{384,128},{1,257},{129,385},{257,1},{385... | collective-permute-start | bytes 1179656 | tf_op jit(solution)/shard_map/ppermute | solution.py:175
  53.4 1.9 %collective-permute-start.8 = (bf16[8,32,768]{2,1,0:T(8,128)(2,1)S(1)}, bf16[8,32,768]{2,1,0:T(8,128)(2,1)S(1)}, u32[]{:S(2)}, u32[]{:S(2)}) collective-permute-start(bf16[8,32,768]{2,1,0:T(8,128)(2,1)S(1)} %bitcast.26), channel_id=1, source_target_pairs={{0,256},{128,384},{256,0},{384,128},{1,257},{129,385},{257,1},{385... | collective-permute-start | bytes 1179656 | tf_op jit(solution)/shard_map/ppermute | solution.py:173
  55.3 2.7 %collective-permute-start.6 = (bf16[8,32,768]{2,1,0:T(8,128)(2,1)S(1)}, bf16[8,32,768]{2,1,0:T(8,128)(2,1)S(1)}, u32[]{:S(2)}, u32[]{:S(2)}) collective-permute-start(bf16[8,32,768]{2,1,0:T(8,128)(2,1)S(1)} %collective-permute-done.3.xb), channel_id=1, source_target_pairs={{0,128},{128,256},{256,384},{384,0},{1,129},{129,257},{257,385},{3... | collective-permute-start | bytes 1179656 | tf_op jit(solution)/shard_map/ppermute | solution.py:175
  58.0 3.8 %collective-permute-start.7 = (bf16[8,32,768]{2,1,0:T(8,128)(2,1)S(1)}, bf16[8,32,768]{2,1,0:T(8,128)(2,1)}, u32[]{:S(2)}, u32[]{:S(2)}) collective-permute-start(bf16[8,32,768]{2,1,0:T(8,128)(2,1)S(1)} %collective-permute-done.3.xb), channel_id=1, source_target_pairs={{0,384},{128,0},{256,128},{384,256},{1,385},{129,1},{257,129},{385... | collective-permute-start | bytes 1179656 | tf_op jit(solution)/shard_map/ppermute | solution.py:175
  61.9 2.2 %collective-permute-start.13 = (bf16[512,768]{1,0:T(8,128)(2,1)}, bf16[512,768]{1,0:T(8,128)(2,1)}, u32[]{:S(2)}, u32[]{:S(2)}) collective-permute-start(bf16[512,768]{1,0:T(8,128)(2,1)} %get-tuple-element.23), channel_id=1, source_target_pairs={{0,8},{8,0},{1,9},{9,1},{2,10},{10,2},{3,11},{11,3},{4,12},{12,4},... | collective-permute-start | bytes 2359304 | tf_op jit(solution)/shard_map/ppermute | solution.py:23
  64.3 4.7 %collective-permute-done.8.oa_hbm = bf16[8,32,768]{2,1,0:T(8,128)(2,1)S(1)} collective-permute-done((bf16[8,32,768]{2,1,0:T(8,128)(2,1)S(1)}, bf16[8,32,768]{2,1,0:T(8,128)(2,1)S(1)}, u32[]{:S(2)}, u32[]{:S(2)}) %collective-permute-start.8) | collective-permute-done | bytes 393248 | tf_op jit(solution)/shard_map/ppermute | solution.py:173
  69.0 10.9 %collective-permute-done.6.lb = bf16[8,32,768]{2,1,0:T(8,128)(2,1)S(1)} collective-permute-done((bf16[8,32,768]{2,1,0:T(8,128)(2,1)S(1)}, bf16[8,32,768]{2,1,0:T(8,128)(2,1)S(1)}, u32[]{:S(2)}, u32[]{:S(2)}) %collective-permute-start.6) | collective-permute-done | bytes 393248 | tf_op jit(solution)/shard_map/ppermute | solution.py:175
  79.9 1.7 %all-gather.2.cloned.1.call-done.w_hbm = bf16[4,1536,384]{2,1,0:T(8,128)(2,1)} async-done(((bf16[4,96,384]{2,1,0:T(8,128)(2,1)}), bf16[4,1536,384]{2,1,0:T(8,128)(2,1)}) %all-gather.2.cloned.1.call-update) | async-done | bytes 4718608 | tf_op jit(solution)/shard_map/all_gather | solution.py:171
  81.7 8.9 %shard_map.47 = bf16[4,8,2,16,256]{4,3,2,1,0:T(8,128)(2,1)} custom-call(s32[3]{0:T(128)} %copy-done.2, bf16[8,32,768]{2,1,0:T(8,128)(2,1)} %bitcast.27, bf16[8,32,768]{2,1,0:T(8,128)(2,1)} %copy-done.5, bf16[8,32,768]{2,1,0:T(8,128)(2,1)} %copy-done.6, bf16[8,32,768]{2,1,0:T(8,128)(2,1)} %copy-done.10, bf16[8,32,768]{2,1,0:T(8,128)(2,1)} %copy-done.7, ...), custom_call_target="tpu_custom_call" | custom-call | flops 3000000000 | bytes 9000000 | tf_op jit(solution)/shard_map/pallas_call | solution.py:138
  90.6 8.6 %all-to-all-start.1 = ((bf16[64,16,256]{2,1,0:T(8,128)(2,1)}), bf16[64,16,256]{2,1,0:T(8,128)(2,1)S(1)}, u32[]{:S(2)}, u32[]{:S(2)}) async-start(bf16[64,16,256]{2,1,0:T(8,128)(2,1)} %bitcast.22), calls=%async_computation.1 | async-start | bytes 1048576 | tf_op jit(solution)/shard_map/all_to_all | solution.py:207
  99.2 2.4 %constant_dynamic-slice_fusion.1 = (bf16[512,768]{1,0:T(8,128)(2,1)}, bf16[512,768]{1,0:T(8,128)(2,1)S(1)}) fusion(bf16[512,3072]{1,0:T(8,128)(2,1)} %param.7, s32[]{:T(128)S(6)} %select_n.14, s32[]{:T(128)S(6)} %select_n.13), kind=kLoop, calls=%fused_computation.2 | loop fusion | bytes 3145736 | tf_op jit(solution)/shard_map/dynamic_slice | solution.py:178
  101.6 2.4 %collective-permute-start.12 = (bf16[512,768]{1,0:T(8,128)(2,1)}, bf16[512,768]{1,0:T(8,128)(2,1)S(1)}, u32[]{:S(2)}, u32[]{:S(2)}) collective-permute-start(bf16[512,768]{1,0:T(8,128)(2,1)} %get-tuple-element.25), channel_id=1, source_target_pairs={{0,4},{4,0},{1,5},{5,1},{2,6},{6,2},{3,7},{7,3},{8,12},{12,8},{9,1... | collective-permute-start | bytes 2359304 | tf_op jit(solution)/shard_map/ppermute | solution.py:23
  104.0 1.9 %collective-permute-start.14 = (bf16[512,768]{1,0:T(8,128)(2,1)}, bf16[512,768]{1,0:T(8,128)(2,1)}, u32[]{:S(2)}, u32[]{:S(2)}) collective-permute-start(bf16[512,768]{1,0:T(8,128)(2,1)} %collective-permute-done.13), channel_id=1, source_target_pairs={{0,4},{4,0},{1,5},{5,1},{2,6},{6,2},{3,7},{7,3},{8,12},{12,8},{9,1... | collective-permute-start | bytes 2359304 | tf_op jit(solution)/shard_map/ppermute | solution.py:23
  106.0 9.2 %all-to-all-done.1 = bf16[64,16,256]{2,1,0:T(8,128)(2,1)S(1)} async-done(((bf16[64,16,256]{2,1,0:T(8,128)(2,1)}), bf16[64,16,256]{2,1,0:T(8,128)(2,1)S(1)}, u32[]{:S(2)}, u32[]{:S(2)}) %all-to-all-start.1) | async-done | bytes 524320 | tf_op jit(solution)/shard_map/all_to_all | solution.py:207
  115.2 4.7 %collective-permute-start.11 = (bf16[64,16,256]{2,1,0:T(8,128)(2,1)S(1)}, bf16[64,16,256]{2,1,0:T(8,128)(2,1)S(1)}, u32[]{:S(2)}, u32[]{:S(2)}) collective-permute-start(bf16[64,16,256]{2,1,0:T(8,128)(2,1)S(1)} %all-to-all-done.1), channel_id=1, source_target_pairs={{0,4},{4,0},{1,5},{5,1},{2,6},{6,2},{3,7},{7,3},{8,12},{12,8},{9,1... | collective-permute-start | bytes 1572872 | tf_op jit(solution)/shard_map/ppermute | solution.py:23
  119.9 1.5 %collective-permute-done.11 = bf16[64,16,256]{2,1,0:T(8,128)(2,1)S(1)} collective-permute-done((bf16[64,16,256]{2,1,0:T(8,128)(2,1)S(1)}, bf16[64,16,256]{2,1,0:T(8,128)(2,1)S(1)}, u32[]{:S(2)}, u32[]{:S(2)}) %collective-permute-start.11) | collective-permute-done | bytes 524320 | tf_op jit(solution)/shard_map/ppermute | solution.py:23
  121.4 3.0 %shard_map.48 = bf16[8,2,16,768]{3,2,1,0:T(8,128)(2,1)} custom-call(s32[3]{0:T(128)S(1)} %copy-done.3, bf16[4,8,2,16,256]{4,3,2,1,0:T(8,128)(2,1)S(1)} %bitcast.16, bf16[4,8,2,16,256]{4,3,2,1,0:T(8,128)(2,1)S(1)} %bitcast.19, bf16[512,768]{1,0:T(8,128)(2,1)S(1)} %get-tuple-element.26.wo00, bf16[512,768]{1,0:T(8,128)(2,1)S(1)} %collective-permute-done.10.wo10, ...), custom_call_target="tpu_custom_call" | custom-call | flops 800000000 | bytes 6000000 | tf_op jit(solution)/shard_map/pallas_call | solution.py:138
  (34 shorter events, 0.9 us)
Async XLA Ops:
  6.5 24.8 %all-to-all-start = ((bf16[16,16,768]{2,1,0:T(8,128)(2,1)}), bf16[16,16,768]{2,1,0:T(8,128)(2,1)S(1)}, u32[]{:S(2)}, u32[]{:S(2)}) async-start(bf16[16,16,768]{2,1,0:T(8,128)(2,1)} %bitcast.17), calls=%async_computation | async-start | bytes 786432 | tf_op jit(solution)/shard_map/all_to_all | solution.py:169
  16.8 64.9 %all-gather.2.cloned.1.call-start = ((), (), s32[]{:S(2)}) async-start(), calls=%async_computation.2 | async-start | bytes 5013504 | tf_op jit(solution)/shard_map/all_gather | solution.py:171
  16.9 64.8 %copy-start.2 = (s32[3]{0:T(128)}, s32[3]{0:T(128)S(1)}, u32[]{:S(2)}) copy-start(s32[3]{0:T(128)S(1)} %pad_add_fusion.place) | copy-start | bytes 40
  16.9 1.0 copy-start.1
  18.5 9.0 %collective-permute-start = (bf16[96,384]{1,0:T(8,128)(2,1)S(1)}, bf16[96,384]{1,0:T(8,128)(2,1)S(1)}, u32[]{:S(2)}, u32[]{:S(2)}) collective-permute-start(bf16[96,384]{1,0:T(8,128)(2,1)S(1)} %get-tuple-element.15), channel_id=1, source_target_pairs={{0,128},{128,256},{256,384},{384,0},{1,129},{129,257},{257,385},{3... | collective-permute-start | bytes 221192 | tf_op jit(solution)/shard_map/ppermute | solution.py:165
  20.4 7.1 %collective-permute-start.1 = (bf16[96,384]{1,0:T(8,128)(2,1)S(1)}, bf16[96,384]{1,0:T(8,128)(2,1)S(1)}, u32[]{:S(2)}, u32[]{:S(2)}) collective-permute-start(bf16[96,384]{1,0:T(8,128)(2,1)S(1)} %get-tuple-element.16), channel_id=1, source_target_pairs={{0,256},{128,384},{256,0},{384,128},{1,257},{129,385},{257,1},{385... | collective-permute-start | bytes 221192 | tf_op jit(solution)/shard_map/ppermute | solution.py:165
  24.4 5.4 %collective-permute-start.2 = (bf16[96,384]{1,0:T(8,128)(2,1)S(1)}, bf16[96,384]{1,0:T(8,128)(2,1)S(1)}, u32[]{:S(2)}, u32[]{:S(2)}) collective-permute-start(bf16[96,384]{1,0:T(8,128)(2,1)S(1)} %get-tuple-element.17), channel_id=1, source_target_pairs={{0,384},{128,0},{256,128},{384,256},{1,385},{129,1},{257,129},{385... | collective-permute-start | bytes 221192 | tf_op jit(solution)/shard_map/ppermute | solution.py:165
  31.3 50.3 %copy-start.4 = (bf16[16,16,768]{2,1,0:T(8,128)(2,1)}, bf16[16,16,768]{2,1,0:T(8,128)(2,1)S(1)}, u32[]{:S(2)}) copy-start(bf16[16,16,768]{2,1,0:T(8,128)(2,1)S(1)} %all-to-all-done) | copy-start | bytes 1179652
  31.3 11.4 %collective-permute-start.3 = (bf16[8,32,768]{2,1,0:T(8,128)(2,1)S(1)}, bf16[8,32,768]{2,1,0:T(8,128)(2,1)S(1)}, u32[]{:S(2)}, u32[]{:S(2)}) collective-permute-start(bf16[8,32,768]{2,1,0:T(8,128)(2,1)S(1)} %bitcast.23), channel_id=1, source_target_pairs={{0,8},{8,0},{1,9},{9,1},{2,10},{10,2},{3,11},{11,3},{4,12},{12,4},... | collective-permute-start | bytes 1179656 | tf_op jit(solution)/shard_map/ppermute | solution.py:23
  34.3 13.2 %collective-permute-start.4 = (bf16[8,32,768]{2,1,0:T(8,128)(2,1)S(1)}, bf16[8,32,768]{2,1,0:T(8,128)(2,1)S(1)}, u32[]{:S(2)}, u32[]{:S(2)}) collective-permute-start(bf16[8,32,768]{2,1,0:T(8,128)(2,1)S(1)} %bitcast.24), channel_id=1, source_target_pairs={{0,128},{128,256},{256,384},{384,0},{1,129},{129,257},{257,385},{3... | collective-permute-start | bytes 1179656 | tf_op jit(solution)/shard_map/ppermute | solution.py:173
  36.9 11.1 %collective-permute-start.5 = (bf16[8,32,768]{2,1,0:T(8,128)(2,1)S(1)}, bf16[8,32,768]{2,1,0:T(8,128)(2,1)S(1)}, u32[]{:S(2)}, u32[]{:S(2)}) collective-permute-start(bf16[8,32,768]{2,1,0:T(8,128)(2,1)S(1)} %bitcast.25), channel_id=1, source_target_pairs={{0,384},{128,0},{256,128},{384,256},{1,385},{129,1},{257,129},{385... | collective-permute-start | bytes 1179656 | tf_op jit(solution)/shard_map/ppermute | solution.py:173
  42.7 38.9 %copy-start.5 = (bf16[8,32,768]{2,1,0:T(8,128)(2,1)}, bf16[8,32,768]{2,1,0:T(8,128)(2,1)S(1)}, u32[]{:S(2)}) copy-start(bf16[8,32,768]{2,1,0:T(8,128)(2,1)S(1)} %collective-permute-done.3.xb) | copy-start | bytes 1179652
  45.3 19.0 %collective-permute-start.10 = (bf16[512,768]{1,0:T(8,128)(2,1)S(1)}, bf16[512,768]{1,0:T(8,128)(2,1)S(1)}, u32[]{:S(2)}, u32[]{:S(2)}) collective-permute-start(bf16[512,768]{1,0:T(8,128)(2,1)S(1)} %get-tuple-element.24), channel_id=1, source_target_pairs={{0,8},{8,0},{1,9},{9,1},{2,10},{10,2},{3,11},{11,3},{4,12},{12,4},... | collective-permute-start | bytes 2359304 | tf_op jit(solution)/shard_map/ppermute | solution.py:23
  47.5 34.1 %copy-start.6 = (bf16[8,32,768]{2,1,0:T(8,128)(2,1)}, bf16[8,32,768]{2,1,0:T(8,128)(2,1)S(1)}, u32[]{:S(2)}) copy-start(bf16[8,32,768]{2,1,0:T(8,128)(2,1)S(1)} %collective-permute-done.4.la) | copy-start | bytes 1179652
  48.0 33.7 %copy-start.7 = (bf16[8,32,768]{2,1,0:T(8,128)(2,1)}, bf16[8,32,768]{2,1,0:T(8,128)(2,1)S(1)}, u32[]{:S(2)}) copy-start(bf16[8,32,768]{2,1,0:T(8,128)(2,1)S(1)} %collective-permute-done.5.ra) | copy-start | bytes 1179652
  48.0 13.9 %collective-permute-start.9 = (bf16[8,32,768]{2,1,0:T(8,128)(2,1)S(1)}, bf16[8,32,768]{2,1,0:T(8,128)(2,1)S(1)}, u32[]{:S(2)}, u32[]{:S(2)}) collective-permute-start(bf16[8,32,768]{2,1,0:T(8,128)(2,1)S(1)} %collective-permute-done.3.xb), channel_id=1, source_target_pairs={{0,256},{128,384},{256,0},{384,128},{1,257},{129,385},{257,1},{385... | collective-permute-start | bytes 1179656 | tf_op jit(solution)/shard_map/ppermute | solution.py:175
  53.4 15.6 %collective-permute-start.8 = (bf16[8,32,768]{2,1,0:T(8,128)(2,1)S(1)}, bf16[8,32,768]{2,1,0:T(8,128)(2,1)S(1)}, u32[]{:S(2)}, u32[]{:S(2)}) collective-permute-start(bf16[8,32,768]{2,1,0:T(8,128)(2,1)S(1)} %bitcast.26), channel_id=1, source_target_pairs={{0,256},{128,384},{256,0},{384,128},{1,257},{129,385},{257,1},{385... | collective-permute-start | bytes 1179656 | tf_op jit(solution)/shard_map/ppermute | solution.py:173
  55.3 24.6 %collective-permute-start.6 = (bf16[8,32,768]{2,1,0:T(8,128)(2,1)S(1)}, bf16[8,32,768]{2,1,0:T(8,128)(2,1)S(1)}, u32[]{:S(2)}, u32[]{:S(2)}) collective-permute-start(bf16[8,32,768]{2,1,0:T(8,128)(2,1)S(1)} %collective-permute-done.3.xb), channel_id=1, source_target_pairs={{0,128},{128,256},{256,384},{384,0},{1,129},{129,257},{257,385},{3... | collective-permute-start | bytes 1179656 | tf_op jit(solution)/shard_map/ppermute | solution.py:175
  58.0 21.9 %collective-permute-start.7 = (bf16[8,32,768]{2,1,0:T(8,128)(2,1)S(1)}, bf16[8,32,768]{2,1,0:T(8,128)(2,1)}, u32[]{:S(2)}, u32[]{:S(2)}) collective-permute-start(bf16[8,32,768]{2,1,0:T(8,128)(2,1)S(1)} %collective-permute-done.3.xb), channel_id=1, source_target_pairs={{0,384},{128,0},{256,128},{384,256},{1,385},{129,1},{257,129},{385... | collective-permute-start | bytes 1179656 | tf_op jit(solution)/shard_map/ppermute | solution.py:175
  61.9 19.8 %copy-start.8 = (bf16[8,32,768]{2,1,0:T(8,128)(2,1)}, bf16[8,32,768]{2,1,0:T(8,128)(2,1)S(1)}, u32[]{:S(2)}) copy-start(bf16[8,32,768]{2,1,0:T(8,128)(2,1)S(1)} %collective-permute-done.9.ob_hbm) | copy-start | bytes 1179652
  61.9 42.2 %collective-permute-start.13 = (bf16[512,768]{1,0:T(8,128)(2,1)}, bf16[512,768]{1,0:T(8,128)(2,1)}, u32[]{:S(2)}, u32[]{:S(2)}) collective-permute-start(bf16[512,768]{1,0:T(8,128)(2,1)} %get-tuple-element.23), channel_id=1, source_target_pairs={{0,8},{8,0},{1,9},{9,1},{2,10},{10,2},{3,11},{11,3},{4,12},{12,4},... | collective-permute-start | bytes 2359304 | tf_op jit(solution)/shard_map/ppermute | solution.py:23
  69.0 12.7 %copy-start.9 = (bf16[8,32,768]{2,1,0:T(8,128)(2,1)}, bf16[8,32,768]{2,1,0:T(8,128)(2,1)S(1)}, u32[]{:S(2)}) copy-start(bf16[8,32,768]{2,1,0:T(8,128)(2,1)S(1)} %collective-permute-done.8.oa_hbm) | copy-start | bytes 1179652
  79.9 1.8 %copy-start.10 = (bf16[8,32,768]{2,1,0:T(8,128)(2,1)}, bf16[8,32,768]{2,1,0:T(8,128)(2,1)S(1)}, u32[]{:S(2)}) copy-start(bf16[8,32,768]{2,1,0:T(8,128)(2,1)S(1)} %collective-permute-done.6.lb) | copy-start | bytes 1179652
  90.5 30.8 %copy-start = (bf16[1,1,256,768]{3,2,1,0:T(8,128)(2,1)S(1)}, bf16[1,1,256,768]{3,2,1,0:T(8,128)(2,1)}, u32[]{:S(2)}) copy-start(bf16[1,1,256,768]{3,2,1,0:T(8,128)(2,1)} %param.4) | copy-start | bytes 1179652
  90.6 30.8 %copy-start.3 = (s32[3]{0:T(128)S(1)}, s32[3]{0:T(128)}, u32[]{:S(2)}) copy-start(s32[3]{0:T(128)} %copy-done.2) | copy-start | bytes 40
  90.6 24.6 %all-to-all-start.1 = ((bf16[64,16,256]{2,1,0:T(8,128)(2,1)}), bf16[64,16,256]{2,1,0:T(8,128)(2,1)S(1)}, u32[]{:S(2)}, u32[]{:S(2)}) async-start(bf16[64,16,256]{2,1,0:T(8,128)(2,1)} %bitcast.22), calls=%async_computation.1 | async-start | bytes 1048576 | tf_op jit(solution)/shard_map/all_to_all | solution.py:207
  101.6 18.3 %collective-permute-start.12 = (bf16[512,768]{1,0:T(8,128)(2,1)}, bf16[512,768]{1,0:T(8,128)(2,1)S(1)}, u32[]{:S(2)}, u32[]{:S(2)}) collective-permute-start(bf16[512,768]{1,0:T(8,128)(2,1)} %get-tuple-element.25), channel_id=1, source_target_pairs={{0,4},{4,0},{1,5},{5,1},{2,6},{6,2},{3,7},{7,3},{8,12},{12,8},{9,1... | collective-permute-start | bytes 2359304 | tf_op jit(solution)/shard_map/ppermute | solution.py:23
  104.0 15.8 %collective-permute-start.14 = (bf16[512,768]{1,0:T(8,128)(2,1)}, bf16[512,768]{1,0:T(8,128)(2,1)}, u32[]{:S(2)}, u32[]{:S(2)}) collective-permute-start(bf16[512,768]{1,0:T(8,128)(2,1)} %collective-permute-done.13), channel_id=1, source_target_pairs={{0,4},{4,0},{1,5},{5,1},{2,6},{6,2},{3,7},{7,3},{8,12},{12,8},{9,1... | collective-permute-start | bytes 2359304 | tf_op jit(solution)/shard_map/ppermute | solution.py:23
  115.2 6.2 %collective-permute-start.11 = (bf16[64,16,256]{2,1,0:T(8,128)(2,1)S(1)}, bf16[64,16,256]{2,1,0:T(8,128)(2,1)S(1)}, u32[]{:S(2)}, u32[]{:S(2)}) collective-permute-start(bf16[64,16,256]{2,1,0:T(8,128)(2,1)S(1)} %all-to-all-done.1), channel_id=1, source_target_pairs={{0,4},{4,0},{1,5},{5,1},{2,6},{6,2},{3,7},{7,3},{8,12},{12,8},{9,1... | collective-permute-start | bytes 1572872 | tf_op jit(solution)/shard_map/ppermute | solution.py:23
Sparse Core Ops, SparseCore 0:
  31.5 50.1 all-gather.1

commit v3 on v2

--- a/solution.py
+++ b/solution.py
@@ -66,13 +66,10 @@
     return jnp.concatenate(heads, axis=2).astype(BF16)
 
 
-def attend_kernel(place, xa, xb, la, lb, ra, rb, oa_hbm, ob_hbm, gain, w_hbm, out, *scratch):
-    opposite, normed, w_rows, projected, opposite_sent, w_sent = scratch
+def attend_kernel(place, xa, xb, la, lb, ra, rb, opposite, gain, w_hbm, out, *scratch):
+    normed, w_rows, projected, w_sent = scratch
     x, z = place[0], place[1]
-    copies = [
-        pltpu.make_async_copy(source, opposite.at[i], opposite_sent.at[i])
-        for i, source in enumerate((oa_hbm, ob_hbm))
-    ]
+    copies = []
     for k in range(4):
         for core in range(2):
             target = w_rows.at[pl.ds(QUARTER * k, QUARTER), pl.ds(3 * HD * core, 3 * HD)]
@@ -89,12 +86,11 @@
             normed[rows, pl.ds(slot, QUARTER)] = value
 
         normalize_block(z, near, far, gain, store)
-        if i == 1:
-            for copy in copies:
-                copy.wait()
-            projected[:128] = jnp.dot(normed[:128], w_rows[...], preferred_element_type=F32)
-        if i >= 1:
-            projected[rows] = jnp.dot(normed[rows], w_rows[...], preferred_element_type=F32)
+    for copy in copies:
+        copy.wait()
+    for i in range(2):
+        rows = slice(256 * i, 256 * i + 256)
+        projected[rows] = jnp.dot(normed[rows], w_rows[...], preferred_element_type=F32)
     attended = attend(projected[...])
     for i, shift in enumerate((0, 3, 1, 2)):
         frame = lax.rem(x + shift, 4)
@@ -107,16 +103,14 @@
     total = jnp.zeros((256, QUARTER), F32)
     for z_far, weights in enumerate(((wo00, wo01), (wo10, wo11))):
         source = lax.rem(z + z_far, 2)
-        for core in range(2):
+        for c_far, weight in enumerate(weights):
+            first = pl.multiple_of(lax.rem(c + c_far, 2) * HD, HD)
             pieces = []
             for half in (near, far):
-                columns = [
-                    half[s, :, source, :, HD * core : HD * core + HD].reshape(128, HD) for s in range(4)
-                ]
+                columns = [half[s, :, source, :, pl.ds(first, HD)].reshape(128, HD) for s in range(4)]
                 pieces.append(jnp.concatenate(columns, axis=1))
             attended = jnp.concatenate(pieces, axis=0)
-            weight = jnp.where(c == core, weights[0][...], weights[1][...])
-            total = total + jnp.dot(attended, weight, preferred_element_type=F32)
+            total = total + jnp.dot(attended, weight[...], preferred_element_type=F32)
     for half in range(2):
         side = lax.rem(c + half, 2)
         mixed = residual[:, side].astype(F32) + total[128 * half : 128 * half + 128].reshape(8, 16, QUARTER)
@@ -170,38 +164,33 @@
     xa, w_rows = lax.optimization_barrier((xa, w_rows))
     w_rows = lax.all_gather(w_rows, ("c", "y"), axis=1, tiled=True)
     xb = swap(xa, "z")
-    la, ra, oa = (lax.ppermute(xa, "x", ring(4, shift)) for shift in (1, 3, 2))
+    la, ra = (lax.ppermute(xa, "x", ring(4, shift)) for shift in (1, 3))
     xb_late = after(xb, la, ra)
-    lb, rb, ob = (lax.ppermute(xb_late, "x", ring(4, shift)) for shift in (1, 3, 2))
+    lb, rb = (lax.ppermute(xb_late, "x", ring(4, shift)) for shift in (1, 3))
+    oab = lax.ppermute(jnp.stack([xa, xb_late]), "x", ring(4, 2))
 
     def half(value, index, size):
         return lax.dynamic_slice_in_dim(value, index * size, size, axis=1)
 
-    columns = [2 * z + c, 2 * z + 1 - c]
-    far_columns = [2 * (1 - z) + c, 2 * (1 - z) + 1 - c]
-    w_late = after(w_out, xb)
-    wo00 = half(w_out, columns[0], QUARTER)
-    wo10 = swap(half(w_late, far_columns[0], QUARTER), "z")
-    wo_side = swap(half(w_late, far_columns[1], QUARTER), "z")
-    wo01 = swap(half(w_out, columns[1], QUARTER), "c")
-    wo11 = swap(wo_side, "c")
+    wo_keep = half(w_out, z, 2 * QUARTER)
+    wo_got = swap(half(after(w_out, xb), 1 - z, 2 * QUARTER), "z")
+    wo00, wo10 = half(wo_keep, c, QUARTER), half(wo_got, c, QUARTER)
+    wo01, wo11 = swap(half(wo_keep, 1 - c, QUARTER), "c"), swap(half(wo_got, 1 - c, QUARTER), "c")
 
     attended = kernel_call(
         attend_kernel,
         jax.ShapeDtypeStruct((4, 8, 2, 16, 2 * HD), BF16),
-        (place, xa, xb, la, lb, ra, rb, oa, after(ob, wo10), gain, w_rows),
+        (place, xa, xb, la, lb, ra, rb, oab, gain, w_rows),
         3 * 10**9,
         9 * 10**6,
-        57,
+        48,
         [
-            pltpu.VMEM((2, 8, 32, QUARTER), BF16),
             pltpu.VMEM((512, WIDTH), BF16),
             pltpu.VMEM((WIDTH, 6 * HD), BF16),
             pltpu.VMEM((512, 6 * HD), F32),
-            pltpu.SemaphoreType.DMA((2,)),
             pltpu.SemaphoreType.DMA((8,)),
         ],
-        left_out=(7, 8, 10),
+        left_out=(9,),
     )
 
     attended = lax.all_to_all(attended.reshape(64, 16, 2 * HD), ("x", "y", "z"), 0, 0, tiled=True)

time: 132 us -> 130 us (0.985)
  starting transfers between devices: 64.5 us -> 58.5 us
  local copies, waits for them, and re-layouts: 5.94 us -> 9.17 us
  waiting for transfers between devices: 33.8 us -> 35.8 us
  Pallas kernels: 12.5 us -> 11.1 us
    ppermute x6 -> x5, waiting for transfers between devices: 16 us -> 20.5 us  [the longest x2 15.6 us: body(): lb, rb = (lax.ppermute(xb_late, 'x', ring(4, shift)) for shift in (1, 3))]
    dynamic_slice x2 -> x3, local copies, waits for them, and re-layouts: 4.94 us -> 8.19 us  [half(): return lax.dynamic_slice_in_dim(value, index * size, size, axis=1)]
    all_to_all x1, waiting for transfers between devices: 9.21 us -> 6.07 us  [body(): lax.all_to_all(attended.reshape(64, 16, 2 * HD), ('x', 'y', 'z'), 0, 0, t...]
    ppermute x6 -> x5, starting transfers between devices: 20.3 us -> 17.4 us  [the longest x2 6.49 us: body(): lb, rb = (lax.ppermute(xb_late, 'x', ring(4, shift)) for shift in (1, 3))]
    ppermute x6 -> x5, starting transfers between devices: 16.4 us -> 14.6 us  [swap(): return lax.ppermute(value, axis, [(0, 1), (1, 0)])]
    ppermute x3, waiting for transfers between devices: 2.31 us -> 3.87 us  [body(): lax.ppermute(slots[k], 'x', ring(4, k))]
    pallas_call x3, Pallas kernels: 12.5 us -> 11.1 us  [kernel_call(): pl.pallas_call(kernel, out_shape=shapes, in_specs=[SMEM if value.dtype ==...]
    ppermute x6 -> x5, waiting for transfers between devices: 3.71 us -> 2.61 us  [swap(): return lax.ppermute(value, axis, [(0, 1), (1, 0)])]
  transfers between devices with their start and end apart: 18 -> 16, of which waited for: 10 -> 10; matrix products, arithmetic and copies ran while one was open for 4% -> 7% of each run, Pallas kernels for 7% -> 6%
where the time goes in v3:
time: 130 us; the launch traced here: 129 us
  starting transfers between devices  58.5 us (45%)
  waiting for transfers between devices  35.8 us (28%)
  between operations  13.6 us (10%)
  Pallas kernels  11.1 us (9%)
  local copies, waits for them, and re-layouts  9.17 us (7%)
    ppermute x2, waiting for transfers between devices, body(): lb, rb = (lax.ppermute(xb_late, 'x', ring(4, shift)) for shift in (1, 3))  15.6 us
    ppermute x5, starting transfers between devices, swap(): return lax.ppermute(value, axis, [(0, 1), (1, 0)])  14.6 us
    pallas_call x3, Pallas kernels, kernel_call(): pl.pallas_call(kernel, out_shape=shapes, in_specs=[SMEM if value.dtype ==...  11.1 us
    all_to_all x1, starting transfers between devices, body(): lax.all_to_all(tokens, ('y', 'c'), 0, 0, tiled=True).reshape(8, 32, QUARTER)  10.2 us
    all_to_all x1, starting transfers between devices, body(): lax.all_to_all(attended.reshape(64, 16, 2 * HD), ('x', 'y', 'z'), 0, 0, t...  8.43 us
    dynamic_slice x3, local copies, waits for them, and re-layouts, half(): return lax.dynamic_slice_in_dim(value, index * size, size, axis=1)  8.19 us
    ppermute x3, starting transfers between devices, body(): lax.ppermute(slots[k], 'x', ring(4, k))  7.75 us
    ppermute x2, starting transfers between devices, body(): lb, rb = (lax.ppermute(xb_late, 'x', ring(4, shift)) for shift in (1, 3))  6.49 us
  transfers between devices with their start and end apart: 16, of which 10 were waited for; matrix products, arithmetic and copies ran while one was open for 7% of the time, Pallas kernels for 6%

profile of v3, /device:TPU:1, one launch (start us, length us, event | category | flops | bytes accessed | tf_op | source)
XLA Modules:
  0.0 129.1 jit_solution(15544299986353991988)
XLA Ops:
  6.5 10.2 %all-to-all-start = ((bf16[16,16,768]{2,1,0:T(8,128)(2,1)}), bf16[16,16,768]{2,1,0:T(8,128)(2,1)S(1)}, u32[]{:S(2)}, u32[]{:S(2)}) async-start(bf16[16,16,768]{2,1,0:T(8,128)(2,1)} %bitcast.19), calls=%async_computation | async-start | bytes 786432 | tf_op jit(solution)/shard_map/all_to_all | solution.py:163
  16.9 1.0 copy-done.1
  17.9 0.6 shard_map.46
  18.5 2.8 %collective-permute-start.2 = (bf16[96,384]{1,0:T(8,128)(2,1)S(1)}, bf16[96,384]{1,0:T(8,128)(2,1)S(1)}, u32[]{:S(2)}, u32[]{:S(2)}) collective-permute-start(bf16[96,384]{1,0:T(8,128)(2,1)S(1)} %get-tuple-element.16), channel_id=1, source_target_pairs={{0,384},{128,0},{256,128},{384,256},{1,385},{129,1},{257,129},{385... | collective-permute-start | bytes 221192 | tf_op jit(solution)/shard_map/ppermute | solution.py:159
  21.3 2.4 %collective-permute-start.1 = (bf16[96,384]{1,0:T(8,128)(2,1)S(1)}, bf16[96,384]{1,0:T(8,128)(2,1)S(1)}, u32[]{:S(2)}, u32[]{:S(2)}) collective-permute-start(bf16[96,384]{1,0:T(8,128)(2,1)S(1)} %get-tuple-element.15), channel_id=1, source_target_pairs={{0,256},{128,384},{256,0},{384,128},{1,257},{129,385},{257,1},{385... | collective-permute-start | bytes 221192 | tf_op jit(solution)/shard_map/ppermute | solution.py:159
  23.7 2.5 %collective-permute-start = (bf16[96,384]{1,0:T(8,128)(2,1)S(1)}, bf16[96,384]{1,0:T(8,128)(2,1)S(1)}, u32[]{:S(2)}, u32[]{:S(2)}) collective-permute-start(bf16[96,384]{1,0:T(8,128)(2,1)S(1)} %get-tuple-element.14), channel_id=1, source_target_pairs={{0,128},{128,256},{256,384},{384,0},{1,129},{129,257},{257,385},{3... | collective-permute-start | bytes 221192 | tf_op jit(solution)/shard_map/ppermute | solution.py:159
  26.3 1.6 %collective-permute-done.1 = bf16[96,384]{1,0:T(8,128)(2,1)S(1)} collective-permute-done((bf16[96,384]{1,0:T(8,128)(2,1)S(1)}, bf16[96,384]{1,0:T(8,128)(2,1)S(1)}, u32[]{:S(2)}, u32[]{:S(2)}) %collective-permute-start.1) | collective-permute-done | bytes 73760 | tf_op jit(solution)/shard_map/ppermute | solution.py:159
  27.9 2.2 %collective-permute-done = bf16[96,384]{1,0:T(8,128)(2,1)S(1)} collective-permute-done((bf16[96,384]{1,0:T(8,128)(2,1)S(1)}, bf16[96,384]{1,0:T(8,128)(2,1)S(1)}, u32[]{:S(2)}, u32[]{:S(2)}) %collective-permute-start) | collective-permute-done | bytes 73760 | tf_op jit(solution)/shard_map/ppermute | solution.py:159
  30.1 0.8 pad_maximum_fusion.1
  31.3 3.5 %collective-permute-start.3 = (bf16[8,32,768]{2,1,0:T(8,128)(2,1)S(1)}, bf16[8,32,768]{2,1,0:T(8,128)(2,1)S(1)}, u32[]{:S(2)}, u32[]{:S(2)}) collective-permute-start(bf16[8,32,768]{2,1,0:T(8,128)(2,1)S(1)} %bitcast.21), channel_id=1, source_target_pairs={{0,8},{8,0},{1,9},{9,1},{2,10},{10,2},{3,11},{11,3},{4,12},{12,4},... | collective-permute-start | bytes 1179656 | tf_op jit(solution)/shard_map/ppermute | solution.py:23
  34.8 2.0 %collective-permute-start.4 = (bf16[8,32,768]{2,1,0:T(8,128)(2,1)S(1)}, bf16[8,32,768]{2,1,0:T(8,128)(2,1)S(1)}, u32[]{:S(2)}, u32[]{:S(2)}) collective-permute-start(bf16[8,32,768]{2,1,0:T(8,128)(2,1)S(1)} %bitcast.22), channel_id=1, source_target_pairs={{0,128},{128,256},{256,384},{384,0},{1,129},{129,257},{257,385},{3... | collective-permute-start | bytes 1179656 | tf_op jit(solution)/shard_map/ppermute | solution.py:167
  36.9 4.5 %collective-permute-start.5 = (bf16[8,32,768]{2,1,0:T(8,128)(2,1)S(1)}, bf16[8,32,768]{2,1,0:T(8,128)(2,1)S(1)}, u32[]{:S(2)}, u32[]{:S(2)}) collective-permute-start(bf16[8,32,768]{2,1,0:T(8,128)(2,1)S(1)} %bitcast.23), channel_id=1, source_target_pairs={{0,384},{128,0},{256,128},{384,256},{1,385},{129,1},{257,129},{385... | collective-permute-start | bytes 1179656 | tf_op jit(solution)/shard_map/ppermute | solution.py:167
  41.3 1.1 collective-permute-done.3.xb
  42.5 4.0 %collective-permute-done.4.la = bf16[8,32,768]{2,1,0:T(8,128)(2,1)S(1)} collective-permute-done((bf16[8,32,768]{2,1,0:T(8,128)(2,1)S(1)}, bf16[8,32,768]{2,1,0:T(8,128)(2,1)S(1)}, u32[]{:S(2)}, u32[]{:S(2)}) %collective-permute-start.4) | collective-permute-done | bytes 393248 | tf_op jit(solution)/shard_map/ppermute | solution.py:167
  46.5 0.9 collective-permute-done.5.ra
  47.5 4.4 %collective-permute-start.8 = (bf16[2,8,32,768]{3,2,1,0:T(8,128)(2,1)S(1)}, bf16[2,8,32,768]{3,2,1,0:T(8,128)(2,1)S(1)}, u32[]{:S(2)}, u32[]{:S(2)}) collective-permute-start(bf16[2,8,32,768]{3,2,1,0:T(8,128)(2,1)S(1)} %pad_maximum_fusion), channel_id=1, source_target_pairs={{0,256},{128,384},{256,0},{384,128},{1,257},{129,385},{257,1},{385... | collective-permute-start | bytes 2359304 | tf_op jit(solution)/shard_map/ppermute | solution.py:170
  51.9 2.7 %constant_dynamic-slice_fusion.3 = bf16[512,1536]{1,0:T(8,128)(2,1)} fusion(bf16[512,3072]{1,0:T(8,128)(2,1)} %param.7, s32[]{:T(128)S(6)} %select_n.24), kind=kLoop, calls=%fused_computation.5 | loop fusion | bytes 3145732 | tf_op jit(solution)/shard_map/dynamic_slice | solution.py:173
  54.6 2.1 %collective-permute-start.10 = (bf16[512,1536]{1,0:T(8,128)(2,1)}, bf16[512,1536]{1,0:T(8,128)(2,1)}, u32[]{:S(2)}, u32[]{:S(2)}) collective-permute-start(bf16[512,1536]{1,0:T(8,128)(2,1)} %constant_dynamic-slice_fusion.3), channel_id=1, source_target_pairs={{0,8},{8,0},{1,9},{9,1},{2,10},{10,2},{3,11},{11,3},{4,12},{12,4},... | collective-permute-start | bytes 4718600 | tf_op jit(solution)/shard_map/ppermute | solution.py:23
  56.7 3.4 %collective-permute-start.6 = (bf16[8,32,768]{2,1,0:T(8,128)(2,1)S(1)}, bf16[8,32,768]{2,1,0:T(8,128)(2,1)S(1)}, u32[]{:S(2)}, u32[]{:S(2)}) collective-permute-start(bf16[8,32,768]{2,1,0:T(8,128)(2,1)S(1)} %collective-permute-done.3.xb), channel_id=1, source_target_pairs={{0,128},{128,256},{256,384},{384,0},{1,129},{129,257},{257,385},{3... | collective-permute-start | bytes 1179656 | tf_op jit(solution)/shard_map/ppermute | solution.py:169
  60.1 3.1 %collective-permute-start.7 = (bf16[8,32,768]{2,1,0:T(8,128)(2,1)S(1)}, bf16[8,32,768]{2,1,0:T(8,128)(2,1)S(1)}, u32[]{:S(2)}, u32[]{:S(2)}) collective-permute-start(bf16[8,32,768]{2,1,0:T(8,128)(2,1)S(1)} %collective-permute-done.3.xb), channel_id=1, source_target_pairs={{0,384},{128,0},{256,128},{384,256},{1,385},{129,1},{257,129},{385... | collective-permute-start | bytes 1179656 | tf_op jit(solution)/shard_map/ppermute | solution.py:169
  63.2 15.6 %collective-permute-done.6.lb = bf16[8,32,768]{2,1,0:T(8,128)(2,1)S(1)} collective-permute-done((bf16[8,32,768]{2,1,0:T(8,128)(2,1)S(1)}, bf16[8,32,768]{2,1,0:T(8,128)(2,1)S(1)}, u32[]{:S(2)}, u32[]{:S(2)}) %collective-permute-start.6) | collective-permute-done | bytes 393248 | tf_op jit(solution)/shard_map/ppermute | solution.py:169
  78.8 2.3 %all-gather.2.cloned.1.call-done.w_hbm = bf16[4,1536,384]{2,1,0:T(8,128)(2,1)} async-done(((bf16[4,96,384]{2,1,0:T(8,128)(2,1)}), bf16[4,1536,384]{2,1,0:T(8,128)(2,1)}) %all-gather.2.cloned.1.call-update) | async-done | bytes 4718608 | tf_op jit(solution)/shard_map/all_gather | solution.py:165
  81.1 7.6 %shard_map.47 = bf16[4,8,2,16,256]{4,3,2,1,0:T(8,128)(2,1)} custom-call(s32[3]{0:T(128)S(1)} %pad_add_fusion.place, bf16[8,32,768]{2,1,0:T(8,128)(2,1)S(1)} %bitcast.25, bf16[8,32,768]{2,1,0:T(8,128)(2,1)S(1)} %collective-permute-done.3.xb, bf16[8,32,768]{2,1,0:T(8,128)(2,1)S(1)} %collective-permute-done.4.la, ...), custom_call_target="tpu_custom_call" | custom-call | flops 3000000000 | bytes 9000000 | tf_op jit(solution)/shard_map/pallas_call | solution.py:132
  88.7 8.4 %all-to-all-start.1 = ((bf16[64,16,256]{2,1,0:T(8,128)(2,1)}), bf16[64,16,256]{2,1,0:T(8,128)(2,1)S(1)}, u32[]{:S(2)}, u32[]{:S(2)}) async-start(bf16[64,16,256]{2,1,0:T(8,128)(2,1)} %bitcast.13), calls=%async_computation.1 | async-start | bytes 1048576 | tf_op jit(solution)/shard_map/all_to_all | solution.py:196
  97.1 3.1 %constant_dynamic-slice_fusion.1 = (bf16[512,768]{1,0:T(8,128)(2,1)}, bf16[512,768]{1,0:T(8,128)(2,1)S(1)}) fusion(bf16[512,3072]{1,0:T(8,128)(2,1)} %param.7, s32[]{:T(128)S(6)} %dynamic_slice.25, s32[]{:T(128)S(6)} %dynamic_slice.21), kind=kLoop, calls=%fused_computation.3 | loop fusion | bytes 3145736 | tf_op jit(solution)/shard_map/dynamic_slice | solution.py:173
  100.3 2.4 %collective-permute-start.11 = (bf16[512,768]{1,0:T(8,128)(2,1)}, bf16[512,768]{1,0:T(8,128)(2,1)S(1)}, u32[]{:S(2)}, u32[]{:S(2)}) collective-permute-start(bf16[512,768]{1,0:T(8,128)(2,1)} %get-tuple-element.21), channel_id=1, source_target_pairs={{0,4},{4,0},{1,5},{5,1},{2,6},{6,2},{3,7},{7,3},{8,12},{12,8},{9,1... | collective-permute-start | bytes 2359304 | tf_op jit(solution)/shard_map/ppermute | solution.py:23
  102.7 2.4 %constant_dynamic-slice_fusion = (bf16[512,768]{1,0:T(8,128)(2,1)}, bf16[512,768]{1,0:T(8,128)(2,1)S(1)}) fusion(bf16[512,1536]{1,0:T(8,128)(2,1)} %collective-permute-done.10, s32[]{:T(128)S(6)} %select_n.25, s32[]{:T(128)S(6)} %select_n.20), kind=kLoop, calls=%fused_computation.2 | loop fusion | bytes 3145736 | tf_op jit(solution)/shard_map/dynamic_slice | solution.py:173
  105.1 1.9 %collective-permute-start.12 = (bf16[512,768]{1,0:T(8,128)(2,1)}, bf16[512,768]{1,0:T(8,128)(2,1)}, u32[]{:S(2)}, u32[]{:S(2)}) collective-permute-start(bf16[512,768]{1,0:T(8,128)(2,1)} %get-tuple-element.23), channel_id=1, source_target_pairs={{0,4},{4,0},{1,5},{5,1},{2,6},{6,2},{3,7},{7,3},{8,12},{12,8},{9,1... | collective-permute-start | bytes 2359304 | tf_op jit(solution)/shard_map/ppermute | solution.py:23
  107.0 6.1 %all-to-all-done.1 = bf16[64,16,256]{2,1,0:T(8,128)(2,1)S(1)} async-done(((bf16[64,16,256]{2,1,0:T(8,128)(2,1)}), bf16[64,16,256]{2,1,0:T(8,128)(2,1)S(1)}, u32[]{:S(2)}, u32[]{:S(2)}) %all-to-all-start.1) | async-done | bytes 524320 | tf_op jit(solution)/shard_map/all_to_all | solution.py:196
  113.1 4.7 %collective-permute-start.9 = (bf16[64,16,256]{2,1,0:T(8,128)(2,1)S(1)}, bf16[64,16,256]{2,1,0:T(8,128)(2,1)S(1)}, u32[]{:S(2)}, u32[]{:S(2)}) collective-permute-start(bf16[64,16,256]{2,1,0:T(8,128)(2,1)S(1)} %all-to-all-done.1), channel_id=1, source_target_pairs={{0,4},{4,0},{1,5},{5,1},{2,6},{6,2},{3,7},{7,3},{8,12},{12,8},{9,1... | collective-permute-start | bytes 1572872 | tf_op jit(solution)/shard_map/ppermute | solution.py:23
  117.8 1.5 %collective-permute-done.9 = bf16[64,16,256]{2,1,0:T(8,128)(2,1)S(1)} collective-permute-done((bf16[64,16,256]{2,1,0:T(8,128)(2,1)S(1)}, bf16[64,16,256]{2,1,0:T(8,128)(2,1)S(1)}, u32[]{:S(2)}, u32[]{:S(2)}) %collective-permute-start.9) | collective-permute-done | bytes 524320 | tf_op jit(solution)/shard_map/ppermute | solution.py:23
  119.3 2.9 %shard_map.48 = bf16[8,2,16,768]{3,2,1,0:T(8,128)(2,1)} custom-call(s32[3]{0:T(128)S(1)} %pad_add_fusion.place, bf16[4,8,2,16,256]{4,3,2,1,0:T(8,128)(2,1)S(1)} %bitcast.18, bf16[4,8,2,16,256]{4,3,2,1,0:T(8,128)(2,1)S(1)} %bitcast.26, bf16[512,768]{1,0:T(8,128)(2,1)S(1)} %get-tuple-element.22.wo00, bf16[512,768]{1,0:T(8,128)(2,1)S(1)} %get-tuple-element.24.wo10, ...), custom_call_target="tpu_custom_call" | custom-call | flops 800000000 | bytes 6000000 | tf_op jit(solution)/shard_map/pallas_call | solution.py:132
  (16 shorter events, 0.7 us)
Async XLA Ops:
  6.5 24.8 %all-to-all-start = ((bf16[16,16,768]{2,1,0:T(8,128)(2,1)}), bf16[16,16,768]{2,1,0:T(8,128)(2,1)S(1)}, u32[]{:S(2)}, u32[]{:S(2)}) async-start(bf16[16,16,768]{2,1,0:T(8,128)(2,1)} %bitcast.19), calls=%async_computation | async-start | bytes 786432 | tf_op jit(solution)/shard_map/all_to_all | solution.py:163
  16.8 64.3 %copy-start.2 = (f32[3072]{0:T(1024)S(1)}, f32[3072]{0:T(1024)}, u32[]{:S(2)}) copy-start(f32[3072]{0:T(1024)} %param.5) | copy-start | bytes 36868
  16.8 64.3 %all-gather.2.cloned.1.call-start = ((), (), s32[]{:S(2)}) async-start(), calls=%async_computation.2 | async-start | bytes 5013504 | tf_op jit(solution)/shard_map/all_gather | solution.py:165
  16.9 1.0 copy-start.1
  18.5 7.8 %collective-permute-start.2 = (bf16[96,384]{1,0:T(8,128)(2,1)S(1)}, bf16[96,384]{1,0:T(8,128)(2,1)S(1)}, u32[]{:S(2)}, u32[]{:S(2)}) collective-permute-start(bf16[96,384]{1,0:T(8,128)(2,1)S(1)} %get-tuple-element.16), channel_id=1, source_target_pairs={{0,384},{128,0},{256,128},{384,256},{1,385},{129,1},{257,129},{385... | collective-permute-start | bytes 221192 | tf_op jit(solution)/shard_map/ppermute | solution.py:159
  21.3 6.6 %collective-permute-start.1 = (bf16[96,384]{1,0:T(8,128)(2,1)S(1)}, bf16[96,384]{1,0:T(8,128)(2,1)S(1)}, u32[]{:S(2)}, u32[]{:S(2)}) collective-permute-start(bf16[96,384]{1,0:T(8,128)(2,1)S(1)} %get-tuple-element.15), channel_id=1, source_target_pairs={{0,256},{128,384},{256,0},{384,128},{1,257},{129,385},{257,1},{385... | collective-permute-start | bytes 221192 | tf_op jit(solution)/shard_map/ppermute | solution.py:159
  23.7 6.4 %collective-permute-start = (bf16[96,384]{1,0:T(8,128)(2,1)S(1)}, bf16[96,384]{1,0:T(8,128)(2,1)S(1)}, u32[]{:S(2)}, u32[]{:S(2)}) collective-permute-start(bf16[96,384]{1,0:T(8,128)(2,1)S(1)} %get-tuple-element.14), channel_id=1, source_target_pairs={{0,128},{128,256},{256,384},{384,0},{1,129},{129,257},{257,385},{3... | collective-permute-start | bytes 221192 | tf_op jit(solution)/shard_map/ppermute | solution.py:159
  31.3 11.1 %collective-permute-start.3 = (bf16[8,32,768]{2,1,0:T(8,128)(2,1)S(1)}, bf16[8,32,768]{2,1,0:T(8,128)(2,1)S(1)}, u32[]{:S(2)}, u32[]{:S(2)}) collective-permute-start(bf16[8,32,768]{2,1,0:T(8,128)(2,1)S(1)} %bitcast.21), channel_id=1, source_target_pairs={{0,8},{8,0},{1,9},{9,1},{2,10},{10,2},{3,11},{11,3},{4,12},{12,4},... | collective-permute-start | bytes 1179656 | tf_op jit(solution)/shard_map/ppermute | solution.py:23
  34.8 11.6 %collective-permute-start.4 = (bf16[8,32,768]{2,1,0:T(8,128)(2,1)S(1)}, bf16[8,32,768]{2,1,0:T(8,128)(2,1)S(1)}, u32[]{:S(2)}, u32[]{:S(2)}) collective-permute-start(bf16[8,32,768]{2,1,0:T(8,128)(2,1)S(1)} %bitcast.22), channel_id=1, source_target_pairs={{0,128},{128,256},{256,384},{384,0},{1,129},{129,257},{257,385},{3... | collective-permute-start | bytes 1179656 | tf_op jit(solution)/shard_map/ppermute | solution.py:167
  36.9 10.5 %collective-permute-start.5 = (bf16[8,32,768]{2,1,0:T(8,128)(2,1)S(1)}, bf16[8,32,768]{2,1,0:T(8,128)(2,1)S(1)}, u32[]{:S(2)}, u32[]{:S(2)}) collective-permute-start(bf16[8,32,768]{2,1,0:T(8,128)(2,1)S(1)} %bitcast.23), channel_id=1, source_target_pairs={{0,384},{128,0},{256,128},{384,256},{1,385},{129,1},{257,129},{385... | collective-permute-start | bytes 1179656 | tf_op jit(solution)/shard_map/ppermute | solution.py:167
  47.5 31.3 %collective-permute-start.8 = (bf16[2,8,32,768]{3,2,1,0:T(8,128)(2,1)S(1)}, bf16[2,8,32,768]{3,2,1,0:T(8,128)(2,1)S(1)}, u32[]{:S(2)}, u32[]{:S(2)}) collective-permute-start(bf16[2,8,32,768]{3,2,1,0:T(8,128)(2,1)S(1)} %pad_maximum_fusion), channel_id=1, source_target_pairs={{0,256},{128,384},{256,0},{384,128},{1,257},{129,385},{257,1},{385... | collective-permute-start | bytes 2359304 | tf_op jit(solution)/shard_map/ppermute | solution.py:170
  54.6 48.1 %collective-permute-start.10 = (bf16[512,1536]{1,0:T(8,128)(2,1)}, bf16[512,1536]{1,0:T(8,128)(2,1)}, u32[]{:S(2)}, u32[]{:S(2)}) collective-permute-start(bf16[512,1536]{1,0:T(8,128)(2,1)} %constant_dynamic-slice_fusion.3), channel_id=1, source_target_pairs={{0,8},{8,0},{1,9},{9,1},{2,10},{10,2},{3,11},{11,3},{4,12},{12,4},... | collective-permute-start | bytes 4718600 | tf_op jit(solution)/shard_map/ppermute | solution.py:23
  56.7 22.1 %collective-permute-start.6 = (bf16[8,32,768]{2,1,0:T(8,128)(2,1)S(1)}, bf16[8,32,768]{2,1,0:T(8,128)(2,1)S(1)}, u32[]{:S(2)}, u32[]{:S(2)}) collective-permute-start(bf16[8,32,768]{2,1,0:T(8,128)(2,1)S(1)} %collective-permute-done.3.xb), channel_id=1, source_target_pairs={{0,128},{128,256},{256,384},{384,0},{1,129},{129,257},{257,385},{3... | collective-permute-start | bytes 1179656 | tf_op jit(solution)/shard_map/ppermute | solution.py:169
  60.1 18.6 %collective-permute-start.7 = (bf16[8,32,768]{2,1,0:T(8,128)(2,1)S(1)}, bf16[8,32,768]{2,1,0:T(8,128)(2,1)S(1)}, u32[]{:S(2)}, u32[]{:S(2)}) collective-permute-start(bf16[8,32,768]{2,1,0:T(8,128)(2,1)S(1)} %collective-permute-done.3.xb), channel_id=1, source_target_pairs={{0,384},{128,0},{256,128},{384,256},{1,385},{129,1},{257,129},{385... | collective-permute-start | bytes 1179656 | tf_op jit(solution)/shard_map/ppermute | solution.py:169
  88.7 24.4 %all-to-all-start.1 = ((bf16[64,16,256]{2,1,0:T(8,128)(2,1)}), bf16[64,16,256]{2,1,0:T(8,128)(2,1)S(1)}, u32[]{:S(2)}, u32[]{:S(2)}) async-start(bf16[64,16,256]{2,1,0:T(8,128)(2,1)} %bitcast.13), calls=%async_computation.1 | async-start | bytes 1048576 | tf_op jit(solution)/shard_map/all_to_all | solution.py:196
  97.1 22.2 %copy-start = (bf16[1,1,256,768]{3,2,1,0:T(8,128)(2,1)S(1)}, bf16[1,1,256,768]{3,2,1,0:T(8,128)(2,1)}, u32[]{:S(2)}) copy-start(bf16[1,1,256,768]{3,2,1,0:T(8,128)(2,1)} %param.4) | copy-start | bytes 1179652
  100.3 17.5 %collective-permute-start.11 = (bf16[512,768]{1,0:T(8,128)(2,1)}, bf16[512,768]{1,0:T(8,128)(2,1)S(1)}, u32[]{:S(2)}, u32[]{:S(2)}) collective-permute-start(bf16[512,768]{1,0:T(8,128)(2,1)} %get-tuple-element.21), channel_id=1, source_target_pairs={{0,4},{4,0},{1,5},{5,1},{2,6},{6,2},{3,7},{7,3},{8,12},{12,8},{9,1... | collective-permute-start | bytes 2359304 | tf_op jit(solution)/shard_map/ppermute | solution.py:23
  105.1 12.7 %collective-permute-start.12 = (bf16[512,768]{1,0:T(8,128)(2,1)}, bf16[512,768]{1,0:T(8,128)(2,1)}, u32[]{:S(2)}, u32[]{:S(2)}) collective-permute-start(bf16[512,768]{1,0:T(8,128)(2,1)} %get-tuple-element.23), channel_id=1, source_target_pairs={{0,4},{4,0},{1,5},{5,1},{2,6},{6,2},{3,7},{7,3},{8,12},{12,8},{9,1... | collective-permute-start | bytes 2359304 | tf_op jit(solution)/shard_map/ppermute | solution.py:23
  113.1 6.2 %collective-permute-start.9 = (bf16[64,16,256]{2,1,0:T(8,128)(2,1)S(1)}, bf16[64,16,256]{2,1,0:T(8,128)(2,1)S(1)}, u32[]{:S(2)}, u32[]{:S(2)}) collective-permute-start(bf16[64,16,256]{2,1,0:T(8,128)(2,1)S(1)} %all-to-all-done.1), channel_id=1, source_target_pairs={{0,4},{4,0},{1,5},{5,1},{2,6},{6,2},{3,7},{7,3},{8,12},{12,8},{9,1... | collective-permute-start | bytes 1572872 | tf_op jit(solution)/shard_map/ppermute | solution.py:23
Sparse Core Ops, SparseCore 0:
  31.5 49.5 all-gather.1

commit v4 on v3

--- a/solution.py
+++ b/solution.py
@@ -17,6 +17,14 @@
 
 def ring(size, shift):
     return [(i, (i + shift) % size) for i in range(size)]
+
+
+def across():
+    pairs = []
+    for i in range(4):
+        pairs.append((2 * i, 2 * ((i + 1) % 4)))
+        pairs.append((2 * i + 1, 2 * ((i + 3) % 4) + 1))
+    return pairs
 
 
 def swap(value, axis):
@@ -66,7 +74,7 @@
     return jnp.concatenate(heads, axis=2).astype(BF16)
 
 
-def attend_kernel(place, xa, xb, la, lb, ra, rb, opposite, gain, w_hbm, out, *scratch):
+def attend_kernel(place, xa, xb, la, lb, ra, rb, oa, ob, gain, w_hbm, out, *scratch):
     normed, w_rows, projected, w_sent = scratch
     x, z = place[0], place[1]
     copies = []
@@ -77,7 +85,7 @@
             copies.append(pltpu.make_async_copy(source, target, w_sent.at[2 * k + core]))
     for copy in copies:
         copy.start()
-    blocks = ((xa, xb), (la, lb), (ra, rb), (opposite.at[0], opposite.at[1]))
+    blocks = ((xa, xb), (la, lb), (ra, rb), (oa, ob))
     for i, (near, far) in enumerate(blocks):
         rows = slice(128 * i, 128 * i + 128)
 
@@ -167,7 +175,8 @@
     la, ra = (lax.ppermute(xa, "x", ring(4, shift)) for shift in (1, 3))
     xb_late = after(xb, la, ra)
     lb, rb = (lax.ppermute(xb_late, "x", ring(4, shift)) for shift in (1, 3))
-    oab = lax.ppermute(jnp.stack([xa, xb_late]), "x", ring(4, 2))
+    oa = lax.ppermute(jnp.where(c == 0, la, ra), ("x", "c"), across())
+    ob = lax.ppermute(jnp.where(c == 0, lb, rb), ("x", "c"), across())
 
     def half(value, index, size):
         return lax.dynamic_slice_in_dim(value, index * size, size, axis=1)
@@ -180,7 +189,7 @@
     attended = kernel_call(
         attend_kernel,
         jax.ShapeDtypeStruct((4, 8, 2, 16, 2 * HD), BF16),
-        (place, xa, xb, la, lb, ra, rb, oab, gain, w_rows),
+        (place, xa, xb, la, lb, ra, rb, oa, ob, gain, w_rows),
         3 * 10**9,
         9 * 10**6,
         48,
@@ -190,7 +199,7 @@
             pltpu.VMEM((512, 6 * HD), F32),
             pltpu.SemaphoreType.DMA((8,)),
         ],
-        left_out=(9,),
+        left_out=(10,),
     )
 
     attended = lax.all_to_all(attended.reshape(64, 16, 2 * HD), ("x", "y", "z"), 0, 0, tiled=True)

time: 130 us -> 130 us (level)
  waiting for transfers between devices: 35.8 us -> 34 us
  starting transfers between devices: 58.5 us -> 60.2 us
    ppermute x2, waiting for transfers between devices: 15.6 us -> 0.01 us  [body(): lb, rb = (lax.ppermute(xb_late, 'x', ring(4, shift)) for shift in (1, 3))]
    ppermute x1 -> x2, waiting for transfers between devices: 0.01 us -> 7.56 us  [the longest x1 4.21 us: body(): ob = lax.ppermute(jnp.where(c == 0, lb, rb), ('x', 'c'), across())]
    all_gather x1, waiting for transfers between devices: 2.3 us -> 8.46 us  [body(): w_rows = lax.all_gather(w_rows, ('c', 'y'), axis=1, tiled=True)]
    ppermute x1 -> x2, starting transfers between devices: 4.41 us -> 5.48 us  [the longest x1 3.36 us: body(): oa = lax.ppermute(jnp.where(c == 0, la, ra), ('x', 'c'), across())]
  transfers between devices with their start and end apart: 16 -> 17, of which waited for: 10 -> 11; matrix products, arithmetic and copies ran while one was open for 7% -> 7% of each run, Pallas kernels for 6% -> 6%
where the time goes in v4:
time: 130 us; the launch traced here: 129 us
  starting transfers between devices  60.2 us (46%)
  waiting for transfers between devices  34 us (26%)
  between operations  13.6 us (10%)
  Pallas kernels  11.1 us (9%)
  local copies, waits for them, and re-layouts  9.21 us (7%)
    ppermute x5, starting transfers between devices, swap(): return lax.ppermute(value, axis, [(0, 1), (1, 0)])  14.7 us
    pallas_call x3, Pallas kernels, kernel_call(): pl.pallas_call(kernel, out_shape=shapes, in_specs=[SMEM if value.dtype ==...  11.1 us
    all_to_all x1, starting transfers between devices, body(): lax.all_to_all(tokens, ('y', 'c'), 0, 0, tiled=True).reshape(8, 32, QUARTER)  10.2 us
    all_gather x1, waiting for transfers between devices, body(): w_rows = lax.all_gather(w_rows, ('c', 'y'), axis=1, tiled=True)  8.46 us
    all_to_all x1, starting transfers between devices, body(): lax.all_to_all(attended.reshape(64, 16, 2 * HD), ('x', 'y', 'z'), 0, 0, t...  8.36 us
    dynamic_slice x3, local copies, waits for them, and re-layouts, half(): return lax.dynamic_slice_in_dim(value, index * size, size, axis=1)  8.23 us
    ppermute x3, starting transfers between devices, body(): lax.ppermute(slots[k], 'x', ring(4, k))  7.75 us
    ppermute x2, starting transfers between devices, body(): lb, rb = (lax.ppermute(xb_late, 'x', ring(4, shift)) for shift in (1, 3))  7.18 us
  transfers between devices with their start and end apart: 17, of which 11 were waited for; matrix products, arithmetic and copies ran while one was open for 7% of the time, Pallas kernels for 6%

profile of v4, /device:TPU:1, one launch (start us, length us, event | category | flops | bytes accessed | tf_op | source)
XLA Modules:
  0.0 129.1 jit_solution(10200038258002546869)
XLA Ops:
  6.5 10.2 %all-to-all-start = ((bf16[16,16,768]{2,1,0:T(8,128)(2,1)}), bf16[16,16,768]{2,1,0:T(8,128)(2,1)S(1)}, u32[]{:S(2)}, u32[]{:S(2)}) async-start(bf16[16,16,768]{2,1,0:T(8,128)(2,1)} %bitcast.17), calls=%async_computation | async-start | bytes 786432 | tf_op jit(solution)/shard_map/all_to_all | solution.py:171
  16.9 1.0 copy-done.1
  18.5 2.8 %collective-permute-start.2 = (bf16[96,384]{1,0:T(8,128)(2,1)S(1)}, bf16[96,384]{1,0:T(8,128)(2,1)S(1)}, u32[]{:S(2)}, u32[]{:S(2)}) collective-permute-start(bf16[96,384]{1,0:T(8,128)(2,1)S(1)} %get-tuple-element.16), channel_id=1, source_target_pairs={{0,384},{128,0},{256,128},{384,256},{1,385},{129,1},{257,129},{385... | collective-permute-start | bytes 221192 | tf_op jit(solution)/shard_map/ppermute | solution.py:167
  21.3 2.4 %collective-permute-start.1 = (bf16[96,384]{1,0:T(8,128)(2,1)S(1)}, bf16[96,384]{1,0:T(8,128)(2,1)S(1)}, u32[]{:S(2)}, u32[]{:S(2)}) collective-permute-start(bf16[96,384]{1,0:T(8,128)(2,1)S(1)} %get-tuple-element.15), channel_id=1, source_target_pairs={{0,256},{128,384},{256,0},{384,128},{1,257},{129,385},{257,1},{385... | collective-permute-start | bytes 221192 | tf_op jit(solution)/shard_map/ppermute | solution.py:167
  23.7 2.5 %collective-permute-start = (bf16[96,384]{1,0:T(8,128)(2,1)S(1)}, bf16[96,384]{1,0:T(8,128)(2,1)S(1)}, u32[]{:S(2)}, u32[]{:S(2)}) collective-permute-start(bf16[96,384]{1,0:T(8,128)(2,1)S(1)} %get-tuple-element.14), channel_id=1, source_target_pairs={{0,128},{128,256},{256,384},{384,0},{1,129},{129,257},{257,385},{3... | collective-permute-start | bytes 221192 | tf_op jit(solution)/shard_map/ppermute | solution.py:167
  26.2 1.6 %collective-permute-done.1 = bf16[96,384]{1,0:T(8,128)(2,1)S(1)} collective-permute-done((bf16[96,384]{1,0:T(8,128)(2,1)S(1)}, bf16[96,384]{1,0:T(8,128)(2,1)S(1)}, u32[]{:S(2)}, u32[]{:S(2)}) %collective-permute-start.1) | collective-permute-done | bytes 73760 | tf_op jit(solution)/shard_map/ppermute | solution.py:167
  27.9 2.2 %collective-permute-done = bf16[96,384]{1,0:T(8,128)(2,1)S(1)} collective-permute-done((bf16[96,384]{1,0:T(8,128)(2,1)S(1)}, bf16[96,384]{1,0:T(8,128)(2,1)S(1)}, u32[]{:S(2)}, u32[]{:S(2)}) %collective-permute-start) | collective-permute-done | bytes 73760 | tf_op jit(solution)/shard_map/ppermute | solution.py:167
  31.3 3.5 %collective-permute-start.3 = (bf16[8,32,768]{2,1,0:T(8,128)(2,1)S(1)}, bf16[8,32,768]{2,1,0:T(8,128)(2,1)S(1)}, u32[]{:S(2)}, u32[]{:S(2)}) collective-permute-start(bf16[8,32,768]{2,1,0:T(8,128)(2,1)S(1)} %bitcast.20), channel_id=1, source_target_pairs={{0,8},{8,0},{1,9},{9,1},{2,10},{10,2},{3,11},{11,3},{4,12},{12,4},... | collective-permute-start | bytes 1179656 | tf_op jit(solution)/shard_map/ppermute | solution.py:31
  34.8 2.0 %collective-permute-start.4 = (bf16[8,32,768]{2,1,0:T(8,128)(2,1)S(1)}, bf16[8,32,768]{2,1,0:T(8,128)(2,1)S(1)}, u32[]{:S(2)}, u32[]{:S(2)}) collective-permute-start(bf16[8,32,768]{2,1,0:T(8,128)(2,1)S(1)} %bitcast.21), channel_id=1, source_target_pairs={{0,128},{128,256},{256,384},{384,0},{1,129},{129,257},{257,385},{3... | collective-permute-start | bytes 1179656 | tf_op jit(solution)/shard_map/ppermute | solution.py:175
  36.9 4.5 %collective-permute-start.5 = (bf16[8,32,768]{2,1,0:T(8,128)(2,1)S(1)}, bf16[8,32,768]{2,1,0:T(8,128)(2,1)S(1)}, u32[]{:S(2)}, u32[]{:S(2)}) collective-permute-start(bf16[8,32,768]{2,1,0:T(8,128)(2,1)S(1)} %bitcast.22), channel_id=1, source_target_pairs={{0,384},{128,0},{256,128},{384,256},{1,385},{129,1},{257,129},{385... | collective-permute-start | bytes 1179656 | tf_op jit(solution)/shard_map/ppermute | solution.py:175
  41.3 1.1 collective-permute-done.3.xb
  42.4 4.0 %collective-permute-done.4.la = bf16[8,32,768]{2,1,0:T(8,128)(2,1)S(1)} collective-permute-done((bf16[8,32,768]{2,1,0:T(8,128)(2,1)S(1)}, bf16[8,32,768]{2,1,0:T(8,128)(2,1)S(1)}, u32[]{:S(2)}, u32[]{:S(2)}) %collective-permute-start.4) | collective-permute-done | bytes 393248 | tf_op jit(solution)/shard_map/ppermute | solution.py:175
  46.5 0.9 collective-permute-done.5.ra
  47.4 3.1 %collective-permute-start.6 = (bf16[8,32,768]{2,1,0:T(8,128)(2,1)S(1)}, bf16[8,32,768]{2,1,0:T(8,128)(2,1)S(1)}, u32[]{:S(2)}, u32[]{:S(2)}) collective-permute-start(bf16[8,32,768]{2,1,0:T(8,128)(2,1)S(1)} %collective-permute-done.3.xb), channel_id=1, source_target_pairs={{0,128},{128,256},{256,384},{384,0},{1,129},{129,257},{257,385},{3... | collective-permute-start | bytes 1179656 | tf_op jit(solution)/shard_map/ppermute | solution.py:177
  50.6 4.0 %collective-permute-start.7 = (bf16[8,32,768]{2,1,0:T(8,128)(2,1)S(1)}, bf16[8,32,768]{2,1,0:T(8,128)(2,1)S(1)}, u32[]{:S(2)}, u32[]{:S(2)}) collective-permute-start(bf16[8,32,768]{2,1,0:T(8,128)(2,1)S(1)} %collective-permute-done.3.xb), channel_id=1, source_target_pairs={{0,384},{128,0},{256,128},{384,256},{1,385},{129,1},{257,129},{385... | collective-permute-start | bytes 1179656 | tf_op jit(solution)/shard_map/ppermute | solution.py:177
  54.6 2.7 %constant_dynamic-slice_fusion.3 = bf16[512,1536]{1,0:T(8,128)(2,1)} fusion(bf16[512,3072]{1,0:T(8,128)(2,1)} %param.7, s32[]{:T(128)S(6)} %select_n.39), kind=kLoop, calls=%fused_computation.6 | loop fusion | bytes 3145732 | tf_op jit(solution)/shard_map/dynamic_slice | solution.py:182
  57.3 2.2 %collective-permute-start.11 = (bf16[512,1536]{1,0:T(8,128)(2,1)}, bf16[512,1536]{1,0:T(8,128)(2,1)}, u32[]{:S(2)}, u32[]{:S(2)}) collective-permute-start(bf16[512,1536]{1,0:T(8,128)(2,1)} %constant_dynamic-slice_fusion.3), channel_id=1, source_target_pairs={{0,8},{8,0},{1,9},{9,1},{2,10},{10,2},{3,11},{11,3},{4,12},{12,4},... | collective-permute-start | bytes 4718600 | tf_op jit(solution)/shard_map/ppermute | solution.py:31
  59.5 3.4 %collective-permute-start.8 = (bf16[8,32,768]{2,1,0:T(8,128)(2,1)S(1)}, bf16[8,32,768]{2,1,0:T(8,128)(2,1)S(1)}, u32[]{:S(2)}, u32[]{:S(2)}) collective-permute-start(bf16[8,32,768]{2,1,0:T(8,128)(2,1)S(1)} %broadcast_select_fusion.1), channel_id=1, source_target_pairs={{0,128},{4,388},{128,256},{132,4},{256,384},{260,132},{384,0},{388... | collective-permute-start | bytes 1179656 | tf_op jit(solution)/shard_map/ppermute | solution.py:178
  63.0 2.1 %collective-permute-start.9 = (bf16[8,32,768]{2,1,0:T(8,128)(2,1)S(1)}, bf16[8,32,768]{2,1,0:T(8,128)(2,1)S(1)}, u32[]{:S(2)}, u32[]{:S(2)}) collective-permute-start(bf16[8,32,768]{2,1,0:T(8,128)(2,1)S(1)} %broadcast_select_fusion), channel_id=1, source_target_pairs={{0,128},{4,388},{128,256},{132,4},{256,384},{260,132},{384,0},{388... | collective-permute-start | bytes 1179656 | tf_op jit(solution)/shard_map/ppermute | solution.py:179
  65.1 3.4 %collective-permute-done.8.oa = bf16[8,32,768]{2,1,0:T(8,128)(2,1)S(1)} collective-permute-done((bf16[8,32,768]{2,1,0:T(8,128)(2,1)S(1)}, bf16[8,32,768]{2,1,0:T(8,128)(2,1)S(1)}, u32[]{:S(2)}, u32[]{:S(2)}) %collective-permute-start.8) | collective-permute-done | bytes 393248 | tf_op jit(solution)/shard_map/ppermute | solution.py:178
  68.4 4.2 %collective-permute-done.9.ob = bf16[8,32,768]{2,1,0:T(8,128)(2,1)S(1)} collective-permute-done((bf16[8,32,768]{2,1,0:T(8,128)(2,1)S(1)}, bf16[8,32,768]{2,1,0:T(8,128)(2,1)S(1)}, u32[]{:S(2)}, u32[]{:S(2)}) %collective-permute-start.9) | collective-permute-done | bytes 393248 | tf_op jit(solution)/shard_map/ppermute | solution.py:179
  72.7 8.5 %all-gather.2.cloned.1.call-done.w_hbm = bf16[4,1536,384]{2,1,0:T(8,128)(2,1)} async-done(((bf16[4,96,384]{2,1,0:T(8,128)(2,1)}), bf16[4,1536,384]{2,1,0:T(8,128)(2,1)}) %all-gather.2.cloned.1.call-update) | async-done | bytes 4718608 | tf_op jit(solution)/shard_map/all_gather | solution.py:173
  81.1 7.6 %shard_map.47 = bf16[4,8,2,16,256]{4,3,2,1,0:T(8,128)(2,1)} custom-call(s32[3]{0:T(128)S(1)} %pad_add_fusion.place, bf16[8,32,768]{2,1,0:T(8,128)(2,1)S(1)} %bitcast.23, bf16[8,32,768]{2,1,0:T(8,128)(2,1)S(1)} %collective-permute-done.3.xb, bf16[8,32,768]{2,1,0:T(8,128)(2,1)S(1)} %collective-permute-done.4.la, ...), custom_call_target="tpu_custom_call" | custom-call | flops 3000000000 | bytes 9000000 | tf_op jit(solution)/shard_map/pallas_call | solution.py:140
  88.7 8.4 %all-to-all-start.1 = ((bf16[64,16,256]{2,1,0:T(8,128)(2,1)}), bf16[64,16,256]{2,1,0:T(8,128)(2,1)S(1)}, u32[]{:S(2)}, u32[]{:S(2)}) async-start(bf16[64,16,256]{2,1,0:T(8,128)(2,1)} %bitcast.11), calls=%async_computation.1 | async-start | bytes 1048576 | tf_op jit(solution)/shard_map/all_to_all | solution.py:205
  97.1 3.1 %constant_dynamic-slice_fusion.1 = (bf16[512,768]{1,0:T(8,128)(2,1)}, bf16[512,768]{1,0:T(8,128)(2,1)S(1)}) fusion(bf16[512,3072]{1,0:T(8,128)(2,1)} %param.7, s32[]{:T(128)S(6)} %dynamic_slice.25, s32[]{:T(128)S(6)} %dynamic_slice.21), kind=kLoop, calls=%fused_computation.4 | loop fusion | bytes 3145736 | tf_op jit(solution)/shard_map/dynamic_slice | solution.py:182
  100.3 2.4 %collective-permute-start.12 = (bf16[512,768]{1,0:T(8,128)(2,1)}, bf16[512,768]{1,0:T(8,128)(2,1)S(1)}, u32[]{:S(2)}, u32[]{:S(2)}) collective-permute-start(bf16[512,768]{1,0:T(8,128)(2,1)} %get-tuple-element.21), channel_id=1, source_target_pairs={{0,4},{4,0},{1,5},{5,1},{2,6},{6,2},{3,7},{7,3},{8,12},{12,8},{9,1... | collective-permute-start | bytes 2359304 | tf_op jit(solution)/shard_map/ppermute | solution.py:31
  102.7 2.4 %constant_dynamic-slice_fusion = (bf16[512,768]{1,0:T(8,128)(2,1)}, bf16[512,768]{1,0:T(8,128)(2,1)S(1)}) fusion(bf16[512,1536]{1,0:T(8,128)(2,1)} %collective-permute-done.11, s32[]{:T(128)S(6)} %select_n.40, s32[]{:T(128)S(6)} %select_n.35), kind=kLoop, calls=%fused_computation.3 | loop fusion | bytes 3145736 | tf_op jit(solution)/shard_map/dynamic_slice | solution.py:182
  105.2 1.9 %collective-permute-start.13 = (bf16[512,768]{1,0:T(8,128)(2,1)}, bf16[512,768]{1,0:T(8,128)(2,1)}, u32[]{:S(2)}, u32[]{:S(2)}) collective-permute-start(bf16[512,768]{1,0:T(8,128)(2,1)} %get-tuple-element.23), channel_id=1, source_target_pairs={{0,4},{4,0},{1,5},{5,1},{2,6},{6,2},{3,7},{7,3},{8,12},{12,8},{9,1... | collective-permute-start | bytes 2359304 | tf_op jit(solution)/shard_map/ppermute | solution.py:31
  107.1 6.0 %all-to-all-done.1 = bf16[64,16,256]{2,1,0:T(8,128)(2,1)S(1)} async-done(((bf16[64,16,256]{2,1,0:T(8,128)(2,1)}), bf16[64,16,256]{2,1,0:T(8,128)(2,1)S(1)}, u32[]{:S(2)}, u32[]{:S(2)}) %all-to-all-start.1) | async-done | bytes 524320 | tf_op jit(solution)/shard_map/all_to_all | solution.py:205
  113.1 4.7 %collective-permute-start.10 = (bf16[64,16,256]{2,1,0:T(8,128)(2,1)S(1)}, bf16[64,16,256]{2,1,0:T(8,128)(2,1)S(1)}, u32[]{:S(2)}, u32[]{:S(2)}) collective-permute-start(bf16[64,16,256]{2,1,0:T(8,128)(2,1)S(1)} %all-to-all-done.1), channel_id=1, source_target_pairs={{0,4},{4,0},{1,5},{5,1},{2,6},{6,2},{3,7},{7,3},{8,12},{12,8},{9,1... | collective-permute-start | bytes 1572872 | tf_op jit(solution)/shard_map/ppermute | solution.py:31
  117.8 1.5 %collective-permute-done.10 = bf16[64,16,256]{2,1,0:T(8,128)(2,1)S(1)} collective-permute-done((bf16[64,16,256]{2,1,0:T(8,128)(2,1)S(1)}, bf16[64,16,256]{2,1,0:T(8,128)(2,1)S(1)}, u32[]{:S(2)}, u32[]{:S(2)}) %collective-permute-start.10) | collective-permute-done | bytes 524320 | tf_op jit(solution)/shard_map/ppermute | solution.py:31
  119.3 2.9 %shard_map.48 = bf16[8,2,16,768]{3,2,1,0:T(8,128)(2,1)} custom-call(s32[3]{0:T(128)S(1)} %pad_add_fusion.place, bf16[4,8,2,16,256]{4,3,2,1,0:T(8,128)(2,1)S(1)} %bitcast.16, bf16[4,8,2,16,256]{4,3,2,1,0:T(8,128)(2,1)S(1)} %bitcast.19, bf16[512,768]{1,0:T(8,128)(2,1)S(1)} %get-tuple-element.22.wo00, bf16[512,768]{1,0:T(8,128)(2,1)S(1)} %get-tuple-element.24.wo10, ...), custom_call_target="tpu_custom_call" | custom-call | flops 800000000 | bytes 6000000 | tf_op jit(solution)/shard_map/pallas_call | solution.py:140
  (19 shorter events, 2.0 us)
Async XLA Ops:
  6.5 24.8 %all-to-all-start = ((bf16[16,16,768]{2,1,0:T(8,128)(2,1)}), bf16[16,16,768]{2,1,0:T(8,128)(2,1)S(1)}, u32[]{:S(2)}, u32[]{:S(2)}) async-start(bf16[16,16,768]{2,1,0:T(8,128)(2,1)} %bitcast.17), calls=%async_computation | async-start | bytes 786432 | tf_op jit(solution)/shard_map/all_to_all | solution.py:171
  16.8 64.4 %all-gather.2.cloned.1.call-start = ((), (), s32[]{:S(2)}) async-start(), calls=%async_computation.2 | async-start | bytes 5013504 | tf_op jit(solution)/shard_map/all_gather | solution.py:173
  16.9 1.0 copy-start.1
  18.5 7.8 %collective-permute-start.2 = (bf16[96,384]{1,0:T(8,128)(2,1)S(1)}, bf16[96,384]{1,0:T(8,128)(2,1)S(1)}, u32[]{:S(2)}, u32[]{:S(2)}) collective-permute-start(bf16[96,384]{1,0:T(8,128)(2,1)S(1)} %get-tuple-element.16), channel_id=1, source_target_pairs={{0,384},{128,0},{256,128},{384,256},{1,385},{129,1},{257,129},{385... | collective-permute-start | bytes 221192 | tf_op jit(solution)/shard_map/ppermute | solution.py:167
  21.3 6.6 %collective-permute-start.1 = (bf16[96,384]{1,0:T(8,128)(2,1)S(1)}, bf16[96,384]{1,0:T(8,128)(2,1)S(1)}, u32[]{:S(2)}, u32[]{:S(2)}) collective-permute-start(bf16[96,384]{1,0:T(8,128)(2,1)S(1)} %get-tuple-element.15), channel_id=1, source_target_pairs={{0,256},{128,384},{256,0},{384,128},{1,257},{129,385},{257,1},{385... | collective-permute-start | bytes 221192 | tf_op jit(solution)/shard_map/ppermute | solution.py:167
  23.7 6.4 %collective-permute-start = (bf16[96,384]{1,0:T(8,128)(2,1)S(1)}, bf16[96,384]{1,0:T(8,128)(2,1)S(1)}, u32[]{:S(2)}, u32[]{:S(2)}) collective-permute-start(bf16[96,384]{1,0:T(8,128)(2,1)S(1)} %get-tuple-element.14), channel_id=1, source_target_pairs={{0,128},{128,256},{256,384},{384,0},{1,129},{129,257},{257,385},{3... | collective-permute-start | bytes 221192 | tf_op jit(solution)/shard_map/ppermute | solution.py:167
  30.1 51.0 %copy-start.2 = (f32[3072]{0:T(1024)S(1)}, f32[3072]{0:T(1024)}, u32[]{:S(2)}) copy-start(f32[3072]{0:T(1024)} %param.5) | copy-start | bytes 36868
  31.3 11.1 %collective-permute-start.3 = (bf16[8,32,768]{2,1,0:T(8,128)(2,1)S(1)}, bf16[8,32,768]{2,1,0:T(8,128)(2,1)S(1)}, u32[]{:S(2)}, u32[]{:S(2)}) collective-permute-start(bf16[8,32,768]{2,1,0:T(8,128)(2,1)S(1)} %bitcast.20), channel_id=1, source_target_pairs={{0,8},{8,0},{1,9},{9,1},{2,10},{10,2},{3,11},{11,3},{4,12},{12,4},... | collective-permute-start | bytes 1179656 | tf_op jit(solution)/shard_map/ppermute | solution.py:31
  34.8 11.6 %collective-permute-start.4 = (bf16[8,32,768]{2,1,0:T(8,128)(2,1)S(1)}, bf16[8,32,768]{2,1,0:T(8,128)(2,1)S(1)}, u32[]{:S(2)}, u32[]{:S(2)}) collective-permute-start(bf16[8,32,768]{2,1,0:T(8,128)(2,1)S(1)} %bitcast.21), channel_id=1, source_target_pairs={{0,128},{128,256},{256,384},{384,0},{1,129},{129,257},{257,385},{3... | collective-permute-start | bytes 1179656 | tf_op jit(solution)/shard_map/ppermute | solution.py:175
  36.9 10.5 %collective-permute-start.5 = (bf16[8,32,768]{2,1,0:T(8,128)(2,1)S(1)}, bf16[8,32,768]{2,1,0:T(8,128)(2,1)S(1)}, u32[]{:S(2)}, u32[]{:S(2)}) collective-permute-start(bf16[8,32,768]{2,1,0:T(8,128)(2,1)S(1)} %bitcast.22), channel_id=1, source_target_pairs={{0,384},{128,0},{256,128},{384,256},{1,385},{129,1},{257,129},{385... | collective-permute-start | bytes 1179656 | tf_op jit(solution)/shard_map/ppermute | solution.py:175
  47.4 15.5 %collective-permute-start.6 = (bf16[8,32,768]{2,1,0:T(8,128)(2,1)S(1)}, bf16[8,32,768]{2,1,0:T(8,128)(2,1)S(1)}, u32[]{:S(2)}, u32[]{:S(2)}) collective-permute-start(bf16[8,32,768]{2,1,0:T(8,128)(2,1)S(1)} %collective-permute-done.3.xb), channel_id=1, source_target_pairs={{0,128},{128,256},{256,384},{384,0},{1,129},{129,257},{257,385},{3... | collective-permute-start | bytes 1179656 | tf_op jit(solution)/shard_map/ppermute | solution.py:177
  50.6 12.4 %collective-permute-start.7 = (bf16[8,32,768]{2,1,0:T(8,128)(2,1)S(1)}, bf16[8,32,768]{2,1,0:T(8,128)(2,1)S(1)}, u32[]{:S(2)}, u32[]{:S(2)}) collective-permute-start(bf16[8,32,768]{2,1,0:T(8,128)(2,1)S(1)} %collective-permute-done.3.xb), channel_id=1, source_target_pairs={{0,384},{128,0},{256,128},{384,256},{1,385},{129,1},{257,129},{385... | collective-permute-start | bytes 1179656 | tf_op jit(solution)/shard_map/ppermute | solution.py:177
  57.3 45.4 %collective-permute-start.11 = (bf16[512,1536]{1,0:T(8,128)(2,1)}, bf16[512,1536]{1,0:T(8,128)(2,1)}, u32[]{:S(2)}, u32[]{:S(2)}) collective-permute-start(bf16[512,1536]{1,0:T(8,128)(2,1)} %constant_dynamic-slice_fusion.3), channel_id=1, source_target_pairs={{0,8},{8,0},{1,9},{9,1},{2,10},{10,2},{3,11},{11,3},{4,12},{12,4},... | collective-permute-start | bytes 4718600 | tf_op jit(solution)/shard_map/ppermute | solution.py:31
  59.5 8.9 %collective-permute-start.8 = (bf16[8,32,768]{2,1,0:T(8,128)(2,1)S(1)}, bf16[8,32,768]{2,1,0:T(8,128)(2,1)S(1)}, u32[]{:S(2)}, u32[]{:S(2)}) collective-permute-start(bf16[8,32,768]{2,1,0:T(8,128)(2,1)S(1)} %broadcast_select_fusion.1), channel_id=1, source_target_pairs={{0,128},{4,388},{128,256},{132,4},{256,384},{260,132},{384,0},{388... | collective-permute-start | bytes 1179656 | tf_op jit(solution)/shard_map/ppermute | solution.py:178
  63.0 9.7 %collective-permute-start.9 = (bf16[8,32,768]{2,1,0:T(8,128)(2,1)S(1)}, bf16[8,32,768]{2,1,0:T(8,128)(2,1)S(1)}, u32[]{:S(2)}, u32[]{:S(2)}) collective-permute-start(bf16[8,32,768]{2,1,0:T(8,128)(2,1)S(1)} %broadcast_select_fusion), channel_id=1, source_target_pairs={{0,128},{4,388},{128,256},{132,4},{256,384},{260,132},{384,0},{388... | collective-permute-start | bytes 1179656 | tf_op jit(solution)/shard_map/ppermute | solution.py:179
  88.7 24.4 %all-to-all-start.1 = ((bf16[64,16,256]{2,1,0:T(8,128)(2,1)}), bf16[64,16,256]{2,1,0:T(8,128)(2,1)S(1)}, u32[]{:S(2)}, u32[]{:S(2)}) async-start(bf16[64,16,256]{2,1,0:T(8,128)(2,1)} %bitcast.11), calls=%async_computation.1 | async-start | bytes 1048576 | tf_op jit(solution)/shard_map/all_to_all | solution.py:205
  97.1 22.2 %copy-start = (bf16[1,1,256,768]{3,2,1,0:T(8,128)(2,1)S(1)}, bf16[1,1,256,768]{3,2,1,0:T(8,128)(2,1)}, u32[]{:S(2)}) copy-start(bf16[1,1,256,768]{3,2,1,0:T(8,128)(2,1)} %param.4) | copy-start | bytes 1179652
  100.3 17.5 %collective-permute-start.12 = (bf16[512,768]{1,0:T(8,128)(2,1)}, bf16[512,768]{1,0:T(8,128)(2,1)S(1)}, u32[]{:S(2)}, u32[]{:S(2)}) collective-permute-start(bf16[512,768]{1,0:T(8,128)(2,1)} %get-tuple-element.21), channel_id=1, source_target_pairs={{0,4},{4,0},{1,5},{5,1},{2,6},{6,2},{3,7},{7,3},{8,12},{12,8},{9,1... | collective-permute-start | bytes 2359304 | tf_op jit(solution)/shard_map/ppermute | solution.py:31
  105.2 12.6 %collective-permute-start.13 = (bf16[512,768]{1,0:T(8,128)(2,1)}, bf16[512,768]{1,0:T(8,128)(2,1)}, u32[]{:S(2)}, u32[]{:S(2)}) collective-permute-start(bf16[512,768]{1,0:T(8,128)(2,1)} %get-tuple-element.23), channel_id=1, source_target_pairs={{0,4},{4,0},{1,5},{5,1},{2,6},{6,2},{3,7},{7,3},{8,12},{12,8},{9,1... | collective-permute-start | bytes 2359304 | tf_op jit(solution)/shard_map/ppermute | solution.py:31
  113.1 6.2 %collective-permute-start.10 = (bf16[64,16,256]{2,1,0:T(8,128)(2,1)S(1)}, bf16[64,16,256]{2,1,0:T(8,128)(2,1)S(1)}, u32[]{:S(2)}, u32[]{:S(2)}) collective-permute-start(bf16[64,16,256]{2,1,0:T(8,128)(2,1)S(1)} %all-to-all-done.1), channel_id=1, source_target_pairs={{0,4},{4,0},{1,5},{5,1},{2,6},{6,2},{3,7},{7,3},{8,12},{12,8},{9,1... | collective-permute-start | bytes 1572872 | tf_op jit(solution)/shard_map/ppermute | solution.py:31
Sparse Core Ops, SparseCore 0:
  31.5 49.6 all-gather.1

commit v5 on v4

--- a/solution.py
+++ b/solution.py
@@ -125,11 +125,18 @@
         out[:, side] = mixed.astype(BF16)
 
 
-def slice_kernel(place, source, *outs):
+def slice_kernel(place, source, *refs):
+    outs, sent = refs[:4], refs[4]
+    copies = []
     for k, out in enumerate(outs):
-        head = lax.rem(place[0] + k, 4)
+        head = pl.multiple_of(lax.rem(place[0] + k, 4) * HD, HD)
         for part in range(3):
-            out[:, HD * part : HD * part + HD] = source[part, :, pl.ds(pl.multiple_of(head * HD, HD), HD)]
+            target = out.at[:, pl.ds(HD * part, HD)]
+            copies.append(pltpu.make_async_copy(source.at[part, :, pl.ds(head, HD)], target, sent.at[3 * k + part]))
+    for copy in copies:
+        copy.start()
+    for copy in copies:
+        copy.wait()
 
 
 def after(value, *others):
@@ -163,6 +170,8 @@
         0,
         6 * 10**5,
         4,
+        [pltpu.SemaphoreType.DMA((12,))],
+        left_out=(1,),
     )
     w_rows = [slots[0]] + [lax.ppermute(slots[k], "x", ring(4, k)) for k in (1, 2, 3)]
     w_rows = jnp.stack(w_rows)
@@ -173,7 +182,7 @@
     w_rows = lax.all_gather(w_rows, ("c", "y"), axis=1, tiled=True)
     xb = swap(xa, "z")
     la, ra = (lax.ppermute(xa, "x", ring(4, shift)) for shift in (1, 3))
-    xb_late = after(xb, la, ra)
+    xb_late = after(xb, la)
     lb, rb = (lax.ppermute(xb_late, "x", ring(4, shift)) for shift in (1, 3))
     oa = lax.ppermute(jnp.where(c == 0, la, ra), ("x", "c"), across())
     ob = lax.ppermute(jnp.where(c == 0, lb, rb), ("x", "c"), across())

time: 130 us -> 130 us (level)
    all_gather x1, waiting for transfers between devices: 8.46 us -> 10 us  [body(): w_rows = lax.all_gather(w_rows, ('c', 'y'), axis=1, tiled=True)]
    ppermute x1, starting transfers between devices: 2.12 us -> 3.58 us  [body(): ob = lax.ppermute(jnp.where(c == 0, lb, rb), ('x', 'c'), across())]
    ppermute x1, starting transfers between devices: 3.36 us -> 2 us  [body(): oa = lax.ppermute(jnp.where(c == 0, la, ra), ('x', 'c'), across())]
  transfers between devices with their start and end apart: 17 -> 17, of which waited for: 11 -> 10; matrix products, arithmetic and copies ran while one was open for 7% -> 7% of each run, Pallas kernels for 6% -> 6%
where the time goes in v5:
time: 130 us; the launch traced here: 129 us
  starting transfers between devices  60 us (46%)
  waiting for transfers between devices  34.4 us (26%)
  between operations  13.7 us (11%)
  Pallas kernels  11.3 us (9%)
  local copies, waits for them, and re-layouts  9.24 us (7%)
    ppermute x5, starting transfers between devices, swap(): return lax.ppermute(value, axis, [(0, 1), (1, 0)])  14.8 us
    pallas_call x3, Pallas kernels, kernel_call(): pl.pallas_call(kernel, out_shape=shapes, in_specs=[SMEM if value.dtype ==...  11.3 us
    all_to_all x1, starting transfers between devices, body(): lax.all_to_all(tokens, ('y', 'c'), 0, 0, tiled=True).reshape(8, 32, QUARTER)  10.2 us
    all_gather x1, waiting for transfers between devices, body(): w_rows = lax.all_gather(w_rows, ('c', 'y'), axis=1, tiled=True)  10 us
    all_to_all x1, starting transfers between devices, body(): lax.all_to_all(attended.reshape(64, 16, 2 * HD), ('x', 'y', 'z'), 0, 0, t...  8.66 us
    dynamic_slice x3, local copies, waits for them, and re-layouts, half(): return lax.dynamic_slice_in_dim(value, index * size, size, axis=1)  8.26 us
    ppermute x3, starting transfers between devices, body(): lax.ppermute(slots[k], 'x', ring(4, k))  7.75 us
    ppermute x2, starting transfers between devices, body(): la, ra = (lax.ppermute(xa, 'x', ring(4, shift)) for shift in (1, 3))  6.49 us
  transfers between devices with their start and end apart: 17, of which 10 were waited for; matrix products, arithmetic and copies ran while one was open for 7% of the time, Pallas kernels for 6%

profile of v5, /device:TPU:1, one launch (start us, length us, event | category | flops | bytes accessed | tf_op | source)
XLA Modules:
  0.0 129.4 jit_solution(4350640337214402895)
XLA Ops:
  6.5 10.2 %all-to-all-start = ((bf16[16,16,768]{2,1,0:T(8,128)(2,1)}), bf16[16,16,768]{2,1,0:T(8,128)(2,1)S(1)}, u32[]{:S(2)}, u32[]{:S(2)}) async-start(bf16[16,16,768]{2,1,0:T(8,128)(2,1)} %bitcast.17), calls=%async_computation | async-start | bytes 786432 | tf_op jit(solution)/shard_map/all_to_all | solution.py:180
  16.9 1.0 copy-done.1
  18.6 2.8 %collective-permute-start.2 = (bf16[96,384]{1,0:T(8,128)(2,1)S(1)}, bf16[96,384]{1,0:T(8,128)(2,1)S(1)}, u32[]{:S(2)}, u32[]{:S(2)}) collective-permute-start(bf16[96,384]{1,0:T(8,128)(2,1)S(1)} %get-tuple-element.16), channel_id=1, source_target_pairs={{0,384},{128,0},{256,128},{384,256},{1,385},{129,1},{257,129},{385... | collective-permute-start | bytes 221192 | tf_op jit(solution)/shard_map/ppermute | solution.py:176
  21.4 2.4 %collective-permute-start.1 = (bf16[96,384]{1,0:T(8,128)(2,1)S(1)}, bf16[96,384]{1,0:T(8,128)(2,1)S(1)}, u32[]{:S(2)}, u32[]{:S(2)}) collective-permute-start(bf16[96,384]{1,0:T(8,128)(2,1)S(1)} %get-tuple-element.15), channel_id=1, source_target_pairs={{0,256},{128,384},{256,0},{384,128},{1,257},{129,385},{257,1},{385... | collective-permute-start | bytes 221192 | tf_op jit(solution)/shard_map/ppermute | solution.py:176
  23.8 2.5 %collective-permute-start = (bf16[96,384]{1,0:T(8,128)(2,1)S(1)}, bf16[96,384]{1,0:T(8,128)(2,1)S(1)}, u32[]{:S(2)}, u32[]{:S(2)}) collective-permute-start(bf16[96,384]{1,0:T(8,128)(2,1)S(1)} %get-tuple-element.14), channel_id=1, source_target_pairs={{0,128},{128,256},{256,384},{384,0},{1,129},{129,257},{257,385},{3... | collective-permute-start | bytes 221192 | tf_op jit(solution)/shard_map/ppermute | solution.py:176
  26.4 1.6 %collective-permute-done.1 = bf16[96,384]{1,0:T(8,128)(2,1)S(1)} collective-permute-done((bf16[96,384]{1,0:T(8,128)(2,1)S(1)}, bf16[96,384]{1,0:T(8,128)(2,1)S(1)}, u32[]{:S(2)}, u32[]{:S(2)}) %collective-permute-start.1) | collective-permute-done | bytes 73760 | tf_op jit(solution)/shard_map/ppermute | solution.py:176
  28.0 2.1 %collective-permute-done = bf16[96,384]{1,0:T(8,128)(2,1)S(1)} collective-permute-done((bf16[96,384]{1,0:T(8,128)(2,1)S(1)}, bf16[96,384]{1,0:T(8,128)(2,1)S(1)}, u32[]{:S(2)}, u32[]{:S(2)}) %collective-permute-start) | collective-permute-done | bytes 73760 | tf_op jit(solution)/shard_map/ppermute | solution.py:176
  30.2 0.8 pad_maximum_fusion
  31.3 3.6 %collective-permute-start.3 = (bf16[8,32,768]{2,1,0:T(8,128)(2,1)S(1)}, bf16[8,32,768]{2,1,0:T(8,128)(2,1)S(1)}, u32[]{:S(2)}, u32[]{:S(2)}) collective-permute-start(bf16[8,32,768]{2,1,0:T(8,128)(2,1)S(1)} %bitcast.20), channel_id=1, source_target_pairs={{0,8},{8,0},{1,9},{9,1},{2,10},{10,2},{3,11},{11,3},{4,12},{12,4},... | collective-permute-start | bytes 1179656 | tf_op jit(solution)/shard_map/ppermute | solution.py:31
  35.0 1.9 %collective-permute-start.4 = (bf16[8,32,768]{2,1,0:T(8,128)(2,1)S(1)}, bf16[8,32,768]{2,1,0:T(8,128)(2,1)S(1)}, u32[]{:S(2)}, u32[]{:S(2)}) collective-permute-start(bf16[8,32,768]{2,1,0:T(8,128)(2,1)S(1)} %bitcast.21), channel_id=1, source_target_pairs={{0,128},{128,256},{256,384},{384,0},{1,129},{129,257},{257,385},{3... | collective-permute-start | bytes 1179656 | tf_op jit(solution)/shard_map/ppermute | solution.py:184
  36.9 4.6 %collective-permute-start.6 = (bf16[8,32,768]{2,1,0:T(8,128)(2,1)S(1)}, bf16[8,32,768]{2,1,0:T(8,128)(2,1)S(1)}, u32[]{:S(2)}, u32[]{:S(2)}) collective-permute-start(bf16[8,32,768]{2,1,0:T(8,128)(2,1)S(1)} %bitcast.22), channel_id=1, source_target_pairs={{0,384},{128,0},{256,128},{384,256},{1,385},{129,1},{257,129},{385... | collective-permute-start | bytes 1179656 | tf_op jit(solution)/shard_map/ppermute | solution.py:184
  41.5 1.1 collective-permute-done.3.xb
  42.6 4.0 %collective-permute-done.4.la = bf16[8,32,768]{2,1,0:T(8,128)(2,1)S(1)} collective-permute-done((bf16[8,32,768]{2,1,0:T(8,128)(2,1)S(1)}, bf16[8,32,768]{2,1,0:T(8,128)(2,1)S(1)}, u32[]{:S(2)}, u32[]{:S(2)}) %collective-permute-start.4) | collective-permute-done | bytes 393248 | tf_op jit(solution)/shard_map/ppermute | solution.py:184
  46.6 1.9 %collective-permute-start.5 = (bf16[8,32,768]{2,1,0:T(8,128)(2,1)S(1)}, bf16[8,32,768]{2,1,0:T(8,128)(2,1)S(1)}, u32[]{:S(2)}, u32[]{:S(2)}) collective-permute-start(bf16[8,32,768]{2,1,0:T(8,128)(2,1)S(1)} %collective-permute-done.3.xb), channel_id=1, source_target_pairs={{0,128},{128,256},{256,384},{384,0},{1,129},{129,257},{257,385},{3... | collective-permute-start | bytes 1179656 | tf_op jit(solution)/shard_map/ppermute | solution.py:186
  48.5 4.6 %collective-permute-start.7 = (bf16[8,32,768]{2,1,0:T(8,128)(2,1)S(1)}, bf16[8,32,768]{2,1,0:T(8,128)(2,1)S(1)}, u32[]{:S(2)}, u32[]{:S(2)}) collective-permute-start(bf16[8,32,768]{2,1,0:T(8,128)(2,1)S(1)} %collective-permute-done.3.xb), channel_id=1, source_target_pairs={{0,384},{128,0},{256,128},{384,256},{1,385},{129,1},{257,129},{385... | collective-permute-start | bytes 1179656 | tf_op jit(solution)/shard_map/ppermute | solution.py:186
  53.1 2.7 %constant_dynamic-slice_fusion.3 = bf16[512,1536]{1,0:T(8,128)(2,1)} fusion(bf16[512,3072]{1,0:T(8,128)(2,1)} %param.7, s32[]{:T(128)S(6)} %select_n.39), kind=kLoop, calls=%fused_computation.6 | loop fusion | bytes 3145732 | tf_op jit(solution)/shard_map/dynamic_slice | solution.py:191
  55.8 2.1 %collective-permute-start.11 = (bf16[512,1536]{1,0:T(8,128)(2,1)}, bf16[512,1536]{1,0:T(8,128)(2,1)}, u32[]{:S(2)}, u32[]{:S(2)}) collective-permute-start(bf16[512,1536]{1,0:T(8,128)(2,1)} %constant_dynamic-slice_fusion.3), channel_id=1, source_target_pairs={{0,8},{8,0},{1,9},{9,1},{2,10},{10,2},{3,11},{11,3},{4,12},{12,4},... | collective-permute-start | bytes 4718600 | tf_op jit(solution)/shard_map/ppermute | solution.py:31
  58.0 2.0 %collective-permute-start.8 = (bf16[8,32,768]{2,1,0:T(8,128)(2,1)S(1)}, bf16[8,32,768]{2,1,0:T(8,128)(2,1)S(1)}, u32[]{:S(2)}, u32[]{:S(2)}) collective-permute-start(bf16[8,32,768]{2,1,0:T(8,128)(2,1)S(1)} %broadcast_select_fusion.1), channel_id=1, source_target_pairs={{0,128},{4,388},{128,256},{132,4},{256,384},{260,132},{384,0},{388... | collective-permute-start | bytes 1179656 | tf_op jit(solution)/shard_map/ppermute | solution.py:187
  60.1 3.6 %collective-permute-start.9 = (bf16[8,32,768]{2,1,0:T(8,128)(2,1)S(1)}, bf16[8,32,768]{2,1,0:T(8,128)(2,1)S(1)}, u32[]{:S(2)}, u32[]{:S(2)}) collective-permute-start(bf16[8,32,768]{2,1,0:T(8,128)(2,1)S(1)} %broadcast_select_fusion), channel_id=1, source_target_pairs={{0,128},{4,388},{128,256},{132,4},{256,384},{260,132},{384,0},{388... | collective-permute-start | bytes 1179656 | tf_op jit(solution)/shard_map/ppermute | solution.py:188
  63.7 3.3 %collective-permute-done.8.oa = bf16[8,32,768]{2,1,0:T(8,128)(2,1)S(1)} collective-permute-done((bf16[8,32,768]{2,1,0:T(8,128)(2,1)S(1)}, bf16[8,32,768]{2,1,0:T(8,128)(2,1)S(1)}, u32[]{:S(2)}, u32[]{:S(2)}) %collective-permute-start.8) | collective-permute-done | bytes 393248 | tf_op jit(solution)/shard_map/ppermute | solution.py:187
  66.9 4.2 %collective-permute-done.9.ob = bf16[8,32,768]{2,1,0:T(8,128)(2,1)S(1)} collective-permute-done((bf16[8,32,768]{2,1,0:T(8,128)(2,1)S(1)}, bf16[8,32,768]{2,1,0:T(8,128)(2,1)S(1)}, u32[]{:S(2)}, u32[]{:S(2)}) %collective-permute-start.9) | collective-permute-done | bytes 393248 | tf_op jit(solution)/shard_map/ppermute | solution.py:188
  71.2 10.0 %all-gather.2.cloned.1.call-done.w_hbm = bf16[4,1536,384]{2,1,0:T(8,128)(2,1)} async-done(((bf16[4,96,384]{2,1,0:T(8,128)(2,1)}), bf16[4,1536,384]{2,1,0:T(8,128)(2,1)}) %all-gather.2.cloned.1.call-update) | async-done | bytes 4718608 | tf_op jit(solution)/shard_map/all_gather | solution.py:182
  81.2 7.6 %shard_map.47 = bf16[4,8,2,16,256]{4,3,2,1,0:T(8,128)(2,1)} custom-call(s32[3]{0:T(128)S(1)} %pad_add_fusion.place, bf16[8,32,768]{2,1,0:T(8,128)(2,1)S(1)} %bitcast.23, bf16[8,32,768]{2,1,0:T(8,128)(2,1)S(1)} %collective-permute-done.3.xb, bf16[8,32,768]{2,1,0:T(8,128)(2,1)S(1)} %collective-permute-done.4.la, ...), custom_call_target="tpu_custom_call" | custom-call | flops 3000000000 | bytes 9000000 | tf_op jit(solution)/shard_map/pallas_call | solution.py:147
  88.8 8.7 %all-to-all-start.1 = ((bf16[64,16,256]{2,1,0:T(8,128)(2,1)}), bf16[64,16,256]{2,1,0:T(8,128)(2,1)S(1)}, u32[]{:S(2)}, u32[]{:S(2)}) async-start(bf16[64,16,256]{2,1,0:T(8,128)(2,1)} %bitcast.11), calls=%async_computation.1 | async-start | bytes 1048576 | tf_op jit(solution)/shard_map/all_to_all | solution.py:214
  97.5 3.1 %constant_dynamic-slice_fusion.1 = (bf16[512,768]{1,0:T(8,128)(2,1)}, bf16[512,768]{1,0:T(8,128)(2,1)S(1)}) fusion(bf16[512,3072]{1,0:T(8,128)(2,1)} %param.7, s32[]{:T(128)S(6)} %dynamic_slice.25, s32[]{:T(128)S(6)} %dynamic_slice.21), kind=kLoop, calls=%fused_computation.4 | loop fusion | bytes 3145736 | tf_op jit(solution)/shard_map/dynamic_slice | solution.py:191
  100.6 2.4 %collective-permute-start.12 = (bf16[512,768]{1,0:T(8,128)(2,1)}, bf16[512,768]{1,0:T(8,128)(2,1)S(1)}, u32[]{:S(2)}, u32[]{:S(2)}) collective-permute-start(bf16[512,768]{1,0:T(8,128)(2,1)} %get-tuple-element.21), channel_id=1, source_target_pairs={{0,4},{4,0},{1,5},{5,1},{2,6},{6,2},{3,7},{7,3},{8,12},{12,8},{9,1... | collective-permute-start | bytes 2359304 | tf_op jit(solution)/shard_map/ppermute | solution.py:31
  103.1 2.4 %constant_dynamic-slice_fusion = (bf16[512,768]{1,0:T(8,128)(2,1)}, bf16[512,768]{1,0:T(8,128)(2,1)S(1)}) fusion(bf16[512,1536]{1,0:T(8,128)(2,1)} %collective-permute-done.11, s32[]{:T(128)S(6)} %select_n.40, s32[]{:T(128)S(6)} %select_n.35), kind=kLoop, calls=%fused_computation.3 | loop fusion | bytes 3145736 | tf_op jit(solution)/shard_map/dynamic_slice | solution.py:191
  105.5 1.9 %collective-permute-start.13 = (bf16[512,768]{1,0:T(8,128)(2,1)}, bf16[512,768]{1,0:T(8,128)(2,1)}, u32[]{:S(2)}, u32[]{:S(2)}) collective-permute-start(bf16[512,768]{1,0:T(8,128)(2,1)} %get-tuple-element.23), channel_id=1, source_target_pairs={{0,4},{4,0},{1,5},{5,1},{2,6},{6,2},{3,7},{7,3},{8,12},{12,8},{9,1... | collective-permute-start | bytes 2359304 | tf_op jit(solution)/shard_map/ppermute | solution.py:31
  107.4 6.0 %all-to-all-done.1 = bf16[64,16,256]{2,1,0:T(8,128)(2,1)S(1)} async-done(((bf16[64,16,256]{2,1,0:T(8,128)(2,1)}), bf16[64,16,256]{2,1,0:T(8,128)(2,1)S(1)}, u32[]{:S(2)}, u32[]{:S(2)}) %all-to-all-start.1) | async-done | bytes 524320 | tf_op jit(solution)/shard_map/all_to_all | solution.py:214
  113.5 4.7 %collective-permute-start.10 = (bf16[64,16,256]{2,1,0:T(8,128)(2,1)S(1)}, bf16[64,16,256]{2,1,0:T(8,128)(2,1)S(1)}, u32[]{:S(2)}, u32[]{:S(2)}) collective-permute-start(bf16[64,16,256]{2,1,0:T(8,128)(2,1)S(1)} %all-to-all-done.1), channel_id=1, source_target_pairs={{0,4},{4,0},{1,5},{5,1},{2,6},{6,2},{3,7},{7,3},{8,12},{12,8},{9,1... | collective-permute-start | bytes 1572872 | tf_op jit(solution)/shard_map/ppermute | solution.py:31
  118.2 1.5 %collective-permute-done.10 = bf16[64,16,256]{2,1,0:T(8,128)(2,1)S(1)} collective-permute-done((bf16[64,16,256]{2,1,0:T(8,128)(2,1)S(1)}, bf16[64,16,256]{2,1,0:T(8,128)(2,1)S(1)}, u32[]{:S(2)}, u32[]{:S(2)}) %collective-permute-start.10) | collective-permute-done | bytes 524320 | tf_op jit(solution)/shard_map/ppermute | solution.py:31
  119.7 2.9 %shard_map.48 = bf16[8,2,16,768]{3,2,1,0:T(8,128)(2,1)} custom-call(s32[3]{0:T(128)S(1)} %pad_add_fusion.place, bf16[4,8,2,16,256]{4,3,2,1,0:T(8,128)(2,1)S(1)} %bitcast.16, bf16[4,8,2,16,256]{4,3,2,1,0:T(8,128)(2,1)S(1)} %bitcast.19, bf16[512,768]{1,0:T(8,128)(2,1)S(1)} %get-tuple-element.22.wo00, bf16[512,768]{1,0:T(8,128)(2,1)S(1)} %get-tuple-element.24.wo10, ...), custom_call_target="tpu_custom_call" | custom-call | flops 800000000 | bytes 6000000 | tf_op jit(solution)/shard_map/pallas_call | solution.py:147
  (19 shorter events, 1.4 us)
Async XLA Ops:
  6.5 24.8 %all-to-all-start = ((bf16[16,16,768]{2,1,0:T(8,128)(2,1)}), bf16[16,16,768]{2,1,0:T(8,128)(2,1)S(1)}, u32[]{:S(2)}, u32[]{:S(2)}) async-start(bf16[16,16,768]{2,1,0:T(8,128)(2,1)} %bitcast.17), calls=%async_computation | async-start | bytes 786432 | tf_op jit(solution)/shard_map/all_to_all | solution.py:180
  16.8 64.4 %all-gather.2.cloned.1.call-start = ((), (), s32[]{:S(2)}) async-start(), calls=%async_computation.2 | async-start | bytes 5013504 | tf_op jit(solution)/shard_map/all_gather | solution.py:182
  16.9 1.0 copy-start.1
  18.6 7.8 %collective-permute-start.2 = (bf16[96,384]{1,0:T(8,128)(2,1)S(1)}, bf16[96,384]{1,0:T(8,128)(2,1)S(1)}, u32[]{:S(2)}, u32[]{:S(2)}) collective-permute-start(bf16[96,384]{1,0:T(8,128)(2,1)S(1)} %get-tuple-element.16), channel_id=1, source_target_pairs={{0,384},{128,0},{256,128},{384,256},{1,385},{129,1},{257,129},{385... | collective-permute-start | bytes 221192 | tf_op jit(solution)/shard_map/ppermute | solution.py:176
  21.4 6.6 %collective-permute-start.1 = (bf16[96,384]{1,0:T(8,128)(2,1)S(1)}, bf16[96,384]{1,0:T(8,128)(2,1)S(1)}, u32[]{:S(2)}, u32[]{:S(2)}) collective-permute-start(bf16[96,384]{1,0:T(8,128)(2,1)S(1)} %get-tuple-element.15), channel_id=1, source_target_pairs={{0,256},{128,384},{256,0},{384,128},{1,257},{129,385},{257,1},{385... | collective-permute-start | bytes 221192 | tf_op jit(solution)/shard_map/ppermute | solution.py:176
  23.8 6.3 %collective-permute-start = (bf16[96,384]{1,0:T(8,128)(2,1)S(1)}, bf16[96,384]{1,0:T(8,128)(2,1)S(1)}, u32[]{:S(2)}, u32[]{:S(2)}) collective-permute-start(bf16[96,384]{1,0:T(8,128)(2,1)S(1)} %get-tuple-element.14), channel_id=1, source_target_pairs={{0,128},{128,256},{256,384},{384,0},{1,129},{129,257},{257,385},{3... | collective-permute-start | bytes 221192 | tf_op jit(solution)/shard_map/ppermute | solution.py:176
  30.2 51.0 %copy-start.2 = (f32[3072]{0:T(1024)S(1)}, f32[3072]{0:T(1024)}, u32[]{:S(2)}) copy-start(f32[3072]{0:T(1024)} %param.5) | copy-start | bytes 36868
  31.3 11.2 %collective-permute-start.3 = (bf16[8,32,768]{2,1,0:T(8,128)(2,1)S(1)}, bf16[8,32,768]{2,1,0:T(8,128)(2,1)S(1)}, u32[]{:S(2)}, u32[]{:S(2)}) collective-permute-start(bf16[8,32,768]{2,1,0:T(8,128)(2,1)S(1)} %bitcast.20), channel_id=1, source_target_pairs={{0,8},{8,0},{1,9},{9,1},{2,10},{10,2},{3,11},{11,3},{4,12},{12,4},... | collective-permute-start | bytes 1179656 | tf_op jit(solution)/shard_map/ppermute | solution.py:31
  35.0 11.6 %collective-permute-start.4 = (bf16[8,32,768]{2,1,0:T(8,128)(2,1)S(1)}, bf16[8,32,768]{2,1,0:T(8,128)(2,1)S(1)}, u32[]{:S(2)}, u32[]{:S(2)}) collective-permute-start(bf16[8,32,768]{2,1,0:T(8,128)(2,1)S(1)} %bitcast.21), channel_id=1, source_target_pairs={{0,128},{128,256},{256,384},{384,0},{1,129},{129,257},{257,385},{3... | collective-permute-start | bytes 1179656 | tf_op jit(solution)/shard_map/ppermute | solution.py:184
  36.9 21.1 %collective-permute-start.6 = (bf16[8,32,768]{2,1,0:T(8,128)(2,1)S(1)}, bf16[8,32,768]{2,1,0:T(8,128)(2,1)S(1)}, u32[]{:S(2)}, u32[]{:S(2)}) collective-permute-start(bf16[8,32,768]{2,1,0:T(8,128)(2,1)S(1)} %bitcast.22), channel_id=1, source_target_pairs={{0,384},{128,0},{256,128},{384,256},{1,385},{129,1},{257,129},{385... | collective-permute-start | bytes 1179656 | tf_op jit(solution)/shard_map/ppermute | solution.py:184
  46.6 13.4 %collective-permute-start.5 = (bf16[8,32,768]{2,1,0:T(8,128)(2,1)S(1)}, bf16[8,32,768]{2,1,0:T(8,128)(2,1)S(1)}, u32[]{:S(2)}, u32[]{:S(2)}) collective-permute-start(bf16[8,32,768]{2,1,0:T(8,128)(2,1)S(1)} %collective-permute-done.3.xb), channel_id=1, source_target_pairs={{0,128},{128,256},{256,384},{384,0},{1,129},{129,257},{257,385},{3... | collective-permute-start | bytes 1179656 | tf_op jit(solution)/shard_map/ppermute | solution.py:186
  48.5 11.5 %collective-permute-start.7 = (bf16[8,32,768]{2,1,0:T(8,128)(2,1)S(1)}, bf16[8,32,768]{2,1,0:T(8,128)(2,1)S(1)}, u32[]{:S(2)}, u32[]{:S(2)}) collective-permute-start(bf16[8,32,768]{2,1,0:T(8,128)(2,1)S(1)} %collective-permute-done.3.xb), channel_id=1, source_target_pairs={{0,384},{128,0},{256,128},{384,256},{1,385},{129,1},{257,129},{385... | collective-permute-start | bytes 1179656 | tf_op jit(solution)/shard_map/ppermute | solution.py:186
  55.8 47.3 %collective-permute-start.11 = (bf16[512,1536]{1,0:T(8,128)(2,1)}, bf16[512,1536]{1,0:T(8,128)(2,1)}, u32[]{:S(2)}, u32[]{:S(2)}) collective-permute-start(bf16[512,1536]{1,0:T(8,128)(2,1)} %constant_dynamic-slice_fusion.3), channel_id=1, source_target_pairs={{0,8},{8,0},{1,9},{9,1},{2,10},{10,2},{3,11},{11,3},{4,12},{12,4},... | collective-permute-start | bytes 4718600 | tf_op jit(solution)/shard_map/ppermute | solution.py:31
  58.0 8.9 %collective-permute-start.8 = (bf16[8,32,768]{2,1,0:T(8,128)(2,1)S(1)}, bf16[8,32,768]{2,1,0:T(8,128)(2,1)S(1)}, u32[]{:S(2)}, u32[]{:S(2)}) collective-permute-start(bf16[8,32,768]{2,1,0:T(8,128)(2,1)S(1)} %broadcast_select_fusion.1), channel_id=1, source_target_pairs={{0,128},{4,388},{128,256},{132,4},{256,384},{260,132},{384,0},{388... | collective-permute-start | bytes 1179656 | tf_op jit(solution)/shard_map/ppermute | solution.py:187
  60.1 11.1 %collective-permute-start.9 = (bf16[8,32,768]{2,1,0:T(8,128)(2,1)S(1)}, bf16[8,32,768]{2,1,0:T(8,128)(2,1)S(1)}, u32[]{:S(2)}, u32[]{:S(2)}) collective-permute-start(bf16[8,32,768]{2,1,0:T(8,128)(2,1)S(1)} %broadcast_select_fusion), channel_id=1, source_target_pairs={{0,128},{4,388},{128,256},{132,4},{256,384},{260,132},{384,0},{388... | collective-permute-start | bytes 1179656 | tf_op jit(solution)/shard_map/ppermute | solution.py:188
  88.8 24.7 %all-to-all-start.1 = ((bf16[64,16,256]{2,1,0:T(8,128)(2,1)}), bf16[64,16,256]{2,1,0:T(8,128)(2,1)S(1)}, u32[]{:S(2)}, u32[]{:S(2)}) async-start(bf16[64,16,256]{2,1,0:T(8,128)(2,1)} %bitcast.11), calls=%async_computation.1 | async-start | bytes 1048576 | tf_op jit(solution)/shard_map/all_to_all | solution.py:214
  97.5 22.2 %copy-start = (bf16[1,1,256,768]{3,2,1,0:T(8,128)(2,1)S(1)}, bf16[1,1,256,768]{3,2,1,0:T(8,128)(2,1)}, u32[]{:S(2)}) copy-start(bf16[1,1,256,768]{3,2,1,0:T(8,128)(2,1)} %param.4) | copy-start | bytes 1179652
  100.6 17.5 %collective-permute-start.12 = (bf16[512,768]{1,0:T(8,128)(2,1)}, bf16[512,768]{1,0:T(8,128)(2,1)S(1)}, u32[]{:S(2)}, u32[]{:S(2)}) collective-permute-start(bf16[512,768]{1,0:T(8,128)(2,1)} %get-tuple-element.21), channel_id=1, source_target_pairs={{0,4},{4,0},{1,5},{5,1},{2,6},{6,2},{3,7},{7,3},{8,12},{12,8},{9,1... | collective-permute-start | bytes 2359304 | tf_op jit(solution)/shard_map/ppermute | solution.py:31
  105.5 12.6 %collective-permute-start.13 = (bf16[512,768]{1,0:T(8,128)(2,1)}, bf16[512,768]{1,0:T(8,128)(2,1)}, u32[]{:S(2)}, u32[]{:S(2)}) collective-permute-start(bf16[512,768]{1,0:T(8,128)(2,1)} %get-tuple-element.23), channel_id=1, source_target_pairs={{0,4},{4,0},{1,5},{5,1},{2,6},{6,2},{3,7},{7,3},{8,12},{12,8},{9,1... | collective-permute-start | bytes 2359304 | tf_op jit(solution)/shard_map/ppermute | solution.py:31
  113.5 6.2 %collective-permute-start.10 = (bf16[64,16,256]{2,1,0:T(8,128)(2,1)S(1)}, bf16[64,16,256]{2,1,0:T(8,128)(2,1)S(1)}, u32[]{:S(2)}, u32[]{:S(2)}) collective-permute-start(bf16[64,16,256]{2,1,0:T(8,128)(2,1)S(1)} %all-to-all-done.1), channel_id=1, source_target_pairs={{0,4},{4,0},{1,5},{5,1},{2,6},{6,2},{3,7},{7,3},{8,12},{12,8},{9,1... | collective-permute-start | bytes 1572872 | tf_op jit(solution)/shard_map/ppermute | solution.py:31
Sparse Core Ops, SparseCore 0:
  31.5 49.6 all-gather.1

commit v6 on v4

--- a/solution.py
+++ b/solution.py
@@ -80,8 +80,8 @@
     copies = []
     for k in range(4):
         for core in range(2):
-            target = w_rows.at[pl.ds(QUARTER * k, QUARTER), pl.ds(3 * HD * core, 3 * HD)]
-            source = w_hbm.at[k, pl.ds(QUARTER * core, QUARTER)]
+            target = w_rows.at[k, :, :, pl.ds(3 * HD * core, 3 * HD)]
+            source = w_hbm.at[pl.ds(8 * core, 8), k]
             copies.append(pltpu.make_async_copy(source, target, w_sent.at[2 * k + core]))
     for copy in copies:
         copy.start()
@@ -98,7 +98,7 @@
         copy.wait()
     for i in range(2):
         rows = slice(256 * i, 256 * i + 256)
-        projected[rows] = jnp.dot(normed[rows], w_rows[...], preferred_element_type=F32)
+        projected[rows] = jnp.dot(normed[rows], w_rows[...].reshape(WIDTH, 6 * HD), preferred_element_type=F32)
     attended = attend(projected[...])
     for i, shift in enumerate((0, 3, 1, 2)):
         frame = lax.rem(x + shift, 4)
@@ -170,7 +170,7 @@
     tokens = frames_in.reshape(16, 16, QUARTER)
     xa = lax.all_to_all(tokens, ("y", "c"), 0, 0, tiled=True).reshape(8, 32, QUARTER)
     xa, w_rows = lax.optimization_barrier((xa, w_rows))
-    w_rows = lax.all_gather(w_rows, ("c", "y"), axis=1, tiled=True)
+    w_rows = lax.all_gather(w_rows, ("c", "y"))
     xb = swap(xa, "z")
     la, ra = (lax.ppermute(xa, "x", ring(4, shift)) for shift in (1, 3))
     xb_late = after(xb, la, ra)
@@ -195,7 +195,7 @@
         48,
         [
             pltpu.VMEM((512, WIDTH), BF16),
-            pltpu.VMEM((WIDTH, 6 * HD), BF16),
+            pltpu.VMEM((4, 8, 96, 6 * HD), BF16),
             pltpu.VMEM((512, 6 * HD), F32),
             pltpu.SemaphoreType.DMA((8,)),
         ],

time: 130 us -> 129 us (level)
  no operation moved by 1% of the time
where the time goes in v6:
time: 129 us
  starting transfers between devices  60.3 us (47%)
  waiting for transfers between devices  33.9 us (26%)
  between operations  13.6 us (11%)
  Pallas kernels  10.7 us (8%)
  local copies, waits for them, and re-layouts  9.21 us (7%)
    ppermute x5, starting transfers between devices, swap(): return lax.ppermute(value, axis, [(0, 1), (1, 0)])  14.7 us
    pallas_call x3, Pallas kernels, kernel_call(): pl.pallas_call(kernel, out_shape=shapes, in_specs=[SMEM if value.dtype ==...  10.7 us
    all_to_all x1, starting transfers between devices, body(): lax.all_to_all(tokens, ('y', 'c'), 0, 0, tiled=True).reshape(8, 32, QUARTER)  10.2 us
    all_to_all x1, starting transfers between devices, body(): lax.all_to_all(attended.reshape(64, 16, 2 * HD), ('x', 'y', 'z'), 0, 0, t...  8.47 us
    all_gather x1, waiting for transfers between devices, body(): w_rows = lax.all_gather(w_rows, ('c', 'y'))  8.38 us
    dynamic_slice x3, local copies, waits for them, and re-layouts, half(): return lax.dynamic_slice_in_dim(value, index * size, size, axis=1)  8.23 us
    ppermute x3, starting transfers between devices, body(): lax.ppermute(slots[k], 'x', ring(4, k))  7.75 us
    ppermute x2, starting transfers between devices, body(): lb, rb = (lax.ppermute(xb_late, 'x', ring(4, shift)) for shift in (1, 3))  7.18 us
  transfers between devices with their start and end apart: 17, of which 11 were waited for; matrix products, arithmetic and copies ran while one was open for 7% of the time, Pallas kernels for 6%

profile of v6, /device:TPU:1, one launch (start us, length us, event | category | flops | bytes accessed | tf_op | source)
XLA Modules:
  0.0 128.6 jit_solution(1719774546683148796)
XLA Ops:
  6.5 10.2 %all-to-all-start = ((bf16[16,16,768]{2,1,0:T(8,128)(2,1)}), bf16[16,16,768]{2,1,0:T(8,128)(2,1)S(1)}, u32[]{:S(2)}, u32[]{:S(2)}) async-start(bf16[16,16,768]{2,1,0:T(8,128)(2,1)} %bitcast.18), calls=%async_computation | async-start | bytes 786432 | tf_op jit(solution)/shard_map/all_to_all | solution.py:171
  16.9 1.0 copy-done.1
  18.5 2.8 %collective-permute-start.2 = (bf16[96,384]{1,0:T(8,128)(2,1)S(1)}, bf16[96,384]{1,0:T(8,128)(2,1)S(1)}, u32[]{:S(2)}, u32[]{:S(2)}) collective-permute-start(bf16[96,384]{1,0:T(8,128)(2,1)S(1)} %get-tuple-element.16), channel_id=1, source_target_pairs={{0,384},{128,0},{256,128},{384,256},{1,385},{129,1},{257,129},{385... | collective-permute-start | bytes 221192 | tf_op jit(solution)/shard_map/ppermute | solution.py:167
  21.3 2.4 %collective-permute-start.1 = (bf16[96,384]{1,0:T(8,128)(2,1)S(1)}, bf16[96,384]{1,0:T(8,128)(2,1)S(1)}, u32[]{:S(2)}, u32[]{:S(2)}) collective-permute-start(bf16[96,384]{1,0:T(8,128)(2,1)S(1)} %get-tuple-element.15), channel_id=1, source_target_pairs={{0,256},{128,384},{256,0},{384,128},{1,257},{129,385},{257,1},{385... | collective-permute-start | bytes 221192 | tf_op jit(solution)/shard_map/ppermute | solution.py:167
  23.7 2.5 %collective-permute-start = (bf16[96,384]{1,0:T(8,128)(2,1)S(1)}, bf16[96,384]{1,0:T(8,128)(2,1)S(1)}, u32[]{:S(2)}, u32[]{:S(2)}) collective-permute-start(bf16[96,384]{1,0:T(8,128)(2,1)S(1)} %get-tuple-element.14), channel_id=1, source_target_pairs={{0,128},{128,256},{256,384},{384,0},{1,129},{129,257},{257,385},{3... | collective-permute-start | bytes 221192 | tf_op jit(solution)/shard_map/ppermute | solution.py:167
  26.2 1.6 %collective-permute-done.1 = bf16[96,384]{1,0:T(8,128)(2,1)S(1)} collective-permute-done((bf16[96,384]{1,0:T(8,128)(2,1)S(1)}, bf16[96,384]{1,0:T(8,128)(2,1)S(1)}, u32[]{:S(2)}, u32[]{:S(2)}) %collective-permute-start.1) | collective-permute-done | bytes 73760 | tf_op jit(solution)/shard_map/ppermute | solution.py:167
  27.9 2.2 %collective-permute-done = bf16[96,384]{1,0:T(8,128)(2,1)S(1)} collective-permute-done((bf16[96,384]{1,0:T(8,128)(2,1)S(1)}, bf16[96,384]{1,0:T(8,128)(2,1)S(1)}, u32[]{:S(2)}, u32[]{:S(2)}) %collective-permute-start) | collective-permute-done | bytes 73760 | tf_op jit(solution)/shard_map/ppermute | solution.py:167
  31.3 3.5 %collective-permute-start.3 = (bf16[8,32,768]{2,1,0:T(8,128)(2,1)S(1)}, bf16[8,32,768]{2,1,0:T(8,128)(2,1)S(1)}, u32[]{:S(2)}, u32[]{:S(2)}) collective-permute-start(bf16[8,32,768]{2,1,0:T(8,128)(2,1)S(1)} %bitcast.21), channel_id=1, source_target_pairs={{0,8},{8,0},{1,9},{9,1},{2,10},{10,2},{3,11},{11,3},{4,12},{12,4},... | collective-permute-start | bytes 1179656 | tf_op jit(solution)/shard_map/ppermute | solution.py:31
  34.8 2.0 %collective-permute-start.4 = (bf16[8,32,768]{2,1,0:T(8,128)(2,1)S(1)}, bf16[8,32,768]{2,1,0:T(8,128)(2,1)S(1)}, u32[]{:S(2)}, u32[]{:S(2)}) collective-permute-start(bf16[8,32,768]{2,1,0:T(8,128)(2,1)S(1)} %bitcast.22), channel_id=1, source_target_pairs={{0,128},{128,256},{256,384},{384,0},{1,129},{129,257},{257,385},{3... | collective-permute-start | bytes 1179656 | tf_op jit(solution)/shard_map/ppermute | solution.py:175
  36.9 4.5 %collective-permute-start.5 = (bf16[8,32,768]{2,1,0:T(8,128)(2,1)S(1)}, bf16[8,32,768]{2,1,0:T(8,128)(2,1)S(1)}, u32[]{:S(2)}, u32[]{:S(2)}) collective-permute-start(bf16[8,32,768]{2,1,0:T(8,128)(2,1)S(1)} %bitcast.23), channel_id=1, source_target_pairs={{0,384},{128,0},{256,128},{384,256},{1,385},{129,1},{257,129},{385... | collective-permute-start | bytes 1179656 | tf_op jit(solution)/shard_map/ppermute | solution.py:175
  41.3 1.1 collective-permute-done.3.xb
  42.4 4.0 %collective-permute-done.4.la = bf16[8,32,768]{2,1,0:T(8,128)(2,1)S(1)} collective-permute-done((bf16[8,32,768]{2,1,0:T(8,128)(2,1)S(1)}, bf16[8,32,768]{2,1,0:T(8,128)(2,1)S(1)}, u32[]{:S(2)}, u32[]{:S(2)}) %collective-permute-start.4) | collective-permute-done | bytes 393248 | tf_op jit(solution)/shard_map/ppermute | solution.py:175
  46.5 0.9 collective-permute-done.5.ra
  47.4 3.1 %collective-permute-start.6 = (bf16[8,32,768]{2,1,0:T(8,128)(2,1)S(1)}, bf16[8,32,768]{2,1,0:T(8,128)(2,1)S(1)}, u32[]{:S(2)}, u32[]{:S(2)}) collective-permute-start(bf16[8,32,768]{2,1,0:T(8,128)(2,1)S(1)} %collective-permute-done.3.xb), channel_id=1, source_target_pairs={{0,128},{128,256},{256,384},{384,0},{1,129},{129,257},{257,385},{3... | collective-permute-start | bytes 1179656 | tf_op jit(solution)/shard_map/ppermute | solution.py:177
  50.6 4.0 %collective-permute-start.7 = (bf16[8,32,768]{2,1,0:T(8,128)(2,1)S(1)}, bf16[8,32,768]{2,1,0:T(8,128)(2,1)S(1)}, u32[]{:S(2)}, u32[]{:S(2)}) collective-permute-start(bf16[8,32,768]{2,1,0:T(8,128)(2,1)S(1)} %collective-permute-done.3.xb), channel_id=1, source_target_pairs={{0,384},{128,0},{256,128},{384,256},{1,385},{129,1},{257,129},{385... | collective-permute-start | bytes 1179656 | tf_op jit(solution)/shard_map/ppermute | solution.py:177
  54.6 2.7 %constant_dynamic-slice_fusion.3 = bf16[512,1536]{1,0:T(8,128)(2,1)} fusion(bf16[512,3072]{1,0:T(8,128)(2,1)} %param.7, s32[]{:T(128)S(6)} %select_n.39), kind=kLoop, calls=%fused_computation.6 | loop fusion | bytes 3145732 | tf_op jit(solution)/shard_map/dynamic_slice | solution.py:182
  57.3 2.2 %collective-permute-start.11 = (bf16[512,1536]{1,0:T(8,128)(2,1)}, bf16[512,1536]{1,0:T(8,128)(2,1)}, u32[]{:S(2)}, u32[]{:S(2)}) collective-permute-start(bf16[512,1536]{1,0:T(8,128)(2,1)} %constant_dynamic-slice_fusion.3), channel_id=1, source_target_pairs={{0,8},{8,0},{1,9},{9,1},{2,10},{10,2},{3,11},{11,3},{4,12},{12,4},... | collective-permute-start | bytes 4718600 | tf_op jit(solution)/shard_map/ppermute | solution.py:31
  59.5 3.4 %collective-permute-start.8 = (bf16[8,32,768]{2,1,0:T(8,128)(2,1)S(1)}, bf16[8,32,768]{2,1,0:T(8,128)(2,1)S(1)}, u32[]{:S(2)}, u32[]{:S(2)}) collective-permute-start(bf16[8,32,768]{2,1,0:T(8,128)(2,1)S(1)} %broadcast_select_fusion.1), channel_id=1, source_target_pairs={{0,128},{4,388},{128,256},{132,4},{256,384},{260,132},{384,0},{388... | collective-permute-start | bytes 1179656 | tf_op jit(solution)/shard_map/ppermute | solution.py:178
  63.0 2.1 %collective-permute-start.9 = (bf16[8,32,768]{2,1,0:T(8,128)(2,1)S(1)}, bf16[8,32,768]{2,1,0:T(8,128)(2,1)S(1)}, u32[]{:S(2)}, u32[]{:S(2)}) collective-permute-start(bf16[8,32,768]{2,1,0:T(8,128)(2,1)S(1)} %broadcast_select_fusion), channel_id=1, source_target_pairs={{0,128},{4,388},{128,256},{132,4},{256,384},{260,132},{384,0},{388... | collective-permute-start | bytes 1179656 | tf_op jit(solution)/shard_map/ppermute | solution.py:179
  65.1 3.4 %collective-permute-done.8.oa = bf16[8,32,768]{2,1,0:T(8,128)(2,1)S(1)} collective-permute-done((bf16[8,32,768]{2,1,0:T(8,128)(2,1)S(1)}, bf16[8,32,768]{2,1,0:T(8,128)(2,1)S(1)}, u32[]{:S(2)}, u32[]{:S(2)}) %collective-permute-start.8) | collective-permute-done | bytes 393248 | tf_op jit(solution)/shard_map/ppermute | solution.py:178
  68.4 4.2 %collective-permute-done.9.ob = bf16[8,32,768]{2,1,0:T(8,128)(2,1)S(1)} collective-permute-done((bf16[8,32,768]{2,1,0:T(8,128)(2,1)S(1)}, bf16[8,32,768]{2,1,0:T(8,128)(2,1)S(1)}, u32[]{:S(2)}, u32[]{:S(2)}) %collective-permute-start.9) | collective-permute-done | bytes 393248 | tf_op jit(solution)/shard_map/ppermute | solution.py:179
  72.7 8.4 %all-gather.3.cloned.1.call-done = bf16[64,96,384]{2,1,0:T(8,128)(2,1)} async-done(((bf16[4,96,384]{2,1,0:T(8,128)(2,1)}), bf16[64,96,384]{2,1,0:T(8,128)(2,1)}) %all-gather.3.cloned.1.call-update) | async-done | bytes 4718608 | tf_op jit(solution)/shard_map/all_gather | solution.py:173
  81.0 7.1 %shard_map.47 = bf16[4,8,2,16,256]{4,3,2,1,0:T(8,128)(2,1)} custom-call(s32[3]{0:T(128)S(1)} %pad_add_fusion.place, bf16[8,32,768]{2,1,0:T(8,128)(2,1)S(1)} %bitcast.24, bf16[8,32,768]{2,1,0:T(8,128)(2,1)S(1)} %collective-permute-done.3.xb, bf16[8,32,768]{2,1,0:T(8,128)(2,1)S(1)} %collective-permute-done.4.la, ...), custom_call_target="tpu_custom_call" | custom-call | flops 3000000000 | bytes 9000000 | tf_op jit(solution)/shard_map/pallas_call | solution.py:140
  88.2 8.5 %all-to-all-start.1 = ((bf16[64,16,256]{2,1,0:T(8,128)(2,1)}), bf16[64,16,256]{2,1,0:T(8,128)(2,1)S(1)}, u32[]{:S(2)}, u32[]{:S(2)}) async-start(bf16[64,16,256]{2,1,0:T(8,128)(2,1)} %bitcast.12), calls=%async_computation.1 | async-start | bytes 1048576 | tf_op jit(solution)/shard_map/all_to_all | solution.py:205
  96.7 3.1 %constant_dynamic-slice_fusion.1 = (bf16[512,768]{1,0:T(8,128)(2,1)}, bf16[512,768]{1,0:T(8,128)(2,1)S(1)}) fusion(bf16[512,3072]{1,0:T(8,128)(2,1)} %param.7, s32[]{:T(128)S(6)} %dynamic_slice.25, s32[]{:T(128)S(6)} %dynamic_slice.21), kind=kLoop, calls=%fused_computation.4 | loop fusion | bytes 3145736 | tf_op jit(solution)/shard_map/dynamic_slice | solution.py:182
  99.8 2.4 %collective-permute-start.12 = (bf16[512,768]{1,0:T(8,128)(2,1)}, bf16[512,768]{1,0:T(8,128)(2,1)S(1)}, u32[]{:S(2)}, u32[]{:S(2)}) collective-permute-start(bf16[512,768]{1,0:T(8,128)(2,1)} %get-tuple-element.21), channel_id=1, source_target_pairs={{0,4},{4,0},{1,5},{5,1},{2,6},{6,2},{3,7},{7,3},{8,12},{12,8},{9,1... | collective-permute-start | bytes 2359304 | tf_op jit(solution)/shard_map/ppermute | solution.py:31
  102.3 2.4 %constant_dynamic-slice_fusion = (bf16[512,768]{1,0:T(8,128)(2,1)}, bf16[512,768]{1,0:T(8,128)(2,1)S(1)}) fusion(bf16[512,1536]{1,0:T(8,128)(2,1)} %collective-permute-done.11, s32[]{:T(128)S(6)} %select_n.40, s32[]{:T(128)S(6)} %select_n.35), kind=kLoop, calls=%fused_computation.3 | loop fusion | bytes 3145736 | tf_op jit(solution)/shard_map/dynamic_slice | solution.py:182
  104.7 1.9 %collective-permute-start.13 = (bf16[512,768]{1,0:T(8,128)(2,1)}, bf16[512,768]{1,0:T(8,128)(2,1)}, u32[]{:S(2)}, u32[]{:S(2)}) collective-permute-start(bf16[512,768]{1,0:T(8,128)(2,1)} %get-tuple-element.23), channel_id=1, source_target_pairs={{0,4},{4,0},{1,5},{5,1},{2,6},{6,2},{3,7},{7,3},{8,12},{12,8},{9,1... | collective-permute-start | bytes 2359304 | tf_op jit(solution)/shard_map/ppermute | solution.py:31
  106.6 6.0 %all-to-all-done.1 = bf16[64,16,256]{2,1,0:T(8,128)(2,1)S(1)} async-done(((bf16[64,16,256]{2,1,0:T(8,128)(2,1)}), bf16[64,16,256]{2,1,0:T(8,128)(2,1)S(1)}, u32[]{:S(2)}, u32[]{:S(2)}) %all-to-all-start.1) | async-done | bytes 524320 | tf_op jit(solution)/shard_map/all_to_all | solution.py:205
  112.7 4.7 %collective-permute-start.10 = (bf16[64,16,256]{2,1,0:T(8,128)(2,1)S(1)}, bf16[64,16,256]{2,1,0:T(8,128)(2,1)S(1)}, u32[]{:S(2)}, u32[]{:S(2)}) collective-permute-start(bf16[64,16,256]{2,1,0:T(8,128)(2,1)S(1)} %all-to-all-done.1), channel_id=1, source_target_pairs={{0,4},{4,0},{1,5},{5,1},{2,6},{6,2},{3,7},{7,3},{8,12},{12,8},{9,1... | collective-permute-start | bytes 1572872 | tf_op jit(solution)/shard_map/ppermute | solution.py:31
  117.4 1.5 %collective-permute-done.10 = bf16[64,16,256]{2,1,0:T(8,128)(2,1)S(1)} collective-permute-done((bf16[64,16,256]{2,1,0:T(8,128)(2,1)S(1)}, bf16[64,16,256]{2,1,0:T(8,128)(2,1)S(1)}, u32[]{:S(2)}, u32[]{:S(2)}) %collective-permute-start.10) | collective-permute-done | bytes 524320 | tf_op jit(solution)/shard_map/ppermute | solution.py:31
  118.9 2.9 %shard_map.48 = bf16[8,2,16,768]{3,2,1,0:T(8,128)(2,1)} custom-call(s32[3]{0:T(128)S(1)} %pad_add_fusion.place, bf16[4,8,2,16,256]{4,3,2,1,0:T(8,128)(2,1)S(1)} %bitcast.17, bf16[4,8,2,16,256]{4,3,2,1,0:T(8,128)(2,1)S(1)} %bitcast.20, bf16[512,768]{1,0:T(8,128)(2,1)S(1)} %get-tuple-element.22.wo00, bf16[512,768]{1,0:T(8,128)(2,1)S(1)} %get-tuple-element.24.wo10, ...), custom_call_target="tpu_custom_call" | custom-call | flops 800000000 | bytes 6000000 | tf_op jit(solution)/shard_map/pallas_call | solution.py:140
  (19 shorter events, 2.0 us)
Async XLA Ops:
  6.5 24.8 %all-to-all-start = ((bf16[16,16,768]{2,1,0:T(8,128)(2,1)}), bf16[16,16,768]{2,1,0:T(8,128)(2,1)S(1)}, u32[]{:S(2)}, u32[]{:S(2)}) async-start(bf16[16,16,768]{2,1,0:T(8,128)(2,1)} %bitcast.18), calls=%async_computation | async-start | bytes 786432 | tf_op jit(solution)/shard_map/all_to_all | solution.py:171
  16.8 64.3 %all-gather.3.cloned.1.call-start = ((), (), s32[]{:S(2)}) async-start(), calls=%async_computation.2 | async-start | bytes 5013504 | tf_op jit(solution)/shard_map/all_gather | solution.py:173
  16.9 1.0 copy-start.1
  18.5 7.8 %collective-permute-start.2 = (bf16[96,384]{1,0:T(8,128)(2,1)S(1)}, bf16[96,384]{1,0:T(8,128)(2,1)S(1)}, u32[]{:S(2)}, u32[]{:S(2)}) collective-permute-start(bf16[96,384]{1,0:T(8,128)(2,1)S(1)} %get-tuple-element.16), channel_id=1, source_target_pairs={{0,384},{128,0},{256,128},{384,256},{1,385},{129,1},{257,129},{385... | collective-permute-start | bytes 221192 | tf_op jit(solution)/shard_map/ppermute | solution.py:167
  21.3 6.6 %collective-permute-start.1 = (bf16[96,384]{1,0:T(8,128)(2,1)S(1)}, bf16[96,384]{1,0:T(8,128)(2,1)S(1)}, u32[]{:S(2)}, u32[]{:S(2)}) collective-permute-start(bf16[96,384]{1,0:T(8,128)(2,1)S(1)} %get-tuple-element.15), channel_id=1, source_target_pairs={{0,256},{128,384},{256,0},{384,128},{1,257},{129,385},{257,1},{385... | collective-permute-start | bytes 221192 | tf_op jit(solution)/shard_map/ppermute | solution.py:167
  23.7 6.4 %collective-permute-start = (bf16[96,384]{1,0:T(8,128)(2,1)S(1)}, bf16[96,384]{1,0:T(8,128)(2,1)S(1)}, u32[]{:S(2)}, u32[]{:S(2)}) collective-permute-start(bf16[96,384]{1,0:T(8,128)(2,1)S(1)} %get-tuple-element.14), channel_id=1, source_target_pairs={{0,128},{128,256},{256,384},{384,0},{1,129},{129,257},{257,385},{3... | collective-permute-start | bytes 221192 | tf_op jit(solution)/shard_map/ppermute | solution.py:167
  30.1 50.9 %copy-start.2 = (f32[3072]{0:T(1024)S(1)}, f32[3072]{0:T(1024)}, u32[]{:S(2)}) copy-start(f32[3072]{0:T(1024)} %param.5) | copy-start | bytes 36868
  31.3 11.1 %collective-permute-start.3 = (bf16[8,32,768]{2,1,0:T(8,128)(2,1)S(1)}, bf16[8,32,768]{2,1,0:T(8,128)(2,1)S(1)}, u32[]{:S(2)}, u32[]{:S(2)}) collective-permute-start(bf16[8,32,768]{2,1,0:T(8,128)(2,1)S(1)} %bitcast.21), channel_id=1, source_target_pairs={{0,8},{8,0},{1,9},{9,1},{2,10},{10,2},{3,11},{11,3},{4,12},{12,4},... | collective-permute-start | bytes 1179656 | tf_op jit(solution)/shard_map/ppermute | solution.py:31
  34.8 11.6 %collective-permute-start.4 = (bf16[8,32,768]{2,1,0:T(8,128)(2,1)S(1)}, bf16[8,32,768]{2,1,0:T(8,128)(2,1)S(1)}, u32[]{:S(2)}, u32[]{:S(2)}) collective-permute-start(bf16[8,32,768]{2,1,0:T(8,128)(2,1)S(1)} %bitcast.22), channel_id=1, source_target_pairs={{0,128},{128,256},{256,384},{384,0},{1,129},{129,257},{257,385},{3... | collective-permute-start | bytes 1179656 | tf_op jit(solution)/shard_map/ppermute | solution.py:175
  36.9 10.5 %collective-permute-start.5 = (bf16[8,32,768]{2,1,0:T(8,128)(2,1)S(1)}, bf16[8,32,768]{2,1,0:T(8,128)(2,1)S(1)}, u32[]{:S(2)}, u32[]{:S(2)}) collective-permute-start(bf16[8,32,768]{2,1,0:T(8,128)(2,1)S(1)} %bitcast.23), channel_id=1, source_target_pairs={{0,384},{128,0},{256,128},{384,256},{1,385},{129,1},{257,129},{385... | collective-permute-start | bytes 1179656 | tf_op jit(solution)/shard_map/ppermute | solution.py:175
  47.4 15.5 %collective-permute-start.6 = (bf16[8,32,768]{2,1,0:T(8,128)(2,1)S(1)}, bf16[8,32,768]{2,1,0:T(8,128)(2,1)S(1)}, u32[]{:S(2)}, u32[]{:S(2)}) collective-permute-start(bf16[8,32,768]{2,1,0:T(8,128)(2,1)S(1)} %collective-permute-done.3.xb), channel_id=1, source_target_pairs={{0,128},{128,256},{256,384},{384,0},{1,129},{129,257},{257,385},{3... | collective-permute-start | bytes 1179656 | tf_op jit(solution)/shard_map/ppermute | solution.py:177
  50.6 12.4 %collective-permute-start.7 = (bf16[8,32,768]{2,1,0:T(8,128)(2,1)S(1)}, bf16[8,32,768]{2,1,0:T(8,128)(2,1)S(1)}, u32[]{:S(2)}, u32[]{:S(2)}) collective-permute-start(bf16[8,32,768]{2,1,0:T(8,128)(2,1)S(1)} %collective-permute-done.3.xb), channel_id=1, source_target_pairs={{0,384},{128,0},{256,128},{384,256},{1,385},{129,1},{257,129},{385... | collective-permute-start | bytes 1179656 | tf_op jit(solution)/shard_map/ppermute | solution.py:177
  57.3 45.0 %collective-permute-start.11 = (bf16[512,1536]{1,0:T(8,128)(2,1)}, bf16[512,1536]{1,0:T(8,128)(2,1)}, u32[]{:S(2)}, u32[]{:S(2)}) collective-permute-start(bf16[512,1536]{1,0:T(8,128)(2,1)} %constant_dynamic-slice_fusion.3), channel_id=1, source_target_pairs={{0,8},{8,0},{1,9},{9,1},{2,10},{10,2},{3,11},{11,3},{4,12},{12,4},... | collective-permute-start | bytes 4718600 | tf_op jit(solution)/shard_map/ppermute | solution.py:31
  59.5 8.9 %collective-permute-start.8 = (bf16[8,32,768]{2,1,0:T(8,128)(2,1)S(1)}, bf16[8,32,768]{2,1,0:T(8,128)(2,1)S(1)}, u32[]{:S(2)}, u32[]{:S(2)}) collective-permute-start(bf16[8,32,768]{2,1,0:T(8,128)(2,1)S(1)} %broadcast_select_fusion.1), channel_id=1, source_target_pairs={{0,128},{4,388},{128,256},{132,4},{256,384},{260,132},{384,0},{388... | collective-permute-start | bytes 1179656 | tf_op jit(solution)/shard_map/ppermute | solution.py:178
  63.0 9.7 %collective-permute-start.9 = (bf16[8,32,768]{2,1,0:T(8,128)(2,1)S(1)}, bf16[8,32,768]{2,1,0:T(8,128)(2,1)S(1)}, u32[]{:S(2)}, u32[]{:S(2)}) collective-permute-start(bf16[8,32,768]{2,1,0:T(8,128)(2,1)S(1)} %broadcast_select_fusion), channel_id=1, source_target_pairs={{0,128},{4,388},{128,256},{132,4},{256,384},{260,132},{384,0},{388... | collective-permute-start | bytes 1179656 | tf_op jit(solution)/shard_map/ppermute | solution.py:179
  88.2 24.5 %all-to-all-start.1 = ((bf16[64,16,256]{2,1,0:T(8,128)(2,1)}), bf16[64,16,256]{2,1,0:T(8,128)(2,1)S(1)}, u32[]{:S(2)}, u32[]{:S(2)}) async-start(bf16[64,16,256]{2,1,0:T(8,128)(2,1)} %bitcast.12), calls=%async_computation.1 | async-start | bytes 1048576 | tf_op jit(solution)/shard_map/all_to_all | solution.py:205
  96.7 22.2 %copy-start = (bf16[1,1,256,768]{3,2,1,0:T(8,128)(2,1)S(1)}, bf16[1,1,256,768]{3,2,1,0:T(8,128)(2,1)}, u32[]{:S(2)}) copy-start(bf16[1,1,256,768]{3,2,1,0:T(8,128)(2,1)} %param.4) | copy-start | bytes 1179652
  99.8 17.5 %collective-permute-start.12 = (bf16[512,768]{1,0:T(8,128)(2,1)}, bf16[512,768]{1,0:T(8,128)(2,1)S(1)}, u32[]{:S(2)}, u32[]{:S(2)}) collective-permute-start(bf16[512,768]{1,0:T(8,128)(2,1)} %get-tuple-element.21), channel_id=1, source_target_pairs={{0,4},{4,0},{1,5},{5,1},{2,6},{6,2},{3,7},{7,3},{8,12},{12,8},{9,1... | collective-permute-start | bytes 2359304 | tf_op jit(solution)/shard_map/ppermute | solution.py:31
  104.7 12.6 %collective-permute-start.13 = (bf16[512,768]{1,0:T(8,128)(2,1)}, bf16[512,768]{1,0:T(8,128)(2,1)}, u32[]{:S(2)}, u32[]{:S(2)}) collective-permute-start(bf16[512,768]{1,0:T(8,128)(2,1)} %get-tuple-element.23), channel_id=1, source_target_pairs={{0,4},{4,0},{1,5},{5,1},{2,6},{6,2},{3,7},{7,3},{8,12},{12,8},{9,1... | collective-permute-start | bytes 2359304 | tf_op jit(solution)/shard_map/ppermute | solution.py:31
  112.7 6.2 %collective-permute-start.10 = (bf16[64,16,256]{2,1,0:T(8,128)(2,1)S(1)}, bf16[64,16,256]{2,1,0:T(8,128)(2,1)S(1)}, u32[]{:S(2)}, u32[]{:S(2)}) collective-permute-start(bf16[64,16,256]{2,1,0:T(8,128)(2,1)S(1)} %all-to-all-done.1), channel_id=1, source_target_pairs={{0,4},{4,0},{1,5},{5,1},{2,6},{6,2},{3,7},{7,3},{8,12},{12,8},{9,1... | collective-permute-start | bytes 1572872 | tf_op jit(solution)/shard_map/ppermute | solution.py:31
Sparse Core Ops, SparseCore 0:
  31.5 49.5 all-gather.2

commit v7 on v4

--- a/solution.py
+++ b/solution.py
@@ -173,7 +173,8 @@
     w_rows = lax.all_gather(w_rows, ("c", "y"), axis=1, tiled=True)
     xb = swap(xa, "z")
     la, ra = (lax.ppermute(xa, "x", ring(4, shift)) for shift in (1, 3))
-    xb_late = after(xb, la, ra)
+    wo_give = lax.dynamic_slice_in_dim(after(w_out, xb), (1 - z) * 2 * QUARTER, 2 * QUARTER, axis=1)
+    xb_late, wo_give = lax.optimization_barrier((xb, wo_give, la, ra))[:2]
     lb, rb = (lax.ppermute(xb_late, "x", ring(4, shift)) for shift in (1, 3))
     oa = lax.ppermute(jnp.where(c == 0, la, ra), ("x", "c"), across())
     ob = lax.ppermute(jnp.where(c == 0, lb, rb), ("x", "c"), across())
@@ -182,7 +183,7 @@
         return lax.dynamic_slice_in_dim(value, index * size, size, axis=1)
 
     wo_keep = half(w_out, z, 2 * QUARTER)
-    wo_got = swap(half(after(w_out, xb), 1 - z, 2 * QUARTER), "z")
+    wo_got = swap(wo_give, "z")
     wo00, wo10 = half(wo_keep, c, QUARTER), half(wo_got, c, QUARTER)
     wo01, wo11 = swap(half(wo_keep, 1 - c, QUARTER), "c"), swap(half(wo_got, 1 - c, QUARTER), "c")
 

time: 130 us -> 130 us (level)
  waiting for transfers between devices: 34 us -> 31.2 us
  starting transfers between devices: 60.2 us -> 62.9 us
    dynamic_slice x3 -> x2, local copies, waits for them, and re-layouts: 8.23 us -> 5.55 us  [half(): return lax.dynamic_slice_in_dim(value, index * size, size, axis=1)]
    ppermute x2, waiting for transfers between devices: 4.97 us -> 2.31 us  [body(): la, ra = (lax.ppermute(xa, 'x', ring(4, shift)) for shift in (1, 3))]
    dynamic_slice x0 -> x1, local copies, waits for them, and re-layouts: none -> 2.66 us  [body(): lax.dynamic_slice_in_dim(after(w_out, xb), (1 - z) * 2 * QUARTER, 2 * QUA...]
    ppermute x1, starting transfers between devices: 2.12 us -> 4.77 us  [body(): ob = lax.ppermute(jnp.where(c == 0, lb, rb), ('x', 'c'), across())]
where the time goes in v7:
time: 130 us; the launch traced here: 129 us
  starting transfers between devices  62.9 us (48%)
  waiting for transfers between devices  31.2 us (24%)
  between operations  13.6 us (10%)
  Pallas kernels  11.1 us (9%)
  local copies, waits for them, and re-layouts  9.19 us (7%)
    ppermute x5, starting transfers between devices, swap(): return lax.ppermute(value, axis, [(0, 1), (1, 0)])  14.7 us
    pallas_call x3, Pallas kernels, kernel_call(): pl.pallas_call(kernel, out_shape=shapes, in_specs=[SMEM if value.dtype ==...  11.1 us
    all_to_all x1, starting transfers between devices, body(): lax.all_to_all(tokens, ('y', 'c'), 0, 0, tiled=True).reshape(8, 32, QUARTER)  10.2 us
    all_gather x1, waiting for transfers between devices, body(): w_rows = lax.all_gather(w_rows, ('c', 'y'), axis=1, tiled=True)  8.95 us
    all_to_all x1, starting transfers between devices, body(): lax.all_to_all(attended.reshape(64, 16, 2 * HD), ('x', 'y', 'z'), 0, 0, t...  8.43 us
    ppermute x3, starting transfers between devices, body(): lax.ppermute(slots[k], 'x', ring(4, k))  7.75 us
    ppermute x2, starting transfers between devices, body(): lb, rb = (lax.ppermute(xb_late, 'x', ring(4, shift)) for shift in (1, 3))  7.18 us
    ppermute x2, starting transfers between devices, body(): la, ra = (lax.ppermute(xa, 'x', ring(4, shift)) for shift in (1, 3))  6.49 us
  transfers between devices with their start and end apart: 17, of which 11 were waited for; matrix products, arithmetic and copies ran while one was open for 7% of the time, Pallas kernels for 6%

profile of v7, /device:TPU:1, one launch (start us, length us, event | category | flops | bytes accessed | tf_op | source)
XLA Modules:
  0.0 129.1 jit_solution(1057171703395295412)
XLA Ops:
  6.5 10.2 %all-to-all-start = ((bf16[16,16,768]{2,1,0:T(8,128)(2,1)}), bf16[16,16,768]{2,1,0:T(8,128)(2,1)S(1)}, u32[]{:S(2)}, u32[]{:S(2)}) async-start(bf16[16,16,768]{2,1,0:T(8,128)(2,1)} %bitcast.17), calls=%async_computation | async-start | bytes 786432 | tf_op jit(solution)/shard_map/all_to_all | solution.py:171
  16.9 1.0 copy-done.1
  18.5 2.8 %collective-permute-start.2 = (bf16[96,384]{1,0:T(8,128)(2,1)S(1)}, bf16[96,384]{1,0:T(8,128)(2,1)S(1)}, u32[]{:S(2)}, u32[]{:S(2)}) collective-permute-start(bf16[96,384]{1,0:T(8,128)(2,1)S(1)} %get-tuple-element.17), channel_id=1, source_target_pairs={{0,384},{128,0},{256,128},{384,256},{1,385},{129,1},{257,129},{385... | collective-permute-start | bytes 221192 | tf_op jit(solution)/shard_map/ppermute | solution.py:167
  21.3 2.4 %collective-permute-start.1 = (bf16[96,384]{1,0:T(8,128)(2,1)S(1)}, bf16[96,384]{1,0:T(8,128)(2,1)S(1)}, u32[]{:S(2)}, u32[]{:S(2)}) collective-permute-start(bf16[96,384]{1,0:T(8,128)(2,1)S(1)} %get-tuple-element.16), channel_id=1, source_target_pairs={{0,256},{128,384},{256,0},{384,128},{1,257},{129,385},{257,1},{385... | collective-permute-start | bytes 221192 | tf_op jit(solution)/shard_map/ppermute | solution.py:167
  23.7 2.5 %collective-permute-start = (bf16[96,384]{1,0:T(8,128)(2,1)S(1)}, bf16[96,384]{1,0:T(8,128)(2,1)S(1)}, u32[]{:S(2)}, u32[]{:S(2)}) collective-permute-start(bf16[96,384]{1,0:T(8,128)(2,1)S(1)} %get-tuple-element.15), channel_id=1, source_target_pairs={{0,128},{128,256},{256,384},{384,0},{1,129},{129,257},{257,385},{3... | collective-permute-start | bytes 221192 | tf_op jit(solution)/shard_map/ppermute | solution.py:167
  26.2 1.6 %collective-permute-done.1 = bf16[96,384]{1,0:T(8,128)(2,1)S(1)} collective-permute-done((bf16[96,384]{1,0:T(8,128)(2,1)S(1)}, bf16[96,384]{1,0:T(8,128)(2,1)S(1)}, u32[]{:S(2)}, u32[]{:S(2)}) %collective-permute-start.1) | collective-permute-done | bytes 73760 | tf_op jit(solution)/shard_map/ppermute | solution.py:167
  27.9 2.2 %collective-permute-done = bf16[96,384]{1,0:T(8,128)(2,1)S(1)} collective-permute-done((bf16[96,384]{1,0:T(8,128)(2,1)S(1)}, bf16[96,384]{1,0:T(8,128)(2,1)S(1)}, u32[]{:S(2)}, u32[]{:S(2)}) %collective-permute-start) | collective-permute-done | bytes 73760 | tf_op jit(solution)/shard_map/ppermute | solution.py:167
  31.3 3.5 %collective-permute-start.3 = (bf16[8,32,768]{2,1,0:T(8,128)(2,1)S(1)}, bf16[8,32,768]{2,1,0:T(8,128)(2,1)S(1)}, u32[]{:S(2)}, u32[]{:S(2)}) collective-permute-start(bf16[8,32,768]{2,1,0:T(8,128)(2,1)S(1)} %bitcast.20), channel_id=1, source_target_pairs={{0,8},{8,0},{1,9},{9,1},{2,10},{10,2},{3,11},{11,3},{4,12},{12,4},... | collective-permute-start | bytes 1179656 | tf_op jit(solution)/shard_map/ppermute | solution.py:31
  34.8 2.0 %collective-permute-start.4 = (bf16[8,32,768]{2,1,0:T(8,128)(2,1)S(1)}, bf16[8,32,768]{2,1,0:T(8,128)(2,1)S(1)}, u32[]{:S(2)}, u32[]{:S(2)}) collective-permute-start(bf16[8,32,768]{2,1,0:T(8,128)(2,1)S(1)} %bitcast.21), channel_id=1, source_target_pairs={{0,128},{128,256},{256,384},{384,0},{1,129},{129,257},{257,385},{3... | collective-permute-start | bytes 1179656 | tf_op jit(solution)/shard_map/ppermute | solution.py:175
  36.9 4.5 %collective-permute-start.5 = (bf16[8,32,768]{2,1,0:T(8,128)(2,1)S(1)}, bf16[8,32,768]{2,1,0:T(8,128)(2,1)S(1)}, u32[]{:S(2)}, u32[]{:S(2)}) collective-permute-start(bf16[8,32,768]{2,1,0:T(8,128)(2,1)S(1)} %bitcast.22), channel_id=1, source_target_pairs={{0,384},{128,0},{256,128},{384,256},{1,385},{129,1},{257,129},{385... | collective-permute-start | bytes 1179656 | tf_op jit(solution)/shard_map/ppermute | solution.py:175
  41.3 1.1 collective-permute-done.3.xb
  42.4 2.7 %constant_dynamic-slice_fusion.4 = bf16[512,1536]{1,0:T(8,128)(2,1)} fusion(bf16[512,3072]{1,0:T(8,128)(2,1)} %param.7, s32[]{:T(128)S(6)} %select_n.32), kind=kLoop, calls=%fused_computation.7 | loop fusion | bytes 3145732 | tf_op jit(solution)/shard_map/dynamic_slice | solution.py:176
  45.1 1.4 %collective-permute-done.4.la = bf16[8,32,768]{2,1,0:T(8,128)(2,1)S(1)} collective-permute-done((bf16[8,32,768]{2,1,0:T(8,128)(2,1)S(1)}, bf16[8,32,768]{2,1,0:T(8,128)(2,1)S(1)}, u32[]{:S(2)}, u32[]{:S(2)}) %collective-permute-start.4) | collective-permute-done | bytes 393248 | tf_op jit(solution)/shard_map/ppermute | solution.py:175
  46.5 0.9 collective-permute-done.5.ra
  47.4 3.1 %collective-permute-start.6 = (bf16[8,32,768]{2,1,0:T(8,128)(2,1)S(1)}, bf16[8,32,768]{2,1,0:T(8,128)(2,1)S(1)}, u32[]{:S(2)}, u32[]{:S(2)}) collective-permute-start(bf16[8,32,768]{2,1,0:T(8,128)(2,1)S(1)} %collective-permute-done.3.xb), channel_id=1, source_target_pairs={{0,128},{128,256},{256,384},{384,0},{1,129},{129,257},{257,385},{3... | collective-permute-start | bytes 1179656 | tf_op jit(solution)/shard_map/ppermute | solution.py:178
  50.6 4.0 %collective-permute-start.7 = (bf16[8,32,768]{2,1,0:T(8,128)(2,1)S(1)}, bf16[8,32,768]{2,1,0:T(8,128)(2,1)S(1)}, u32[]{:S(2)}, u32[]{:S(2)}) collective-permute-start(bf16[8,32,768]{2,1,0:T(8,128)(2,1)S(1)} %collective-permute-done.3.xb), channel_id=1, source_target_pairs={{0,384},{128,0},{256,128},{384,256},{1,385},{129,1},{257,129},{385... | collective-permute-start | bytes 1179656 | tf_op jit(solution)/shard_map/ppermute | solution.py:178
  54.6 2.2 %collective-permute-start.11 = (bf16[512,1536]{1,0:T(8,128)(2,1)}, bf16[512,1536]{1,0:T(8,128)(2,1)}, u32[]{:S(2)}, u32[]{:S(2)}) collective-permute-start(bf16[512,1536]{1,0:T(8,128)(2,1)} %constant_dynamic-slice_fusion.4), channel_id=1, source_target_pairs={{0,8},{8,0},{1,9},{9,1},{2,10},{10,2},{3,11},{11,3},{4,12},{12,4},... | collective-permute-start | bytes 4718600 | tf_op jit(solution)/shard_map/ppermute | solution.py:31
  56.9 3.4 %collective-permute-start.8 = (bf16[8,32,768]{2,1,0:T(8,128)(2,1)S(1)}, bf16[8,32,768]{2,1,0:T(8,128)(2,1)S(1)}, u32[]{:S(2)}, u32[]{:S(2)}) collective-permute-start(bf16[8,32,768]{2,1,0:T(8,128)(2,1)S(1)} %broadcast_select_fusion.1), channel_id=1, source_target_pairs={{0,128},{4,388},{128,256},{132,4},{256,384},{260,132},{384,0},{388... | collective-permute-start | bytes 1179656 | tf_op jit(solution)/shard_map/ppermute | solution.py:179
  60.3 4.8 %collective-permute-start.9 = (bf16[8,32,768]{2,1,0:T(8,128)(2,1)S(1)}, bf16[8,32,768]{2,1,0:T(8,128)(2,1)S(1)}, u32[]{:S(2)}, u32[]{:S(2)}) collective-permute-start(bf16[8,32,768]{2,1,0:T(8,128)(2,1)S(1)} %broadcast_select_fusion), channel_id=1, source_target_pairs={{0,128},{4,388},{128,256},{132,4},{256,384},{260,132},{384,0},{388... | collective-permute-start | bytes 1179656 | tf_op jit(solution)/shard_map/ppermute | solution.py:180
  65.1 2.8 %collective-permute-done.8.oa = bf16[8,32,768]{2,1,0:T(8,128)(2,1)S(1)} collective-permute-done((bf16[8,32,768]{2,1,0:T(8,128)(2,1)S(1)}, bf16[8,32,768]{2,1,0:T(8,128)(2,1)S(1)}, u32[]{:S(2)}, u32[]{:S(2)}) %collective-permute-start.8) | collective-permute-done | bytes 393248 | tf_op jit(solution)/shard_map/ppermute | solution.py:179
  67.9 4.2 %collective-permute-done.9.ob = bf16[8,32,768]{2,1,0:T(8,128)(2,1)S(1)} collective-permute-done((bf16[8,32,768]{2,1,0:T(8,128)(2,1)S(1)}, bf16[8,32,768]{2,1,0:T(8,128)(2,1)S(1)}, u32[]{:S(2)}, u32[]{:S(2)}) %collective-permute-start.9) | collective-permute-done | bytes 393248 | tf_op jit(solution)/shard_map/ppermute | solution.py:180
  72.1 8.9 %all-gather.2.cloned.1.call-done.w_hbm = bf16[4,1536,384]{2,1,0:T(8,128)(2,1)} async-done(((bf16[4,96,384]{2,1,0:T(8,128)(2,1)}), bf16[4,1536,384]{2,1,0:T(8,128)(2,1)}) %all-gather.2.cloned.1.call-update) | async-done | bytes 4718608 | tf_op jit(solution)/shard_map/all_gather | solution.py:173
  81.1 7.6 %shard_map.47 = bf16[4,8,2,16,256]{4,3,2,1,0:T(8,128)(2,1)} custom-call(s32[3]{0:T(128)S(1)} %pad_add_fusion.place, bf16[8,32,768]{2,1,0:T(8,128)(2,1)S(1)} %bitcast.23, bf16[8,32,768]{2,1,0:T(8,128)(2,1)S(1)} %collective-permute-done.3.xb, bf16[8,32,768]{2,1,0:T(8,128)(2,1)S(1)} %collective-permute-done.4.la, ...), custom_call_target="tpu_custom_call" | custom-call | flops 3000000000 | bytes 9000000 | tf_op jit(solution)/shard_map/pallas_call | solution.py:140
  88.7 8.4 %all-to-all-start.1 = ((bf16[64,16,256]{2,1,0:T(8,128)(2,1)}), bf16[64,16,256]{2,1,0:T(8,128)(2,1)S(1)}, u32[]{:S(2)}, u32[]{:S(2)}) async-start(bf16[64,16,256]{2,1,0:T(8,128)(2,1)} %bitcast.11), calls=%async_computation.1 | async-start | bytes 1048576 | tf_op jit(solution)/shard_map/all_to_all | solution.py:206
  97.1 3.1 %constant_dynamic-slice_fusion.1 = (bf16[512,768]{1,0:T(8,128)(2,1)}, bf16[512,768]{1,0:T(8,128)(2,1)S(1)}) fusion(bf16[512,3072]{1,0:T(8,128)(2,1)} %param.7, s32[]{:T(128)S(6)} %dynamic_slice.25, s32[]{:T(128)S(6)} %dynamic_slice.22), kind=kLoop, calls=%fused_computation.4 | loop fusion | bytes 3145736 | tf_op jit(solution)/shard_map/dynamic_slice | solution.py:183
  100.3 2.4 %collective-permute-start.12 = (bf16[512,768]{1,0:T(8,128)(2,1)}, bf16[512,768]{1,0:T(8,128)(2,1)S(1)}, u32[]{:S(2)}, u32[]{:S(2)}) collective-permute-start(bf16[512,768]{1,0:T(8,128)(2,1)} %get-tuple-element.23), channel_id=1, source_target_pairs={{0,4},{4,0},{1,5},{5,1},{2,6},{6,2},{3,7},{7,3},{8,12},{12,8},{9,1... | collective-permute-start | bytes 2359304 | tf_op jit(solution)/shard_map/ppermute | solution.py:31
  102.7 2.4 %constant_dynamic-slice_fusion = (bf16[512,768]{1,0:T(8,128)(2,1)}, bf16[512,768]{1,0:T(8,128)(2,1)S(1)}) fusion(bf16[512,1536]{1,0:T(8,128)(2,1)} %collective-permute-done.11, s32[]{:T(128)S(6)} %select_n.40, s32[]{:T(128)S(6)} %select_n.36), kind=kLoop, calls=%fused_computation.3 | loop fusion | bytes 3145736 | tf_op jit(solution)/shard_map/dynamic_slice | solution.py:183
  105.2 1.9 %collective-permute-start.13 = (bf16[512,768]{1,0:T(8,128)(2,1)}, bf16[512,768]{1,0:T(8,128)(2,1)}, u32[]{:S(2)}, u32[]{:S(2)}) collective-permute-start(bf16[512,768]{1,0:T(8,128)(2,1)} %get-tuple-element.25), channel_id=1, source_target_pairs={{0,4},{4,0},{1,5},{5,1},{2,6},{6,2},{3,7},{7,3},{8,12},{12,8},{9,1... | collective-permute-start | bytes 2359304 | tf_op jit(solution)/shard_map/ppermute | solution.py:31
  107.1 6.0 %all-to-all-done.1 = bf16[64,16,256]{2,1,0:T(8,128)(2,1)S(1)} async-done(((bf16[64,16,256]{2,1,0:T(8,128)(2,1)}), bf16[64,16,256]{2,1,0:T(8,128)(2,1)S(1)}, u32[]{:S(2)}, u32[]{:S(2)}) %all-to-all-start.1) | async-done | bytes 524320 | tf_op jit(solution)/shard_map/all_to_all | solution.py:206
  113.1 4.7 %collective-permute-start.10 = (bf16[64,16,256]{2,1,0:T(8,128)(2,1)S(1)}, bf16[64,16,256]{2,1,0:T(8,128)(2,1)S(1)}, u32[]{:S(2)}, u32[]{:S(2)}) collective-permute-start(bf16[64,16,256]{2,1,0:T(8,128)(2,1)S(1)} %all-to-all-done.1), channel_id=1, source_target_pairs={{0,4},{4,0},{1,5},{5,1},{2,6},{6,2},{3,7},{7,3},{8,12},{12,8},{9,1... | collective-permute-start | bytes 1572872 | tf_op jit(solution)/shard_map/ppermute | solution.py:31
  117.8 1.5 %collective-permute-done.10 = bf16[64,16,256]{2,1,0:T(8,128)(2,1)S(1)} collective-permute-done((bf16[64,16,256]{2,1,0:T(8,128)(2,1)S(1)}, bf16[64,16,256]{2,1,0:T(8,128)(2,1)S(1)}, u32[]{:S(2)}, u32[]{:S(2)}) %collective-permute-start.10) | collective-permute-done | bytes 524320 | tf_op jit(solution)/shard_map/ppermute | solution.py:31
  119.3 2.9 %shard_map.48 = bf16[8,2,16,768]{3,2,1,0:T(8,128)(2,1)} custom-call(s32[3]{0:T(128)S(1)} %pad_add_fusion.place, bf16[4,8,2,16,256]{4,3,2,1,0:T(8,128)(2,1)S(1)} %bitcast.16, bf16[4,8,2,16,256]{4,3,2,1,0:T(8,128)(2,1)S(1)} %bitcast.19, bf16[512,768]{1,0:T(8,128)(2,1)S(1)} %get-tuple-element.24.wo00, bf16[512,768]{1,0:T(8,128)(2,1)S(1)} %get-tuple-element.26.wo10, ...), custom_call_target="tpu_custom_call" | custom-call | flops 800000000 | bytes 6000000 | tf_op jit(solution)/shard_map/pallas_call | solution.py:140
  (19 shorter events, 2.0 us)
Async XLA Ops:
  6.5 24.8 %all-to-all-start = ((bf16[16,16,768]{2,1,0:T(8,128)(2,1)}), bf16[16,16,768]{2,1,0:T(8,128)(2,1)S(1)}, u32[]{:S(2)}, u32[]{:S(2)}) async-start(bf16[16,16,768]{2,1,0:T(8,128)(2,1)} %bitcast.17), calls=%async_computation | async-start | bytes 786432 | tf_op jit(solution)/shard_map/all_to_all | solution.py:171
  16.8 64.3 %all-gather.2.cloned.1.call-start = ((), (), s32[]{:S(2)}) async-start(), calls=%async_computation.2 | async-start | bytes 5013504 | tf_op jit(solution)/shard_map/all_gather | solution.py:173
  16.9 1.0 copy-start.1
  18.5 7.8 %collective-permute-start.2 = (bf16[96,384]{1,0:T(8,128)(2,1)S(1)}, bf16[96,384]{1,0:T(8,128)(2,1)S(1)}, u32[]{:S(2)}, u32[]{:S(2)}) collective-permute-start(bf16[96,384]{1,0:T(8,128)(2,1)S(1)} %get-tuple-element.17), channel_id=1, source_target_pairs={{0,384},{128,0},{256,128},{384,256},{1,385},{129,1},{257,129},{385... | collective-permute-start | bytes 221192 | tf_op jit(solution)/shard_map/ppermute | solution.py:167
  21.3 6.6 %collective-permute-start.1 = (bf16[96,384]{1,0:T(8,128)(2,1)S(1)}, bf16[96,384]{1,0:T(8,128)(2,1)S(1)}, u32[]{:S(2)}, u32[]{:S(2)}) collective-permute-start(bf16[96,384]{1,0:T(8,128)(2,1)S(1)} %get-tuple-element.16), channel_id=1, source_target_pairs={{0,256},{128,384},{256,0},{384,128},{1,257},{129,385},{257,1},{385... | collective-permute-start | bytes 221192 | tf_op jit(solution)/shard_map/ppermute | solution.py:167
  23.7 6.4 %collective-permute-start = (bf16[96,384]{1,0:T(8,128)(2,1)S(1)}, bf16[96,384]{1,0:T(8,128)(2,1)S(1)}, u32[]{:S(2)}, u32[]{:S(2)}) collective-permute-start(bf16[96,384]{1,0:T(8,128)(2,1)S(1)} %get-tuple-element.15), channel_id=1, source_target_pairs={{0,128},{128,256},{256,384},{384,0},{1,129},{129,257},{257,385},{3... | collective-permute-start | bytes 221192 | tf_op jit(solution)/shard_map/ppermute | solution.py:167
  30.1 50.9 %copy-start.2 = (f32[3072]{0:T(1024)S(1)}, f32[3072]{0:T(1024)}, u32[]{:S(2)}) copy-start(f32[3072]{0:T(1024)} %param.5) | copy-start | bytes 36868
  31.3 11.1 %collective-permute-start.3 = (bf16[8,32,768]{2,1,0:T(8,128)(2,1)S(1)}, bf16[8,32,768]{2,1,0:T(8,128)(2,1)S(1)}, u32[]{:S(2)}, u32[]{:S(2)}) collective-permute-start(bf16[8,32,768]{2,1,0:T(8,128)(2,1)S(1)} %bitcast.20), channel_id=1, source_target_pairs={{0,8},{8,0},{1,9},{9,1},{2,10},{10,2},{3,11},{11,3},{4,12},{12,4},... | collective-permute-start | bytes 1179656 | tf_op jit(solution)/shard_map/ppermute | solution.py:31
  34.8 11.6 %collective-permute-start.4 = (bf16[8,32,768]{2,1,0:T(8,128)(2,1)S(1)}, bf16[8,32,768]{2,1,0:T(8,128)(2,1)S(1)}, u32[]{:S(2)}, u32[]{:S(2)}) collective-permute-start(bf16[8,32,768]{2,1,0:T(8,128)(2,1)S(1)} %bitcast.21), channel_id=1, source_target_pairs={{0,128},{128,256},{256,384},{384,0},{1,129},{129,257},{257,385},{3... | collective-permute-start | bytes 1179656 | tf_op jit(solution)/shard_map/ppermute | solution.py:175
  36.9 10.5 %collective-permute-start.5 = (bf16[8,32,768]{2,1,0:T(8,128)(2,1)S(1)}, bf16[8,32,768]{2,1,0:T(8,128)(2,1)S(1)}, u32[]{:S(2)}, u32[]{:S(2)}) collective-permute-start(bf16[8,32,768]{2,1,0:T(8,128)(2,1)S(1)} %bitcast.22), channel_id=1, source_target_pairs={{0,384},{128,0},{256,128},{384,256},{1,385},{129,1},{257,129},{385... | collective-permute-start | bytes 1179656 | tf_op jit(solution)/shard_map/ppermute | solution.py:175
  47.4 12.8 %collective-permute-start.6 = (bf16[8,32,768]{2,1,0:T(8,128)(2,1)S(1)}, bf16[8,32,768]{2,1,0:T(8,128)(2,1)S(1)}, u32[]{:S(2)}, u32[]{:S(2)}) collective-permute-start(bf16[8,32,768]{2,1,0:T(8,128)(2,1)S(1)} %collective-permute-done.3.xb), channel_id=1, source_target_pairs={{0,128},{128,256},{256,384},{384,0},{1,129},{129,257},{257,385},{3... | collective-permute-start | bytes 1179656 | tf_op jit(solution)/shard_map/ppermute | solution.py:178
  50.6 9.7 %collective-permute-start.7 = (bf16[8,32,768]{2,1,0:T(8,128)(2,1)S(1)}, bf16[8,32,768]{2,1,0:T(8,128)(2,1)S(1)}, u32[]{:S(2)}, u32[]{:S(2)}) collective-permute-start(bf16[8,32,768]{2,1,0:T(8,128)(2,1)S(1)} %collective-permute-done.3.xb), channel_id=1, source_target_pairs={{0,384},{128,0},{256,128},{384,256},{1,385},{129,1},{257,129},{385... | collective-permute-start | bytes 1179656 | tf_op jit(solution)/shard_map/ppermute | solution.py:178
  54.6 48.1 %collective-permute-start.11 = (bf16[512,1536]{1,0:T(8,128)(2,1)}, bf16[512,1536]{1,0:T(8,128)(2,1)}, u32[]{:S(2)}, u32[]{:S(2)}) collective-permute-start(bf16[512,1536]{1,0:T(8,128)(2,1)} %constant_dynamic-slice_fusion.4), channel_id=1, source_target_pairs={{0,8},{8,0},{1,9},{9,1},{2,10},{10,2},{3,11},{11,3},{4,12},{12,4},... | collective-permute-start | bytes 4718600 | tf_op jit(solution)/shard_map/ppermute | solution.py:31
  56.9 11.0 %collective-permute-start.8 = (bf16[8,32,768]{2,1,0:T(8,128)(2,1)S(1)}, bf16[8,32,768]{2,1,0:T(8,128)(2,1)S(1)}, u32[]{:S(2)}, u32[]{:S(2)}) collective-permute-start(bf16[8,32,768]{2,1,0:T(8,128)(2,1)S(1)} %broadcast_select_fusion.1), channel_id=1, source_target_pairs={{0,128},{4,388},{128,256},{132,4},{256,384},{260,132},{384,0},{388... | collective-permute-start | bytes 1179656 | tf_op jit(solution)/shard_map/ppermute | solution.py:179
  60.3 11.8 %collective-permute-start.9 = (bf16[8,32,768]{2,1,0:T(8,128)(2,1)S(1)}, bf16[8,32,768]{2,1,0:T(8,128)(2,1)S(1)}, u32[]{:S(2)}, u32[]{:S(2)}) collective-permute-start(bf16[8,32,768]{2,1,0:T(8,128)(2,1)S(1)} %broadcast_select_fusion), channel_id=1, source_target_pairs={{0,128},{4,388},{128,256},{132,4},{256,384},{260,132},{384,0},{388... | collective-permute-start | bytes 1179656 | tf_op jit(solution)/shard_map/ppermute | solution.py:180
  88.7 24.4 %all-to-all-start.1 = ((bf16[64,16,256]{2,1,0:T(8,128)(2,1)}), bf16[64,16,256]{2,1,0:T(8,128)(2,1)S(1)}, u32[]{:S(2)}, u32[]{:S(2)}) async-start(bf16[64,16,256]{2,1,0:T(8,128)(2,1)} %bitcast.11), calls=%async_computation.1 | async-start | bytes 1048576 | tf_op jit(solution)/shard_map/all_to_all | solution.py:206
  97.1 22.2 %copy-start = (bf16[1,1,256,768]{3,2,1,0:T(8,128)(2,1)S(1)}, bf16[1,1,256,768]{3,2,1,0:T(8,128)(2,1)}, u32[]{:S(2)}) copy-start(bf16[1,1,256,768]{3,2,1,0:T(8,128)(2,1)} %param.4) | copy-start | bytes 1179652
  100.3 17.5 %collective-permute-start.12 = (bf16[512,768]{1,0:T(8,128)(2,1)}, bf16[512,768]{1,0:T(8,128)(2,1)S(1)}, u32[]{:S(2)}, u32[]{:S(2)}) collective-permute-start(bf16[512,768]{1,0:T(8,128)(2,1)} %get-tuple-element.23), channel_id=1, source_target_pairs={{0,4},{4,0},{1,5},{5,1},{2,6},{6,2},{3,7},{7,3},{8,12},{12,8},{9,1... | collective-permute-start | bytes 2359304 | tf_op jit(solution)/shard_map/ppermute | solution.py:31
  105.2 12.6 %collective-permute-start.13 = (bf16[512,768]{1,0:T(8,128)(2,1)}, bf16[512,768]{1,0:T(8,128)(2,1)}, u32[]{:S(2)}, u32[]{:S(2)}) collective-permute-start(bf16[512,768]{1,0:T(8,128)(2,1)} %get-tuple-element.25), channel_id=1, source_target_pairs={{0,4},{4,0},{1,5},{5,1},{2,6},{6,2},{3,7},{7,3},{8,12},{12,8},{9,1... | collective-permute-start | bytes 2359304 | tf_op jit(solution)/shard_map/ppermute | solution.py:31
  113.1 6.2 %collective-permute-start.10 = (bf16[64,16,256]{2,1,0:T(8,128)(2,1)S(1)}, bf16[64,16,256]{2,1,0:T(8,128)(2,1)S(1)}, u32[]{:S(2)}, u32[]{:S(2)}) collective-permute-start(bf16[64,16,256]{2,1,0:T(8,128)(2,1)S(1)} %all-to-all-done.1), channel_id=1, source_target_pairs={{0,4},{4,0},{1,5},{5,1},{2,6},{6,2},{3,7},{7,3},{8,12},{12,8},{9,1... | collective-permute-start | bytes 1572872 | tf_op jit(solution)/shard_map/ppermute | solution.py:31
Sparse Core Ops, SparseCore 0:
  31.5 49.5 all-gather.1
